TPU v7x, 32 devices: a whole 2x2x4 slice. The times are simulated.
32 devices in a mesh: grp: 4 (over z), gene: 8 (over y, x, core).
Axes of the slice: x: 2, y: 2, z: 4, core: 2. Of those that a mesh axis runs over, the one named last changes fastest.
Arguments:
- counts: int32 [1024, 7680], P('grp', 'gene'), may hold values from 0 to 12
- panels: int32 [7680], P('gene'), may hold values from 0 to 63
- membership: int32 [4, 256], P('grp'), may hold values from 0 to 3, never falling along the last dimension, each value on 1 to 128 neighbouring positions
- w_proj: bfloat16 [7680, 6400], P('gene'), may hold values from -0.03125 to 0.03125
- w_qkv_within: bfloat16 [1600, 32, 150], P(None, 'gene'), may hold values from -0.15625 to 0.15625
- w_out_within: bfloat16 [32, 50, 1600], P('gene'), may hold values from -0.4375 to 0.4375
- w_qkv_cross: bfloat16 [1600, 32, 150], P(None, 'gene'), may hold values from -0.15625 to 0.15625
- w_out_cross: bfloat16 [32, 50, 1600], P('gene'), may hold values from -0.4375 to 0.4375
- w_mean: bfloat16 [1600, 7680], P(None, 'gene'), may hold values from -0.25 to 0.25
- w_disp: bfloat16 [1600, 64], replicated, may hold values from -0.25 to 0.25
Outputs:
- cell_loss: float32 [1024], P('grp')
- grad_mean: float32 [1600, 7680], P('grp', 'gene')
- grad_disp: float32 [1600, 64], replicated
Inputs may be any that keep to these rules, and one draw needn't show every extreme that they name: `membership`: group numbers never fall along a row; a group has at most 128 cells.
All inputs are finite; a program needn't handle non-finite values.
Results may differ from a plain program's by a relative error of at most 0.00055.
Values may be sent and summed in bfloat16 or wider, within the bound.
No kernel may reach another device: no remote copies, remote signals or barrier semaphores. Data moves between devices by JAX's collectives and lax.ppermute only.
A program may use at most 128 MiB of HBM per device.

v0:
```python
import jax
import jax.numpy as jnp
from jax import lax
from jax.sharding import PartitionSpec as P

EPS = 1e-06
FLOOR = 0.3
TARGET = 10000.0
DISP_BASE = 0.5


def rms_rows(values):
    return values * lax.rsqrt(jnp.mean(values * values, axis=-1, keepdims=True) + EPS)


def head_norm(values):
    return values * lax.rsqrt(jnp.maximum(jnp.mean(values * values, axis=-1, keepdims=True), FLOOR))


def split_heads(qkv, heads):
    qkv = qkv.reshape(qkv.shape[0], heads, 3, -1)
    query = head_norm(qkv[:, :, 0]).astype(jnp.bfloat16)
    keys = head_norm(qkv[:, :, 1]).astype(jnp.bfloat16)
    values = qkv[:, :, 2].astype(jnp.bfloat16)
    return (query, keys, values)


def within_cells(query, keys, values, modules):
    rows, heads, width = query.shape
    cells = rows // modules
    q_all = query.reshape(cells, modules, heads, width)
    k_all = keys.reshape(cells, modules, heads, width)
    v_all = values.reshape(cells, modules, heads, width)
    scores = jnp.einsum(
        "cmhd,cnhd->chmn", q_all, k_all, preferred_element_type=jnp.float32
    ) * width ** (-0.5)
    weights = jnp.exp(scores)
    probs = (weights / jnp.sum(weights, axis=-1, keepdims=True)).astype(jnp.bfloat16)
    mixed = jnp.einsum("chmn,cnhd->cmhd", probs, v_all, preferred_element_type=jnp.float32)
    return mixed.astype(jnp.bfloat16).reshape(rows, heads * width)


def across_cells(query, keys, values, groups, modules):
    rows, heads, width = query.shape
    cells = rows // modules
    q_all = query.reshape(cells, modules, heads, width)
    k_all = keys.reshape(cells, modules, heads, width)
    v_all = values.reshape(cells, modules, heads, width)
    scores = jnp.einsum(
        "cmhd,nmhd->mhcn", q_all, k_all, preferred_element_type=jnp.float32
    ) * width ** (-0.5)
    same = groups[:, None] == groups[None, :]
    weights = jnp.where(same[None, None], jnp.exp(scores), 0.0)
    probs = (weights / jnp.sum(weights, axis=-1, keepdims=True)).astype(jnp.bfloat16)
    mixed = jnp.einsum("mhcn,nmhd->cmhd", probs, v_all, preferred_element_type=jnp.float32)
    return mixed.astype(jnp.bfloat16).reshape(rows, heads * width)


def nb_terms(observed, rate, theta):
    total = theta + rate
    log_total = jnp.log(total)
    nll = -(
        lax.lgamma(observed + theta)
        - lax.lgamma(theta)
        - lax.lgamma(observed + 1.0)
        + theta * (jnp.log(theta) - log_total)
        + observed * (jnp.log(rate) - log_total)
    )
    d_rate = (theta + observed) / total - observed / rate
    d_theta = -(
        lax.digamma(observed + theta)
        - lax.digamma(theta)
        + jnp.log(theta)
        + 1.0
        - log_total
        - (theta + observed) / total
    )
    return (nll, d_rate, d_theta)


def shards(
    counts,
    panels,
    membership,
    w_proj,
    w_qkv_within,
    w_out_within,
    w_qkv_cross,
    w_out_cross,
    w_mean,
    w_disp,
):
    cells, genes_here = counts.shape
    width = w_qkv_within.shape[0]
    heads_here = w_qkv_within.shape[1]
    modules = w_proj.shape[1] // width
    gene_count = lax.axis_size("gene")
    genes_all = genes_here * gene_count
    rows = cells * modules
    share = rows // gene_count
    cell_share = cells // gene_count
    first = lax.axis_index("gene") * share
    observed = counts.astype(jnp.float32)
    library = 1.0 + lax.psum(jnp.sum(observed, axis=1), "gene")
    scaled = jnp.log1p(observed * (TARGET / library)[:, None]).astype(jnp.bfloat16)
    partial_value = jnp.dot(scaled, w_proj, preferred_element_type=jnp.float32).reshape(rows, width)
    tokens = lax.psum(partial_value, "gene")
    normed = rms_rows(tokens).astype(jnp.bfloat16)
    resid = lax.dynamic_slice_in_dim(tokens, first, share, 0)
    flat_within = w_qkv_within.reshape(width, -1)
    query, keys, values = split_heads(
        jnp.dot(normed, flat_within, preferred_element_type=jnp.float32), heads_here
    )
    mixed = within_cells(query, keys, values, modules)
    out_within = w_out_within.reshape(-1, width)
    block = mixed
    resid = resid + lax.psum_scatter(
        jnp.dot(block, out_within, preferred_element_type=jnp.float32),
        "gene",
        scatter_dimension=0,
        tiled=True,
    )
    flat_cross = w_qkv_cross.reshape(width, -1)
    qkv_cross = jnp.dot(
        lax.all_gather(rms_rows(resid).astype(jnp.bfloat16), "gene", axis=0, tiled=True),
        flat_cross,
        preferred_element_type=jnp.float32,
    )
    query, keys, values = split_heads(qkv_cross, heads_here)
    mixed = across_cells(query, keys, values, membership[0], modules)
    out_cross = w_out_cross.reshape(-1, width)
    block = mixed
    resid = resid + lax.psum_scatter(
        jnp.dot(block, out_cross, preferred_element_type=jnp.float32),
        "gene",
        scatter_dimension=0,
        tiled=True,
    )
    pooled = jnp.mean(resid.reshape(cell_share, modules, width), axis=1)
    hidden = lax.all_gather(rms_rows(pooled).astype(jnp.bfloat16), "gene", axis=0, tiled=True)
    panel_count = w_disp.shape[1]
    logit = jnp.dot(hidden, w_mean, preferred_element_type=jnp.float32)
    disp = jnp.dot(hidden, w_disp, preferred_element_type=jnp.float32)
    onehot = (panels[None, :] == jnp.arange(panel_count, dtype=jnp.int32)[:, None]).astype(
        jnp.float32
    )
    theta = jnp.dot(DISP_BASE + jax.nn.softplus(disp), onehot, precision=lax.Precision.HIGHEST)
    rate_scale = (library / genes_all)[:, None]
    rate = rate_scale * jax.nn.softplus(logit)
    nll, d_rate, d_theta = nb_terms(observed, rate, theta)
    norm_scale = (cells * lax.axis_size("grp")) ** (-0.5)
    d_logit = d_rate * rate_scale * jax.nn.sigmoid(logit) * norm_scale
    d_panel = jnp.dot(d_theta, onehot.T, precision=lax.Precision.HIGHEST)
    cell_part = jnp.sum(nll, axis=1)
    hidden_f = hidden.astype(jnp.float32)
    dims = (((0,), (0,)), ((), ()))
    cell_total, panel_total = lax.psum((cell_part, d_panel), "gene")
    d_disp = panel_total * jax.nn.sigmoid(disp) * norm_scale
    local_disp = lax.dot_general(hidden_f, d_disp, dims, precision=lax.Precision.HIGHEST)
    grad_disp = lax.psum(local_disp, "grp")
    cell_loss = cell_total / genes_all
    block = hidden_f
    grad_mean = lax.psum_scatter(
        lax.dot_general(block, d_logit, dims, precision=lax.Precision.HIGHEST),
        "grp",
        scatter_dimension=0,
        tiled=True,
    )
    return (cell_loss, grad_mean, grad_disp)


def solution(mesh):
    return jax.shard_map(
        shards,
        mesh=mesh,
        in_specs=(
            P("grp", "gene"),
            P("gene"),
            P("grp", None),
            P("gene", None),
            P(None, "gene", None),
            P("gene", None, None),
            P(None, "gene", None),
            P("gene", None, None),
            P(None, "gene"),
            P(),
        ),
        out_specs=(P("grp"), P("grp", "gene"), P()),
        check_vma=False,
    )
```

profile of v0, /device:TPU:0, one launch (start us, length us, event | category | flops | bytes accessed | tf_op | source)
XLA Modules:
  0.0 676.6 jit_solution(11574047277872424266)
XLA Ops:
  7.2 1.5 convert_reduce_fusion
  8.7 15.1 %psum.35 = f32[256]{0:T(256)S(1)} all-reduce(f32[256]{0:T(256)S(1)} %convert_reduce_fusion), channel_id=1, replica_groups=mesh['grp'=4,'gene'=8] {'gene'}, use_global_device_ids=true, to_apply=%region_1.0 | all-reduce | flops 256 | bytes 2048 | tf_op jit(solution)/shard_map/psum | solution.py:104
  23.9 11.2 %fusion.88 = f32[256,6400]{1,0:T(8,128)} fusion(bf16[960,6400]{1,0:T(8,128)(2,1)} %param.13, s32[256,960]{0,1:T(8,128)} %param.10, f32[256]{0:T(256)S(1)} %get-tuple-element.14), kind=kOutput, calls=%fused_computation.118 | convolution fusion | flops 3146465280 | bytes 19825664 | tf_op jit(solution)/shard_map/dot_general | solution.py:106
  35.1 8.7 %reshape.175 = f32[1024,1600]{1,0:T(8,128)} reshape(f32[256,6400]{1,0:T(8,128)} %fusion.88) | data formatting | bytes 13107200 | tf_op jit(solution)/shard_map/reshape | solution.py:106
  43.8 7.5 %copy.66 = f32[1024,1600]{0,1:T(8,128)} copy(f32[1024,1600]{1,0:T(8,128)} %reshape.175) | data formatting | bytes 13107200 | tf_op jit(solution)/shard_map/reshape | solution.py:106
  51.5 3.1 copy.67
  54.5 3.8 reshape.176
  58.3 4.1 dot_general.55
  62.4 2.1 copy.77
  64.5 2.3 reshape.178
  66.7 91.3 %all-reduce.4.cloned.1.call-done = f32[1024,1600]{0,1:T(8,128)} async-done(((f32[1024,1600]{0,1:T(8,128)}), f32[1024,1600]{0,1:T(8,128)}) %all-reduce.4.cloned.1.call-update) | async-done | bytes 6553616 | tf_op jit(solution)/shard_map/psum | solution.py:107
  158.0 3.5 multiply_reduce_fusion
  161.5 1.2 copy-done.3
  162.7 4.4 fusion.2
  167.1 1.5 multiply_reduce_fusion.4
  169.5 1.4 rsqrt.70
  170.9 1.4 rsqrt.72
  172.2 3.2 copy.69
  175.4 3.2 copy.70
  178.6 5.2 fusion.16
  183.8 1.9 copy.73
  185.8 1.7 copy.75
  187.5 2.4 copy.68
  190.0 2.8 fusion.8
  192.7 1.5 copy.76
  194.2 2.6 reshape.177
  196.8 5.0 fusion.177
  202.0 63.2 %reduce-scatter.4.cloned.1.call-done = f32[128,1600]{0,1:T(8,128)} async-done(((f32[1024,1600]{0,1:T(8,128)}), f32[128,1600]{0,1:T(8,128)}) %reduce-scatter.4.cloned.1.call-update) | async-done | bytes 819216 | tf_op jit(solution)/shard_map/reduce_scatter | solution.py:117
  265.2 1.6 multiply_reduce_fusion.5
  269.0 3.1 copy.78
  272.1 3.8 reshape.179
  275.9 4.0 dot_general.61
  279.9 2.0 copy.87
  281.9 2.3 reshape.181
  284.3 17.7 %all-gather.2.cloned.1.call-done = bf16[1024,1600]{0,1:T(8,128)(2,1)} async-done(((bf16[128,1600]{0,1:T(8,128)(2,1)}), bf16[1024,1600]{0,1:T(8,128)(2,1)}) %all-gather.2.cloned.1.call-update) | async-done | bytes 3276816 | tf_op jit(solution)/shard_map/all_gather | solution.py:125
  302.1 5.3 fusion.4
  307.4 1.5 multiply_reduce_fusion.2
  309.8 3.1 copy.80
  312.9 1.3 rsqrt.75
  314.2 3.2 copy.81
  317.4 1.3 rsqrt.77
  318.8 2.4 copy.79
  321.2 2.7 multiply_convert_fusion.2
  323.9 1.4 multiply_convert_fusion.1
  325.2 1.2 fusion
  326.5 1.9 fusion.10
  328.4 2.6 copy.86
  331.0 2.6 reshape.180
  333.6 5.1 fusion.178
  338.9 62.9 %reduce-scatter.6.cloned.1.call-done = f32[128,1600]{0,1:T(8,128)} async-done(((f32[1024,1600]{0,1:T(8,128)}), f32[128,1600]{0,1:T(8,128)}) %reduce-scatter.6.cloned.1.call-update) | async-done | bytes 819216 | tf_op jit(solution)/shard_map/reduce_scatter | solution.py:133
  401.8 2.4 add.121
  404.2 2.3 copy.88
  406.5 2.3 reshape.182
  408.8 1.7 reduce_sum.117
  410.7 10.6 %all_gather.7 = bf16[256,1600]{1,0:T(8,128)(2,1)S(1)} all-gather(bf16[32,1600]{1,0:T(8,128)(2,1)S(1)} %multiply_convert_fusion.6), channel_id=1, replica_groups=mesh['grp'=4,'gene'=8] {'gene'}, dimensions={0}, use_global_device_ids=true | all-gather | bytes 921600 | tf_op jit(solution)/shard_map/all_gather | solution.py:140
  422.9 19.3 %add_reduce_fusion = (f32[256]{0:T(256)S(1)}, f32[256,960]{0,1:T(8,128)S(1)}) fusion(s32[256,960]{0,1:T(8,128)S(1)} %copy-done.7, f32[256,960]{0,1:T(8,128)S(1)} %fusion.180, f32[256]{0:T(256)S(1)} %get-tuple-element.13, s32[960]{0:T(1024)S(1)} %copy-done.13, f32[256,64]{0,1:T(8,128)S(1)} %fusion.179), kind=kOutput, calls=%fused_computation.68 | convolution fusion | flops 231927552 | bytes 3020544 | tf_op jit(solution)/shard_map/dot_general | solution.py:147
  442.1 16.1 %fusion.54 = f32[256,64]{0,1:T(8,128)} fusion(f32[256,960]{0,1:T(8,128)S(1)} %get-tuple-element.18, s32[256,960]{0,1:T(8,128)S(1)} %copy-done.7, f32[256,960]{0,1:T(8,128)S(1)} %fusion.180, f32[256]{0:T(256)S(1)} %get-tuple-element.13, s32[960]{0:T(1024)S(1)} %copy-done.13), kind=kOutput, calls=%fused_computation.84 | convolution fusion | flops 229847040 | bytes 3019520 | tf_op jit(solution)/shard_map/dot_general | solution.py:153
  458.3 52.6 %all-reduce.6.cloned.1.call-done = f32[256,64]{0,1:T(8,128)} async-done(((f32[256,64]{0,1:T(8,128)}), f32[256,64]{0,1:T(8,128)}) %all-reduce.6.cloned.1.call-update) | async-done | bytes 65552 | tf_op jit(solution)/shard_map/psum | solution.py:157
  510.9 2.1 fusion.125
  513.1 8.1 %fusion.39 = f32[1600,960]{1,0:T(8,128)} fusion(bf16[256,1600]{1,0:T(8,128)(2,1)S(1)} %copy-done.5, f32[256,960]{0,1:T(8,128)} %copy-done.14, s32[256,960]{0,1:T(8,128)S(1)} %copy-done.8, f32[256,960]{0,1:T(8,128)S(1)} %get-tuple-element.18, f32[256]{0:T(256)S(1)} %get-tuple-element.13), kind=kOutput, calls=%fused_computation.58 | convolution fusion | flops 4723261440 | bytes 9913344 | tf_op jit(solution)/shard_map/dot_general | solution.py:164
  521.3 12.3 %psum.37 = f32[256]{0:T(256)S(1)} all-reduce(f32[256]{0:T(256)S(1)} %neg.22), channel_id=1, replica_groups=mesh['grp'=4,'gene'=8] {'gene'}, use_global_device_ids=true, to_apply=%region_16.17 | all-reduce | flops 256 | bytes 2048 | tf_op jit(solution)/shard_map/psum | solution.py:157
  534.1 16.3 %all-reduce.8.cloned.1.call-done = f32[1600,64]{0,1:T(8,128)} async-done(((f32[1600,64]{0,1:T(8,128)}), f32[1600,64]{0,1:T(8,128)}) %all-reduce.8.cloned.1.call-update) | async-done | bytes 409616 | tf_op jit(solution)/shard_map/psum | solution.py:160
  550.4 117.4 %reduce-scatter.8.cloned.1.call-done = f32[400,960]{1,0:T(8,128)} async-done(((f32[1600,960]{1,0:T(8,128)}), f32[400,960]{1,0:T(8,128)}) %reduce-scatter.8.cloned.1.call-update) | async-done | bytes 1536016 | tf_op jit(solution)/shard_map/reduce_scatter | solution.py:163
  667.8 1.8 copy.111
  (62 shorter events, 7.0 us)
Async XLA Ops:
  7.2 414.2 %copy-start = (bf16[1600,960]{0,1:T(8,128)(2,1)S(1)}, bf16[1600,960]{0,1:T(8,128)(2,1)}, u32[]{:S(2)}) copy-start(bf16[1600,960]{0,1:T(8,128)(2,1)} %param.18) | copy-start | bytes 9216004
  7.2 150.8 %all-reduce.4.cloned.1.call-start = ((), (), s32[]{:S(2)}) async-start(), calls=%async_computation.3 | async-start | bytes 13107200 | tf_op jit(solution)/shard_map/psum | solution.py:107
  51.4 213.8 %reduce-scatter.4.cloned.1.call-start = ((), (), s32[]{:S(2)}) async-start(), calls=%async_computation.4 | async-start | bytes 7372800 | tf_op jit(solution)/shard_map/reduce_scatter | solution.py:117
  158.0 4.7 copy-start.3
  201.9 100.1 %all-gather.2.cloned.1.call-start = ((), (), s32[]{:S(2)}) async-start(), calls=%async_computation.5 | async-start | bytes 3686400 | tf_op jit(solution)/shard_map/all_gather | solution.py:125
  266.8 0.9 copy-start.6
  268.5 133.3 %reduce-scatter.6.cloned.1.call-start = ((), (), s32[]{:S(2)}) async-start(), calls=%async_computation.6 | async-start | bytes 7372800 | tf_op jit(solution)/shard_map/reduce_scatter | solution.py:133
  275.9 8.3 %copy-start.12 = (s32[1,256]{1,0:T(1,128)S(1)}, s32[1,256]{1,0:T(1,128)}, u32[]{:S(2)}) copy-start(s32[1,256]{1,0:T(1,128)} %param.12) | copy-start | bytes 3076
  321.2 2.7 copy-start.2
  321.2 2.7 copy-start.9
  325.2 1.2 copy-start.10
  338.7 172.2 %all-reduce.6.cloned.1.call-start = ((), (), s32[]{:S(2)}) async-start(), calls=%async_computation.8 | async-start | bytes 131072 | tf_op jit(solution)/shard_map/psum | solution.py:157
  410.7 11.7 %copy-start.11 = (bf16[1600,64]{0,1:T(8,128)(2,1)S(1)}, bf16[1600,64]{0,1:T(8,128)(2,1)}, u32[]{:S(2)}) copy-start(bf16[1600,64]{0,1:T(8,128)(2,1)} %param.19) | copy-start | bytes 614404
  421.3 1.5 copy-start.4
  421.3 1.5 copy-start.7
  421.3 1.5 copy-start.13
  422.4 19.7 %copy-start.14 = (f32[256,960]{0,1:T(8,128)}, f32[256,960]{0,1:T(8,128)S(1)}, u32[]{:S(2)}) copy-start(f32[256,960]{0,1:T(8,128)S(1)} %fusion.180) | copy-start | bytes 2949124
  442.1 68.8 %copy-start.5 = (bf16[256,1600]{1,0:T(8,128)(2,1)S(1)}, bf16[256,1600]{1,0:T(8,128)(2,1)}, u32[]{:S(2)}) copy-start(bf16[256,1600]{1,0:T(8,128)(2,1)} %copy-done.4) | copy-start | bytes 2457604
  442.1 70.9 %copy-start.8 = (s32[256,960]{0,1:T(8,128)S(1)}, s32[256,960]{0,1:T(8,128)}, u32[]{:S(2)}) copy-start(s32[256,960]{0,1:T(8,128)} %param.10) | copy-start | bytes 2949124
  458.2 92.2 %all-reduce.8.cloned.1.call-start = ((), (), s32[]{:S(2)}) async-start(), calls=%async_computation.9 | async-start | bytes 851968 | tf_op jit(solution)/shard_map/psum | solution.py:160
  513.0 154.8 %reduce-scatter.8.cloned.1.call-start = ((), (), s32[]{:S(2)}) async-start(), calls=%async_computation.7 | async-start | bytes 8192000 | tf_op jit(solution)/shard_map/reduce_scatter | solution.py:163
  521.2 148.3 %copy-start.1 = (bf16[1600,960]{0,1:T(8,128)(2,1)S(1)}, bf16[1600,960]{0,1:T(8,128)(2,1)}, u32[]{:S(2)}) copy-start(bf16[1600,960]{0,1:T(8,128)(2,1)} %param.18) | copy-start | bytes 9216004
Sparse Core Ops, SparseCore 0:
  51.5 106.4 all-reduce.3
  202.0 63.1 reduce-scatter.3
  268.7 33.3 all-gather.1
  338.8 62.9 reduce-scatter.5
  458.4 52.4 all-reduce.5
  513.8 36.5 all-reduce.7
  553.3 114.4 reduce-scatter.7
where the time goes:
time: 683 us; the launch traced here: 677 us
  waiting for transfers between devices  421 us (62%)
  local copies, waits for them, and re-layouts  92.9 us (14%)
  matrix products  89.2 us (13%)
  blocking collectives  38 us (6%)
  other arithmetic  19.6 us (3%)
  between operations  14.6 us (2%)
    reduce_scatter x1, waiting for transfers between devices, shards(): lax.psum_scatter(lax.dot_general(block, d_logit, dims, precision=lax.Prec...  117 us
    psum x1, waiting for transfers between devices, shards(): tokens = lax.psum(partial_value, 'gene')  91.3 us
    reduce_scatter x1, waiting for transfers between devices, shards(): lax.psum_scatter(jnp.dot(block, out_within, preferred_element_type=jnp.fl...  63.2 us
    reduce_scatter x1, waiting for transfers between devices, shards(): lax.psum_scatter(jnp.dot(block, out_cross, preferred_element_type=jnp.flo...  62.9 us
    psum x1, waiting for transfers between devices, shards(): cell_total, panel_total = lax.psum((cell_part, d_panel), 'gene')  52.6 us
    dot_general x1, matrix products, shards(): jnp.dot(DISP_BASE + jax.nn.softplus(disp), onehot, precision=lax.Precisio...  19.3 us
    all_gather x1, waiting for transfers between devices, shards(): lax.all_gather(rms_rows(resid).astype(jnp.bfloat16), 'gene', axis=0, tile...  17.7 us
    reshape x2, local copies, waits for them, and re-layouts, shards(): jnp.dot(scaled, w_proj, preferred_element_type=jnp.float32)  16.3 us
  transfers between devices with their start and end apart: 7, of which 7 were waited for; matrix products, arithmetic and copies ran while one was open for 6% of the time, Pallas kernels for 0%

commit v1 on v0

v1 whole, which is shorter than its diff:
```python
import functools

import jax
import jax.numpy as jnp
from jax import lax
from jax.experimental import pallas as pl
from jax.experimental.pallas import tpu as pltpu
from jax.sharding import PartitionSpec as P

EPS = 1e-06
FLOOR = 0.3
TARGET = 10000.0
DISP_BASE = 0.5
COUNT_MOST = 12
LANES = 128
EXTRA = 16
LOG2_E = 1.4426950408889634

F32 = jnp.float32
BF16 = jnp.bfloat16
NT = (((1,), (1,)), ((), ()))
PARAMS = pltpu.CompilerParams(vmem_limit_bytes=12 * 1024 * 1024)
LARGE = pltpu.CompilerParams(vmem_limit_bytes=20 * 1024 * 1024)
WHOLE = pl.BlockSpec(memory_space=pltpu.VMEM)
SCALAR = pl.BlockSpec(memory_space=pltpu.SMEM)
UNREAD = pl.BlockSpec(memory_space=pl.ANY)


def shape_of(shape, dtype):
    return jax.ShapeDtypeStruct(shape, dtype)


def launch(kernel, args, in_specs, after=(), params=PARAMS, **options):
    count = len(args)

    def body(*refs):
        kernel(*refs[:count], *refs[count + len(after) :])

    return pl.pallas_call(
        body,
        in_specs=list(in_specs) + [UNREAD] * len(after),
        compiler_params=params,
        **options,
    )(*args, *after)


def fixed(*shape):
    return pl.BlockSpec(shape, lambda i: (0,) * len(shape))


def dot_nt(left, right):
    return lax.dot_general(left, right, NT, preferred_element_type=F32)


def dot_nn(left, right):
    return jnp.dot(left, right, preferred_element_type=F32)


def split2(value):
    high = value.astype(BF16)
    return high, (value - high.astype(F32)).astype(BF16)


def split3(value):
    high = value.astype(BF16)
    rest = value - high.astype(F32)
    middle = rest.astype(BF16)
    return high, middle, (rest - middle.astype(F32)).astype(BF16)


def softplus(value):
    return jnp.maximum(value, 0.0) + jnp.log1p(jnp.exp(-jnp.abs(value)))


def softplus_pair(value):
    small = jnp.exp(-jnp.abs(value))
    soft = jnp.maximum(value, 0.0) + jnp.log1p(small)
    return soft, jnp.where(value >= 0.0, 1.0, small) / (1.0 + small)


def sigmoid(value):
    return 1.0 / (1.0 + jnp.exp(-value))


def rms_rows(values):
    return values * lax.rsqrt(jnp.mean(values * values, axis=-1, keepdims=True) + EPS)


def tile_of(extent, unit, most):
    for tile in range(min(most, extent) // unit * unit, 0, -unit):
        if extent % tile == 0:
            return tile
    return extent


def hop(value, axis, key):
    size = lax.axis_size(axis)
    return lax.ppermute(value, axis, [(i, i ^ key[i & 1]) for i in range(size)])


def straight(mask):
    return (mask, mask)


def far_keys(size):
    masks = [1 << bit for bit in range(1, size.bit_length() - 1)]
    return list(zip(masks, masks[::-1]))


def spread_keys(size):
    keys = [(0, 0)]
    for even, odd in far_keys(size):
        keys += [(e ^ even, o ^ odd) for e, o in keys]
    return keys + [(1 ^ o, 1 ^ e) for e, o in keys]


def spread(own, axis):
    size = lax.axis_size(axis)
    blocks = [own]
    for key in far_keys(size) + [straight(1)]:
        blocks += [hop(block, axis, key) for block in blocks]
    return blocks


def holder(me, key):
    even, odd = key
    return me ^ (even + (me & 1) * (odd - even))


def project_kernel(keys, me_ref, counts_ref, scale_ref, w_ref, keep_ref, send_ref, x_ref, flat_ref):
    share = x_ref.shape[0] // len(keys)
    half = keep_ref.shape[0]

    @pl.when(pl.program_id(0) == 0)
    def _():
        scaled = jnp.log1p(counts_ref[...].astype(F32) * scale_ref[...])
        flat_ref[...] = scaled.T.astype(BF16)
        for place, key in enumerate(keys):
            x_ref[place * share : (place + 1) * share, :] = flat_ref[
                pl.ds(holder(me_ref[0], key) * share, share), :
            ]

    part = dot_nn(x_ref[...], w_ref[...])
    keep_ref[...] = part[:half]
    send_ref[...] = part[half:]


def project(me, counts_t, scale, w_proj, keys, chunk, chunks, after):
    genes, cells = counts_t.shape
    columns = w_proj.shape[1] // chunks
    tile = tile_of(columns, LANES, 640)
    steps = columns // tile
    half = cells // 2
    out = shape_of((half, columns), F32)
    return launch(
        functools.partial(project_kernel, keys),
        (me, counts_t, scale, w_proj),
        [
            SCALAR,
            fixed(genes, cells),
            fixed(1, cells),
            pl.BlockSpec((genes, tile), lambda i: (0, chunk * steps + i)),
        ],
        after,
        grid=(steps,),
        out_shape=(out, out),
        out_specs=[pl.BlockSpec((half, tile), lambda i: (0, i))] * 2,
        scratch_shapes=[pltpu.VMEM((cells, genes), BF16), pltpu.VMEM((cells, genes), BF16)],
        cost_estimate=pl.CostEstimate(
            flops=2 * cells * genes * columns,
            bytes_accessed=genes * columns * 2 + cells * columns * 4,
            transcendentals=cells * genes,
        ),
    )


def halve_kernel(keep_ref, got_ref, stay_ref, go_ref):
    half = stay_ref.shape[0]
    total = keep_ref[...] + got_ref[...].astype(F32)
    stay_ref[...] = total[:half]
    go_ref[...] = total[half:].astype(BF16)


def halve(keep, got, after=()):
    rows, columns = keep.shape
    out = (rows // 2, columns)
    return launch(
        halve_kernel,
        (keep, got),
        [WHOLE] * 2,
        after,
        out_shape=(shape_of(out, F32), shape_of(out, BF16)),
        out_specs=[WHOLE] * 2,
        cost_estimate=pl.CostEstimate(
            flops=rows * columns, bytes_accessed=rows * columns * 11, transcendentals=0
        ),
    )


def rows_kernel(chunks, *refs):
    tokens_ref, normed_ref = refs[2 * chunks :]
    width = tokens_ref.shape[2]
    parts = tokens_ref.shape[0] // chunks
    for chunk in range(chunks):
        total = refs[2 * chunk][...] + refs[2 * chunk + 1][...].astype(F32)
        for at in range(parts):
            rows = total[:, at * width : (at + 1) * width]
            tokens_ref[chunk * parts + at] = rows
            normed_ref[chunk * parts + at] = rms_rows(rows).astype(BF16)


def to_rows(pairs, width, after):
    share, columns = pairs[0][0].shape
    shape = (len(pairs) * columns // width, share, width)
    return launch(
        functools.partial(rows_kernel, len(pairs)),
        [part for pair in pairs for part in pair],
        [WHOLE] * 2 * len(pairs),
        after,
        out_shape=(shape_of(shape, F32), shape_of(shape, BF16)),
        out_specs=[WHOLE] * 2,
        cost_estimate=pl.CostEstimate(
            flops=12 * share * columns, bytes_accessed=share * columns * 24, transcendentals=0
        ),
    )


def attend_kernel(pieces, heads, head_width, w_ref, row_ref, col_ref, *refs):
    blocks = refs[:-5]
    out_ref, x_ref, query_ref, keys_ref, values_ref = refs[-5:]
    modules, share, _ = blocks[0].shape
    used = heads * head_width
    lane = lax.broadcasted_iota(jnp.int32, (1, used), 1)
    picks = [(lax.rem(lane, heads) == h).astype(F32).astype(BF16) for h in range(heads)]
    down = lax.rem(lax.broadcasted_iota(jnp.int32, (used, used), 0), heads)
    over = lax.rem(lax.broadcasted_iota(jnp.int32, (used, used), 1), heads)
    same_head = (down == over).astype(F32).astype(BF16)

    def head_norm(values):
        high, low = split2(values * values)
        mean = (dot_nn(high, same_head) + dot_nn(low, same_head)) * (1.0 / head_width)
        return (values * lax.rsqrt(jnp.maximum(mean, FLOOR))).astype(BF16)

    rows = len(pieces[0]) * share
    for at, piece in enumerate(pieces):
        for place, (block, module) in enumerate(piece):
            x_ref[at * rows + place * share : at * rows + (place + 1) * share, :] = blocks[block][
                module
            ]
    every = x_ref.shape[0]
    step = min(every, 256)
    for at in range(0, every, step):
        part = slice(at, at + step)
        qkv = dot_nt(x_ref[part, :], w_ref[...])
        query_ref[part, :] = head_norm(qkv[:, :used])
        keys_ref[part, :] = head_norm(qkv[:, used : 2 * used])
        values_ref[part, :] = qkv[:, 2 * used :].astype(BF16)
    same = row_ref[...] == col_ref[...]
    scale = head_width ** (-0.5) * LOG2_E
    for at, piece in enumerate(pieces):
        part = slice(at * rows, (at + 1) * rows)
        query, keys, values = query_ref[part, :], keys_ref[part, :], values_ref[part, :]
        mixed = jnp.zeros((rows, used), F32)
        for pick in picks:
            weights = jnp.where(same, jnp.exp2(dot_nt(query * pick, keys) * scale), 0.0)
            probs = weights * (1.0 / jnp.sum(weights, axis=-1, keepdims=True))
            mixed = mixed + dot_nn(probs.astype(BF16), values * pick)
        mixed = mixed.astype(BF16)
        for place, (block, module) in enumerate(piece):
            out_ref[block, module * share : (module + 1) * share, :] = mixed[
                place * share : (place + 1) * share
            ]


def attend(blocks, w_flat, ids, pieces, heads, head_width, after):
    count = len(blocks)
    modules, share, width = blocks[0].shape
    rows = len(pieces[0]) * share
    every = len(pieces) * rows
    used = heads * head_width
    return launch(
        functools.partial(attend_kernel, pieces, heads, head_width),
        (w_flat, *ids, *blocks),
        [WHOLE] * (3 + len(blocks)),
        after,
        out_shape=shape_of((count, modules * share, used), BF16),
        out_specs=WHOLE,
        scratch_shapes=[pltpu.VMEM((every, width), BF16)] + [pltpu.VMEM((every, used), BF16)] * 3,
        cost_estimate=pl.CostEstimate(
            flops=2 * every * (width * 3 * used + 2 * heads * rows * used),
            bytes_accessed=every * width * 2 + 3 * used * width * 2 + every * used * 2,
            transcendentals=every * rows * heads,
        ),
    )


def add_mixed(places, keys, me_ref, w_ref, resid_ref, mixed_refs):
    modules, share, _ = resid_ref.shape
    total = None
    for place, key in zip(places, keys):
        mixed = mixed_refs[0][0] if place == 0 else mixed_refs[place][...]
        term = dot_nn(mixed, w_ref[holder(me_ref[0], key)])
        total = term if total is None else total + term
    return [resid_ref[m] + total[m * share : (m + 1) * share] for m in range(modules)]


def out_kernel(places, keys, me_ref, w_ref, resid_ref, *refs):
    mid_ref, normed_ref = refs[-2:]
    for m, rows in enumerate(add_mixed(places, keys, me_ref, w_ref, resid_ref, refs[:-2])):
        mid_ref[m] = rows
        normed_ref[m] = rms_rows(rows).astype(BF16)


def pool_kernel(places, keys, me_ref, w_ref, resid_ref, *refs):
    modules = add_mixed(places, keys, me_ref, w_ref, resid_ref, refs[:-1])
    pooled = functools.reduce(jnp.add, modules) * (1.0 / len(modules))
    refs[-1][...] = rms_rows(pooled).astype(BF16)


def out_call(kernel, me, keys, mixed, w_all, resid, out_shape, after=()):
    back = [(o, e) if e & 1 else (e, o) for e, o in keys]
    _, rows, inner = mixed[0].shape
    width = w_all.shape[-1]
    return launch(
        functools.partial(kernel, [back.index(key) for key in keys], keys),
        (me, w_all, resid, *mixed),
        [SCALAR, WHOLE, WHOLE, fixed(1, rows, inner)] + [WHOLE] * (len(mixed) - 1),
        after,
        grid=(1,),
        out_shape=out_shape,
        out_specs=[WHOLE] * len(out_shape),
        cost_estimate=pl.CostEstimate(
            flops=2 * rows * len(keys) * inner * width,
            bytes_accessed=len(keys) * inner * (width + rows) * 2 + rows * width * 10,
            transcendentals=0,
        ),
    )


def panel_table(w_disp_ref, hidden, with_log):
    base = DISP_BASE + softplus(dot_nt(w_disp_ref[...], hidden))
    parts = split3(base)
    if with_log:
        parts = [jnp.concatenate(pair, axis=1) for pair in zip(parts, split3(jnp.log(base)))]
    return jnp.concatenate([p.astype(F32) for p in parts], axis=0).astype(BF16)


def panel_pick(panel_ref, panel_count):
    genes = panel_ref.shape[0]
    over = lax.rem(lax.broadcasted_iota(jnp.int32, (genes, 3 * panel_count), 1), panel_count)
    return (panel_ref[...] == over).astype(F32).astype(BF16)


def place_cells(keys, me, blocks, hid_ref):
    share = blocks[0].shape[0]
    for key, block in zip(keys, blocks):
        hid_ref[pl.ds(holder(me, key) * share, share), :] = block


def rate_terms(logit, rate_scale, theta, seen, norm):
    soft, d_soft = softplus_pair(logit)
    rate = rate_scale * soft
    total = theta + rate
    d_logit = theta * (rate - seen) * norm * d_soft / (soft * total)
    return rate, total, d_logit


def decode_kernel(
    keys, norm, me_ref, counts_ref, col_ref, row_ref, scale_ref, wm_ref, wd_ref, *refs
):
    hids = refs[: len(keys)]
    high_ref, low_ref, sum_ref, hid_ref, table_ref = refs[len(keys) :]
    cells = hid_ref.shape[0]
    panel_count = wd_ref.shape[0]

    @pl.when(pl.program_id(0) == 0)
    def _():
        place_cells(keys, me_ref[0], [block[...] for block in hids], hid_ref)
        table_ref[...] = panel_table(wd_ref, hid_ref[...], True)
        sum_ref[...] = jnp.zeros_like(sum_ref)

    both = dot_nn(panel_pick(col_ref, panel_count), table_ref[...])
    theta, log_theta = both[:, :cells], both[:, cells:]
    seen = counts_ref[...].astype(F32)
    rate, total, d_logit = rate_terms(
        dot_nt(wm_ref[...], hid_ref[...]), scale_ref[...], theta, seen, norm
    )
    high_ref[...], low_ref[...] = split2(d_logit)
    log_total = jnp.log(total)
    product = jnp.ones_like(theta)
    slope = jnp.zeros_like(theta)
    for k in range(COUNT_MOST):
        inverse = 1.0 / (k + 1.0)
        factor = theta * inverse + k * inverse
        here = seen > k
        slope = jnp.where(here, slope * factor + product * inverse, slope)
        product = jnp.where(here, product * factor, product)
    nll = -(
        jnp.log(product)
        + theta * (log_theta - log_total)
        + seen * (jnp.log(rate) - log_total)
    )
    d_theta = -(slope / product + log_theta + 1.0 - log_total - (theta + seen) / total)
    down = lax.broadcasted_iota(jnp.int32, (panel_count, theta.shape[0]), 0)
    pick = (down == row_ref[0]).astype(F32).astype(BF16)
    high, middle, low = split3(d_theta)
    sum_ref[:panel_count, :] += dot_nn(pick, high) + dot_nn(pick, middle) + dot_nn(pick, low)
    sum_ref[panel_count : panel_count + 1, :] += jnp.sum(nll, axis=0, keepdims=True)


def decode(me, keys, counts_t, panel_col, panel_row, rate_scale, w_mean_t, w_disp_t, hids, norm):
    genes, cells = counts_t.shape
    width = w_mean_t.shape[1]
    panel_count = w_disp_t.shape[0]
    steps, _, tile = panel_row.shape
    wide = -(-(panel_count + 1) // 8) * 8
    by_gene = lambda columns: pl.BlockSpec((tile, columns), lambda i: (i, 0))
    return launch(
        functools.partial(decode_kernel, keys, norm),
        (
            me,
            counts_t,
            panel_col,
            panel_row,
            rate_scale,
            w_mean_t,
            w_disp_t,
            *hids,
        ),
        [
            SCALAR,
            by_gene(cells),
            by_gene(1),
            pl.BlockSpec((1, 1, tile), lambda i: (i, 0, 0)),
            fixed(1, cells),
            by_gene(width),
            fixed(panel_count, width),
        ]
        + [fixed(*hids[0].shape)] * len(hids),
        grid=(steps,),
        out_shape=(
            shape_of((genes, cells), BF16),
            shape_of((genes, cells), BF16),
            shape_of((wide, cells), F32),
            shape_of((cells, width), BF16),
        ),
        out_specs=[by_gene(cells), by_gene(cells), fixed(wide, cells), fixed(cells, width)],
        scratch_shapes=[pltpu.VMEM((3 * panel_count, 2 * cells), BF16)],
        cost_estimate=pl.CostEstimate(
            flops=2 * genes * cells * width + 150 * genes * cells,
            bytes_accessed=genes * (width * 2 + cells * 8),
            transcendentals=8 * genes * cells,
        ),
    )


def far_kernel(keys, norm, genes_all, me_ref, first_ref, last_ref, col_ref, wm_ref, wd_ref, *refs):
    hids = refs[:2]
    high_ref, low_ref, hid_ref, table_ref = refs[2:]
    tile = wm_ref.shape[0]
    first_steps = first_ref.shape[0] // tile
    step = pl.program_id(0)
    late = jnp.maximum(step - first_steps, 0)
    early = jnp.minimum(step, first_steps - 1)
    first = first_ref[pl.ds(pl.multiple_of(early * tile, 16), tile), :].astype(F32)
    last = last_ref[pl.ds(pl.multiple_of(late * tile, 16), tile), :].astype(F32)
    seen = jnp.where(step < first_steps, first, last)
    lib = last_ref[last_ref.shape[0] - EXTRA :, :].astype(F32)
    panel_count = wd_ref.shape[0]

    @pl.when(pl.program_id(0) == 0)
    def _():
        blocks = [half[at, 0] for half in hids for at in range(half.shape[0])]
        place_cells(keys, me_ref[0], blocks, hid_ref)
        table_ref[...] = panel_table(wd_ref, hid_ref[...], False)

    library = jnp.sum(lib, axis=0, keepdims=True)
    _, _, d_logit = rate_terms(
        dot_nt(wm_ref[...], hid_ref[...]),
        library / genes_all,
        dot_nn(panel_pick(col_ref, panel_count), table_ref[...]),
        seen,
        norm,
    )
    high_ref[...], low_ref[...] = split2(d_logit)


def far_call(me, keys, other, seen, panel_col, w_mean_t, w_disp_t, hids, norm, genes_all):
    genes, width = w_mean_t.shape
    cells = seen[0].shape[1]
    panel_count = w_disp_t.shape[0]
    near, _, share, _ = hids[0].shape
    tile = tile_of(genes, 16, min(256, genes // 2))
    by_gene = lambda columns: pl.BlockSpec((tile, columns), lambda i: (i, 0))
    return launch(
        functools.partial(far_kernel, keys, norm, genes_all),
        (me, *seen, panel_col, w_mean_t, w_disp_t, *hids),
        [
            SCALAR,
            WHOLE,
            WHOLE,
            by_gene(1),
            by_gene(width),
            fixed(panel_count, width),
        ]
        + [pl.BlockSpec((near, 1, share, width), lambda i: (0, other, 0, 0))] * len(hids),
        grid=(genes // tile,),
        out_shape=(
            shape_of((genes, cells), BF16),
            shape_of((genes, cells), BF16),
            shape_of((cells, width), BF16),
        ),
        out_specs=[by_gene(cells), by_gene(cells), fixed(cells, width)],
        scratch_shapes=[pltpu.VMEM((3 * panel_count, cells), BF16)],
        cost_estimate=pl.CostEstimate(
            flops=2 * genes * cells * width + 60 * genes * cells,
            bytes_accessed=genes * (width * 2 + cells * 6),
            transcendentals=4 * genes * cells,
        ),
    )


def grad_kernel(place_ref, *refs):
    out_ref = refs[-1]
    mine, width = out_ref.shape[0], refs[0].shape[1]
    down = lax.broadcasted_iota(jnp.int32, (mine, width), 0) + place_ref[1] * mine
    over = lax.broadcasted_iota(jnp.int32, (mine, width), 1)
    pick = (down == over).astype(F32).astype(BF16)
    total = None
    for at in range(0, len(refs) - 1, 3):
        hidden = dot_nt(pick, refs[at][...]).astype(BF16)
        term = dot_nt(hidden, refs[at + 1][...]) + dot_nt(hidden, refs[at + 2][...])
        total = term if total is None else total + term
    out_ref[...] = total


def grad_mean_call(place, groups):
    cells, width = groups[0][0].shape
    genes = groups[0][1].shape[0]
    mine = width // len(groups)
    return launch(
        grad_kernel,
        (place, *[array for group in groups for array in group]),
        [SCALAR] + [WHOLE] * 3 * len(groups),
        params=LARGE,
        out_shape=shape_of((mine, genes), F32),
        out_specs=WHOLE,
        cost_estimate=pl.CostEstimate(
            flops=2 * len(groups) * cells * mine * (width + 2 * genes),
            bytes_accessed=len(groups) * cells * (width + 2 * genes) * 2 + mine * genes * 4,
            transcendentals=0,
        ),
    )


def disp_kernel(norm, genes_all, place_ref, wd_ref, *refs):
    count = (len(refs) - 3) // 2
    sums, hids = refs[:count], refs[count : 2 * count]
    grad_ref, loss_ref, term_ref = refs[2 * count :]
    panel_count = wd_ref.shape[0]
    for other in range(count):
        hidden = hids[other][...]
        d_disp = sums[other][:panel_count] * sigmoid(dot_nt(wd_ref[...], hidden)) * norm
        high, middle, low = split3(d_disp)
        term_ref[place_ref[1] ^ other] = (
            dot_nn(high, hidden) + dot_nn(middle, hidden) + dot_nn(low, hidden)
        )
    total = term_ref[0]
    for block in range(1, count):
        total = total + term_ref[block]
    grad_ref[...] = total
    loss_ref[...] = sums[0][panel_count : panel_count + 1] * (1.0 / genes_all)


def disp_call(place, sums, hids, w_disp_t, norm, genes_all, after):
    panel_count, width = w_disp_t.shape
    cells = sums[0].shape[1]
    return launch(
        functools.partial(disp_kernel, norm, genes_all),
        (place, w_disp_t, *sums, *hids),
        [SCALAR] + [WHOLE] * (1 + len(sums) + len(hids)),
        after,
        out_shape=(shape_of((panel_count, width), F32), shape_of((1, cells), F32)),
        out_specs=[WHOLE] * 2,
        scratch_shapes=[pltpu.VMEM((len(sums), panel_count, width), F32)],
    )


def add_kernel(left_ref, right_ref, out_ref):
    out_ref[...] = left_ref[...] + right_ref[...]


def add(left, right, after):
    return launch(
        add_kernel,
        (left, right),
        [WHOLE] * 2,
        after,
        out_shape=shape_of(left.shape, left.dtype),
        out_specs=WHOLE,
    )


def stack_kernel(*refs):
    for at, ref in enumerate(refs[:-1]):
        refs[-1][at] = ref[...]


def stack(parts, after):
    return launch(
        stack_kernel,
        parts,
        [WHOLE] * len(parts),
        after,
        out_shape=shape_of((len(parts),) + parts[0].shape, parts[0].dtype),
        out_specs=WHOLE,
    )


def flat_qkv(weights):
    return weights.transpose(2, 1, 0).reshape(-1, weights.shape[0])


def flat_out(weights):
    return weights.transpose(1, 0, 2).reshape(-1, weights.shape[2])


def shards(
    counts,
    panels,
    membership,
    w_proj,
    w_qkv_within,
    w_out_within,
    w_qkv_cross,
    w_out_cross,
    w_mean,
    w_disp,
):
    cells, genes_here = counts.shape
    width, heads, triple = w_qkv_within.shape
    head_width = triple // 3
    modules = w_proj.shape[1] // width
    gene_count = lax.axis_size("gene")
    grp_count = lax.axis_size("grp")
    genes_all = genes_here * gene_count
    share = cells // gene_count
    panel_count = w_disp.shape[1]
    norm = float(cells * grp_count) ** (-0.5)
    gene_me = lax.axis_index("gene").astype(jnp.int32)
    grp_me = lax.axis_index("grp").astype(jnp.int32)
    me = gene_me.reshape(1)
    place = jnp.stack([gene_me, grp_me])
    keys = spread_keys(gene_count)
    far = far_keys(gene_count)

    counts_t = counts.T
    w_mean_t = w_mean.T
    w_disp_t = w_disp.T

    library = jnp.sum(counts_t.astype(F32), axis=0, keepdims=True)
    for bit in range(gene_count.bit_length() - 1):
        library = library + hop(library, "gene", straight(1 << bit))
    library = 1.0 + library
    flat_within = flat_qkv(w_qkv_within)
    flat_cross = flat_qkv(w_qkv_cross)
    out_within = lax.all_gather(flat_out(w_out_within), "gene")
    out_cross = lax.all_gather(flat_out(w_out_cross), "gene")

    cell_ids = jnp.tile(jnp.arange(share, dtype=jnp.int32), modules)
    odd = (gene_me & 1) == 1
    owners = gene_me ^ jnp.where(odd, jnp.array([o for _, o in keys]), jnp.array([e for e, _ in keys]))
    group_ids = jnp.take(membership.reshape(gene_count, share), owners, axis=0).reshape(-1)
    cell_ids = (cell_ids.reshape(-1, 1), cell_ids.reshape(1, -1))
    group_ids = (group_ids.reshape(-1, 1), group_ids.reshape(1, -1))
    tile = tile_of(genes_here, 16, min(256, genes_here // 2))
    panel_col = panels.reshape(genes_here, 1)
    panel_row = panels.reshape(genes_here // tile, 1, tile)

    halves = []
    for chunk in range(2):
        early = [flat_within, flat_cross, *cell_ids, *group_ids, panel_col, panel_row]
        keep, send = project(
            me, counts_t, TARGET / library, w_proj, keys, chunk, 2, early if chunk == 0 else []
        )
        halves.append((keep, hop(send, "gene", straight(1))))
    parts = jnp.concatenate([p.astype(F32) for p in split3(library)], axis=0)
    parts = jnp.pad(parts, ((0, EXTRA - parts.shape[0]), (0, 0)))
    middle = genes_here // tile // 2 * tile
    seen_parts = [
        counts_t[:middle].astype(BF16),
        jnp.concatenate([counts_t[middle:].astype(F32), parts], axis=0).astype(BF16),
    ]
    seen = [
        [hop(part, "grp", straight(rel)) for part in seen_parts] for rel in range(1, grp_count)
    ]
    every = [part for pair in seen[1:] for part in pair]
    waits = [every[at::4] for at in range(4)] + [seen[0]]
    for key in far[::-1]:
        nexts = []
        for chunk, (keep, got) in enumerate(halves):
            keep, send = halve(keep, got)
            nexts.append((keep, hop(send, "gene", key)))
        halves = nexts
    resid, normed = to_rows(halves, width, waits[0])

    in_cell = [[(block, m) for m in range(modules)] for block in range(gene_count)]
    across = [[(block, m) for block in range(gene_count)] for m in range(modules)]

    def send_mixed(mixed):
        return [mixed] + [hop(mixed[at], "gene", keys[at]) for at in range(1, gene_count)]

    mixed = attend(
        spread(normed, "gene"), flat_within, cell_ids, in_cell, heads, head_width, waits[1]
    )
    rows = (modules, share, width)
    mid, normed = out_call(
        out_kernel,
        me,
        keys,
        send_mixed(mixed),
        out_within,
        resid,
        [shape_of(rows, F32), shape_of(rows, BF16)],
        waits[2],
    )

    mixed = attend(
        spread(normed, "gene"),
        flat_cross,
        group_ids,
        across,
        heads,
        head_width,
        waits[3],
    )
    (hidden,) = out_call(
        pool_kernel, me, keys, send_mixed(mixed), out_cross, mid, [shape_of((share, width), BF16)], waits[4]
    )

    hids = spread(hidden, "gene")
    far_hids = [stack([hop(hidden, "grp", straight(rel)) for rel in range(1, grp_count)], hids)]
    far_hids += [hop(far_hids[0], "gene", key) for key in keys[1 : gene_count // 2]]
    high, low, sums, own_hid = decode(
        me, keys, counts_t, panel_col, panel_row, library / genes_all, w_mean_t, w_disp_t, hids, norm
    )
    groups = [(own_hid, high, low)]
    far_hids = [stack(far_hids, [high])]
    far_hids.append(hop(far_hids[0], "gene", straight(1)))
    for other in range(grp_count - 1):
        high, low, hid = far_call(
            me, keys, other, seen[other], panel_col, w_mean_t, w_disp_t, far_hids, norm, genes_all
        )
        groups.append((hid, high, low))
    bits = gene_count.bit_length() - 1
    for bit in range(bits):
        after = [groups[1][1]] if bit == bits - 1 else []
        sums = add(sums, hop(sums, "gene", straight(1 << bit)), after)
    sums = [sums] + [hop(sums, "grp", straight(rel)) for rel in range(1, grp_count)]
    grad_mean = grad_mean_call(place, groups)
    grad_disp, loss = disp_call(
        place, sums, [group[0] for group in groups], w_disp_t, norm, genes_all, [grad_mean]
    )
    return (loss.reshape(cells), grad_mean, grad_disp.T)


def solution(mesh):
    return jax.shard_map(
        shards,
        mesh=mesh,
        in_specs=(
            P("grp", "gene"),
            P("gene"),
            P("grp", None),
            P("gene", None),
            P(None, "gene", None),
            P("gene", None, None),
            P(None, "gene", None),
            P("gene", None, None),
            P(None, "gene"),
            P(),
        ),
        out_specs=(P("grp"), P("grp", "gene"), P()),
        check_vma=False,
    )
```

time: 683 us -> 293 us (0.43)
  waiting for transfers between devices: 421 us -> 104 us
  matrix products: 89.2 us -> 0 us
  starting transfers between devices: 0.87 us -> 68.6 us
  Pallas kernels: 0 us -> 58.1 us
  local copies, waits for them, and re-layouts: 92.9 us -> 44.7 us
  blocking collectives: 38 us -> 0 us
  other arithmetic: 19.6 us -> 2.34 us
    reduce_scatter x3 -> x0, waiting for transfers between devices: 244 us -> none  [the longest x1 117 us: shards(): lax.psum_scatter(lax.dot_general(block, d_logit, dims, precision=lax.Prec...]
    psum x3 -> x0, waiting for transfers between devices: 160 us -> none  [the longest x1 91.3 us: shards(): tokens = lax.psum(partial_value, 'gene')]
    ppermute x0 -> x63, waiting for transfers between devices: none -> 104 us  [hop(): return lax.ppermute(value, axis, [(i, i ^ key[i & 1]) for i in range(size)])]
    dot_general x15 -> x0, matrix products: 89.2 us -> none  [the longest x1 19.3 us: shards(): jnp.dot(DISP_BASE + jax.nn.softplus(disp), onehot, precision=lax.Precisio...]
    ppermute x0 -> x63, starting transfers between devices: none -> 68.5 us  [hop(): return lax.ppermute(value, axis, [(i, i ^ key[i & 1]) for i in range(size)])]
    pallas_call x0 -> x22, Pallas kernels: none -> 58.1 us  [launch(): pl.pallas_call(body, in_specs=list(in_specs) + [UNREAD] * len(after), com...]
    reshape x9 -> x5, local copies, waits for them, and re-layouts: 35.9 us -> 5.82 us  [the longest x2 5.45 us: flat_qkv(): return weights.transpose(2, 1, 0).reshape(-1, weights.shape[0])]
    psum x2 -> x0, blocking collectives: 27.4 us -> none  [the longest x1 15.1 us: shards(): library = 1.0 + lax.psum(jnp.sum(observed, axis=1), 'gene')]
  transfers between devices with their start and end apart: 7 -> 65, of which waited for: 7 -> 24; matrix products, arithmetic and copies ran while one was open for 6% -> 4% of each run, Pallas kernels for 0% -> 17%
where the time goes in v1:
time: 293 us; the launch traced here: 292 us
  waiting for transfers between devices  104 us (35%)
  starting transfers between devices  68.6 us (23%)
  Pallas kernels  58.1 us (20%)
  local copies, waits for them, and re-layouts  44.7 us (15%)
  between operations  14.7 us (5%)
    ppermute x63, waiting for transfers between devices, hop(): return lax.ppermute(value, axis, [(i, i ^ key[i & 1]) for i in range(size)])  104 us
    ppermute x63, starting transfers between devices, hop(): return lax.ppermute(value, axis, [(i, i ^ key[i & 1]) for i in range(size)])  68.5 us
    pallas_call x22, Pallas kernels, launch(): pl.pallas_call(body, in_specs=list(in_specs) + [UNREAD] * len(after), com...  58.1 us
    unnamed x123, local copies, waits for them, and re-layouts  32.6 us
  transfers between devices with their start and end apart: 65, of which 24 were waited for; matrix products, arithmetic and copies ran while one was open for 4% of the time, Pallas kernels for 17%

profile of v1, /device:TPU:0, one launch (start us, length us, event | category | flops | bytes accessed | tf_op | source)
XLA Modules:
  0.0 292.4 jit_solution(9359658016341953749)
XLA Ops:
  7.2 2.2 all_gather_reshape.7
  9.6 2.4 all_gather_reshape.6
  13.4 2.8 collective-permute-start.1
  18.6 1.8 collective-permute-start.2
  21.7 2.4 reshape.74.refs_4_.refs_0_
  24.1 3.0 %reshape.75.refs_5_.refs_0_ = bf16[600,1600]{1,0:T(8,128)(2,1)S(1)} reshape(bf16[150,4,1600]{2,1,0:T(4,128)(2,1)} %bitcast.56) | data formatting | bytes 3840000 | tf_op jit(solution)/shard_map/reshape | solution.py:621
  28.1 4.5 %copy-done.1 = bf16[960,6400]{1,0:T(8,128)(2,1)S(1)} copy-done((bf16[960,6400]{1,0:T(8,128)(2,1)S(1)}, bf16[960,6400]{1,0:T(8,128)(2,1)}, u32[]{:S(2)}) %copy-start.1) | copy-done | bytes 12288024
  32.6 1.6 copy-done.8
  35.0 4.2 %shard_map.139 = (f32[128,3200]{1,0:T(8,128)S(1)}, f32[128,3200]{1,0:T(8,128)S(1)}) custom-call(s32[1]{0:T(128)} %bitcast.refs_0_, s32[960,256]{1,0:T(8,128)S(1)} %bitcast.46, f32[1,256]{1,0:T(1,128)S(1)} %get-tuple-element.87.refs_2_, bf16[960,6400]{1,0:T(8,128)(2,1)S(1)} %copy-done.1, bf16[600,1600]{1,0:T(8,128)(2,1)S(1)} %copy-done.8, ...), custom_call_target="tpu_custom_call" | custom-call | flops 1572864000 | bytes 9420800 | tf_op jit(solution)/shard_map/pallas_call | solution.py:39
  39.3 4.2 %shard_map.142 = (f32[128,3200]{1,0:T(8,128)S(1)}, f32[128,3200]{1,0:T(8,128)S(1)}) custom-call(s32[1]{0:T(128)} %bitcast.refs_0_, s32[960,256]{1,0:T(8,128)S(1)} %bitcast.47, f32[1,256]{1,0:T(1,128)S(1)} %get-tuple-element.87.refs_2_, bf16[960,6400]{1,0:T(8,128)(2,1)S(1)} %copy-done.1), custom_call_target="tpu_custom_call" | custom-call | flops 1572864000 | bytes 9420800 | tf_op jit(solution)/shard_map/pallas_call | solution.py:39
  44.5 2.8 collective-permute-done.6.refs_1_
  47.9 2.9 collective-permute-start.9
  50.7 6.0 %collective-permute-done.4.refs_1_ = bf16[64,3200]{1,0:T(8,128)(2,1)S(1)} collective-permute-done((bf16[64,3200]{1,0:T(8,128)(2,1)S(1)}, bf16[64,3200]{1,0:T(8,128)(2,1)S(1)}, u32[]{:S(2)}, u32[]{:S(2)}) %collective-permute-start.4) | collective-permute-done | bytes 409632 | tf_op jit(solution)/shard_map/ppermute | solution.py:98
  56.8 1.5 collective-permute-start.5
  58.3 4.2 %collective-permute-done.7.refs_1_ = bf16[64,3200]{1,0:T(8,128)(2,1)S(1)} collective-permute-done((bf16[64,3200]{1,0:T(8,128)(2,1)S(1)}, bf16[64,3200]{1,0:T(8,128)(2,1)S(1)}, u32[]{:S(2)}, u32[]{:S(2)}) %collective-permute-start.7) | collective-permute-done | bytes 409632 | tf_op jit(solution)/shard_map/ppermute | solution.py:98
  62.6 2.3 collective-permute-start.8
  64.9 5.3 %collective-permute-done.8.refs_3_ = bf16[32,3200]{1,0:T(8,128)(2,1)S(1)} collective-permute-done((bf16[32,3200]{1,0:T(8,128)(2,1)S(1)}, bf16[32,3200]{1,0:T(8,128)(2,1)S(1)}, u32[]{:S(2)}, u32[]{:S(2)}) %collective-permute-start.8) | collective-permute-done | bytes 204832 | tf_op jit(solution)/shard_map/ppermute | solution.py:98
  71.8 2.5 collective-permute-start.10
  74.2 11.3 %collective-permute-done.10.refs_4_ = bf16[4,32,1600]{2,1,0:T(8,128)(2,1)S(1)} collective-permute-done((bf16[4,32,1600]{2,1,0:T(8,128)(2,1)S(1)}, bf16[4,32,1600]{2,1,0:T(8,128)(2,1)S(1)}, u32[]{:S(2)}, u32[]{:S(2)}) %collective-permute-start.10) | collective-permute-done | bytes 409632 | tf_op jit(solution)/shard_map/ppermute | solution.py:98
  85.6 1.4 collective-permute-start.12
  87.5 14.5 %collective-permute-done.12.refs_6_ = bf16[4,32,1600]{2,1,0:T(8,128)(2,1)S(1)} collective-permute-done((bf16[4,32,1600]{2,1,0:T(8,128)(2,1)S(1)}, bf16[4,32,1600]{2,1,0:T(8,128)(2,1)S(1)}, u32[]{:S(2)}, u32[]{:S(2)}) %collective-permute-start.12) | collective-permute-done | bytes 409632 | tf_op jit(solution)/shard_map/ppermute | solution.py:98
  102.1 2.5 collective-permute-start.17
  104.6 12.5 %collective-permute-done.17.refs_11_.refs_2_ = bf16[496,256]{1,0:T(8,128)(2,1)S(1)} collective-permute-done((bf16[496,256]{1,0:T(8,128)(2,1)S(1)}, bf16[496,256]{1,0:T(8,128)(2,1)S(1)}, u32[]{:S(2)}, u32[]{:S(2)}) %collective-permute-start.17) | collective-permute-done | bytes 253984 | tf_op jit(solution)/shard_map/ppermute | solution.py:98
  117.1 3.3 %collective-permute-start.25 = (bf16[480,256]{1,0:T(8,128)(2,1)S(1)}, bf16[480,256]{1,0:T(8,128)(2,1)S(1)}, u32[]{:S(2)}, u32[]{:S(2)}) collective-permute-start(bf16[480,256]{1,0:T(8,128)(2,1)S(1)} %get-tuple-element.70), channel_id=1, source_target_pairs={{0,24},{8,16},{16,8},{24,0},{1,25},{9,17},{17,9},{25,1},{2,26},{10... | collective-permute-start | bytes 737288 | tf_op jit(solution)/shard_map/ppermute | solution.py:98
  120.4 5.6 %shard_map.146.refs_3_ = bf16[8,128,200]{2,1,0:T(8,128)(2,1)S(1)} custom-call(bf16[600,1600]{1,0:T(8,128)(2,1)S(1)} %copy-done.9, s32[128,1]{1,0:T(8,128)S(1)} %reshape_tile.12.refs_6_.refs_1_, s32[1,128]{1,0:T(1,128)S(1)} %reshape_tile.11.refs_7_.refs_2_, bf16[4,32,1600]{2,1,0:T(8,128)(2,1)S(1)} %get-tuple-element.47.refs_3_, ...), custom_call_target="tpu_custom_call" | custom-call | flops 2385510400 | bytes 5606400 | tf_op jit(solution)/shard_map/pallas_call | solution.py:39
  128.2 1.4 collective-permute-start.20
  129.6 2.1 collective-permute-start.22
  131.8 1.4 collective-permute-start.24
  133.6 1.8 collective-permute-done.23.refs_9_
  136.4 2.5 copy-done.11
  138.9 1.2 copy-done.27
  140.1 1.3 shard_map.147
  141.4 1.6 collective-permute-start.26
  143.0 2.0 collective-permute-start.27
  145.1 8.1 %collective-permute-done.26.refs_4_ = bf16[4,32,1600]{2,1,0:T(8,128)(2,1)S(1)} collective-permute-done((bf16[4,32,1600]{2,1,0:T(8,128)(2,1)S(1)}, bf16[4,32,1600]{2,1,0:T(8,128)(2,1)S(1)}, u32[]{:S(2)}, u32[]{:S(2)}) %collective-permute-start.26) | collective-permute-done | bytes 409632 | tf_op jit(solution)/shard_map/ppermute | solution.py:98
  153.2 3.0 %collective-permute-start.28 = (bf16[4,32,1600]{2,1,0:T(8,128)(2,1)S(1)}, bf16[4,32,1600]{2,1,0:T(8,128)(2,1)S(1)}, u32[]{:S(2)}, u32[]{:S(2)}) collective-permute-start(bf16[4,32,1600]{2,1,0:T(8,128)(2,1)S(1)} %collective-permute-done.26.refs_4_), channel_id=1, source_target_pairs={{0,4},{1,3},{2,6},{3,1},{4,0},{5,7},{6,2},{7,5},{8,12},{9,11},{10,... | collective-permute-start | bytes 1228808 | tf_op jit(solution)/shard_map/ppermute | solution.py:98
  156.7 5.6 %collective-permute-done.28.refs_6_ = bf16[4,32,1600]{2,1,0:T(8,128)(2,1)S(1)} collective-permute-done((bf16[4,32,1600]{2,1,0:T(8,128)(2,1)S(1)}, bf16[4,32,1600]{2,1,0:T(8,128)(2,1)S(1)}, u32[]{:S(2)}, u32[]{:S(2)}) %collective-permute-start.28) | collective-permute-done | bytes 409632 | tf_op jit(solution)/shard_map/ppermute | solution.py:98
  162.7 10.0 %collective-permute-done.33.refs_11_.refs_2_ = bf16[496,256]{1,0:T(8,128)(2,1)S(1)} collective-permute-done((bf16[496,256]{1,0:T(8,128)(2,1)S(1)}, bf16[496,256]{1,0:T(8,128)(2,1)S(1)}, u32[]{:S(2)}, u32[]{:S(2)}) %collective-permute-start.33) | collective-permute-done | bytes 253984 | tf_op jit(solution)/shard_map/ppermute | solution.py:98
  172.7 4.6 %collective-permute-start.41 = (bf16[480,256]{1,0:T(8,128)(2,1)S(1)}, bf16[480,256]{1,0:T(8,128)(2,1)S(1)}, u32[]{:S(2)}, u32[]{:S(2)}) collective-permute-start(bf16[480,256]{1,0:T(8,128)(2,1)S(1)} %copy-done.56), channel_id=1, source_target_pairs={{0,8},{8,0},{16,24},{24,16},{1,9},{9,1},{17,25},{25,17},{2,10},{10... | collective-permute-start | bytes 737288 | tf_op jit(solution)/shard_map/ppermute | solution.py:98
  177.4 5.4 %shard_map.148.refs_3_ = bf16[8,128,200]{2,1,0:T(8,128)(2,1)S(1)} custom-call(bf16[600,1600]{1,0:T(8,128)(2,1)S(1)} %reshape.75.refs_5_.refs_0_, s32[256,1]{1,0:T(8,128)S(1)} %copy-done.33, s32[1,256]{1,0:T(1,128)S(1)} %select_n.42.refs_9_.refs_2_, bf16[4,32,1600]{2,1,0:T(8,128)(2,1)S(1)} %get-tuple-element.49.refs_3_, ...), custom_call_target="tpu_custom_call" | custom-call | flops 2804940800 | bytes 5606400 | tf_op jit(solution)/shard_map/pallas_call | solution.py:39
  184.9 2.3 collective-permute-start.36
  189.8 1.2 collective-permute-start.39
  194.3 2.0 collective-permute-done.40.refs_10_
  196.9 2.5 copy-done.10
  207.7 1.3 shard_map.149.refs_7_.refs_3_
  210.3 1.7 collective-permute-start.53
  212.1 2.8 collective-permute-done.43.refs_8_.refs_4_
  215.8 1.6 collective-permute-start.54
  217.4 2.4 collective-permute-start.55
  220.4 4.9 %collective-permute-done.54.refs_1_ = bf16[32,1600]{1,0:T(8,128)(2,1)S(1)} collective-permute-done((bf16[32,1600]{1,0:T(8,128)(2,1)S(1)}, bf16[32,1600]{1,0:T(8,128)(2,1)S(1)}, u32[]{:S(2)}, u32[]{:S(2)}) %collective-permute-start.54) | collective-permute-done | bytes 102432 | tf_op jit(solution)/shard_map/ppermute | solution.py:98
  226.4 1.2 collective-permute-start.57
  227.5 1.4 collective-permute-start.58
  228.9 8.4 %shard_map.150 = (bf16[960,256]{1,0:T(8,128)(2,1)S(1)}, bf16[960,256]{1,0:T(8,128)(2,1)S(1)}, f32[72,256]{1,0:T(8,128)S(1)}, bf16[256,1600]{1,0:T(8,128)(2,1)S(1)}) custom-call(s32[1]{0:T(128)} %bitcast.refs_0_, s32[960,256]{1,0:T(8,128)S(1)} %bitcast.49, s32[960,1]{1,0:T(8,128)S(1)} %copy-done.5, s32[4,1,240]{2,1,0:T(1,128)S(1)} %reshape.73.refs_11_.refs_3_, ...), custom_call_target="tpu_custom_call" | custom-call | flops 823296000 | bytes 5038080 | tf_op jit(solution)/shard_map/pallas_call | solution.py:39
  237.4 2.3 collective-permute-done.57.refs_2_
  241.3 2.2 collective-permute-done.50.refs_1_
  243.8 4.3 %collective-permute-done.51.refs_1_ = f32[72,256]{1,0:T(8,128)S(1)} collective-permute-done((f32[72,256]{1,0:T(8,128)S(1)}, f32[72,256]{1,0:T(8,128)S(1)}, u32[]{:S(2)}, u32[]{:S(2)}) %collective-permute-start.51) | collective-permute-done | bytes 73760 | tf_op jit(solution)/shard_map/ppermute | solution.py:98
  252.2 4.7 %shard_map.155 = (bf16[960,256]{1,0:T(8,128)(2,1)S(1)}, bf16[960,256]{1,0:T(8,128)(2,1)S(1)}, bf16[256,1600]{1,0:T(8,128)(2,1)S(1)}) custom-call(s32[1]{0:T(128)} %bitcast.refs_0_, bf16[480,256]{1,0:T(8,128)(2,1)S(1)} %copy-done.23, bf16[496,256]{1,0:T(8,128)(2,1)S(1)} %copy-done.18, s32[960,1]{1,0:T(8,128)S(1)} %copy-done.6, ...), custom_call_target="tpu_custom_call" | custom-call | flops 801177600 | bytes 4546560 | tf_op jit(solution)/shard_map/pallas_call | solution.py:39
  257.0 3.9 %collective-permute-start.60 = (f32[72,256]{1,0:T(8,128)S(1)}, f32[72,256]{1,0:T(8,128)S(1)}, u32[]{:S(2)}, u32[]{:S(2)}) collective-permute-start(f32[72,256]{1,0:T(8,128)S(1)} %shard_map.156.refs_2_), channel_id=1, source_target_pairs={{0,8},{8,0},{16,24},{24,16},{1,9},{9,1},{17,25},{25,17},{2,10},{10... | collective-permute-start | bytes 221192 | tf_op jit(solution)/shard_map/ppermute | solution.py:98
  260.9 2.4 collective-permute-start.62
  263.3 4.6 %shard_map.158 = (bf16[960,256]{1,0:T(8,128)(2,1)S(1)}, bf16[960,256]{1,0:T(8,128)(2,1)S(1)}, bf16[256,1600]{1,0:T(8,128)(2,1)S(1)}) custom-call(s32[1]{0:T(128)} %bitcast.refs_0_, bf16[480,256]{1,0:T(8,128)(2,1)S(1)} %copy-done.25, bf16[496,256]{1,0:T(8,128)(2,1)S(1)} %copy-done.39, s32[960,1]{1,0:T(8,128)S(1)} %copy-done.7, ...), custom_call_target="tpu_custom_call" | custom-call | flops 801177600 | bytes 4546560 | tf_op jit(solution)/shard_map/pallas_call | solution.py:39
  268.0 4.8 %shard_map.157 = (bf16[960,256]{1,0:T(8,128)(2,1)S(1)}, bf16[960,256]{1,0:T(8,128)(2,1)S(1)}, bf16[256,1600]{1,0:T(8,128)(2,1)S(1)}) custom-call(s32[1]{0:T(128)} %bitcast.refs_0_, bf16[480,256]{1,0:T(8,128)(2,1)S(1)} %copy-done.20, bf16[496,256]{1,0:T(8,128)(2,1)S(1)} %copy-done.37, s32[960,1]{1,0:T(8,128)S(1)} %copy-done.7, ...), custom_call_target="tpu_custom_call" | custom-call | flops 801177600 | bytes 4546560 | tf_op jit(solution)/shard_map/pallas_call | solution.py:39
  272.8 6.2 %shard_map.159.refs_10_ = f32[400,960]{1,0:T(8,128)} custom-call(s32[2]{0:T(128)S(1)} %pad_add_fusion.refs_0_, bf16[256,1600]{1,0:T(8,128)(2,1)S(1)} %copy-done.29, bf16[960,256]{1,0:T(8,128)(2,1)S(1)} %copy-done.35, bf16[960,256]{1,0:T(8,128)(2,1)S(1)} %copy-done.51, bf16[256,1600]{1,0:T(8,128)(2,1)S(1)} %get-tuple-element.54.refs_4_.refs_7_, ...), custom_call_target="tpu_custom_call" | custom-call | flops 2883584000 | bytes 8744960 | tf_op jit(solution)/shard_map/pallas_call | solution.py:39
  279.0 1.4 copy-done.15
  280.5 5.1 %shard_map.160 = (f32[64,1600]{1,0:T(8,128)}, f32[1,256]{1,0:T(1,128)}) custom-call(s32[2]{0:T(128)S(1)} %pad_add_fusion.refs_0_, bf16[64,1600]{1,0:T(8,128)(2,1)S(1)} %bitcast.54, f32[72,256]{1,0:T(8,128)S(1)} %shard_map.156.refs_2_, f32[72,256]{1,0:T(8,128)S(1)} %collective-permute-done.60.refs_3_, f32[72,256]{1,0:T(8,128)S(1)} %collective-permute-done.61.refs_4_, ...), custom_call_target="tpu_custom_call" | custom-call | tf_op jit(solution)/shard_map/pallas_call | solution.py:39
  (242 shorter events, 42.7 us)
Async XLA Ops:
  7.2 129.3 %all-gather.5.cloned.1.call-start = ((), (), s32[]{:S(2)}) async-start(), calls=%async_computation.1 | async-start | bytes 5990400 | tf_op jit(solution)/shard_map/all_gather | solution.py:667
  9.5 182.1 %all-gather.3.cloned.1.call-start = ((), (), s32[]{:S(2)}) async-start(), calls=%async_computation | async-start | bytes 5990400 | tf_op jit(solution)/shard_map/all_gather | solution.py:668
  13.4 4.6 %collective-permute-start.1 = (f32[1,256]{1,0:T(1,128)S(1)}, f32[1,256]{1,0:T(1,128)S(1)}, u32[]{:S(2)}, u32[]{:S(2)}) collective-permute-start(f32[1,256]{1,0:T(1,128)S(1)} %add.21), channel_id=1, source_target_pairs={{0,2},{1,3},{2,0},{3,1},{4,6},{5,7},{6,4},{7,5},{8,10},{9,11},{10,... | collective-permute-start | bytes 3080 | tf_op jit(solution)/shard_map/ppermute | solution.py:98
  18.6 8.7 %collective-permute-start.2 = (f32[1,256]{1,0:T(1,128)}, f32[1,256]{1,0:T(1,128)}, u32[]{:S(2)}, u32[]{:S(2)}) collective-permute-start(f32[1,256]{1,0:T(1,128)} %add.22), channel_id=1, source_target_pairs={{0,4},{1,5},{2,6},{3,7},{4,0},{5,1},{6,2},{7,3},{8,12},{9,13},{10,... | collective-permute-start | bytes 3080 | tf_op jit(solution)/shard_map/ppermute | solution.py:98
  39.2 4.8 %collective-permute-start.3 = (f32[128,3200]{1,0:T(8,128)S(1)}, f32[128,3200]{1,0:T(8,128)S(1)}, u32[]{:S(2)}, u32[]{:S(2)}) collective-permute-start(f32[128,3200]{1,0:T(8,128)S(1)} %get-tuple-element.35), channel_id=1, source_target_pairs={{0,1},{1,0},{2,3},{3,2},{4,5},{5,4},{6,7},{7,6},{8,9},{9,8},{10,11... | collective-permute-start | bytes 4915208 | tf_op jit(solution)/shard_map/ppermute | solution.py:98
  43.4 3.8 %collective-permute-start.6 = (f32[128,3200]{1,0:T(8,128)S(1)}, f32[128,3200]{1,0:T(8,128)S(1)}, u32[]{:S(2)}, u32[]{:S(2)}) collective-permute-start(f32[128,3200]{1,0:T(8,128)S(1)} %get-tuple-element.41), channel_id=1, source_target_pairs={{0,1},{1,0},{2,3},{3,2},{4,5},{5,4},{6,7},{7,6},{8,9},{9,8},{10,11... | collective-permute-start | bytes 4915208 | tf_op jit(solution)/shard_map/ppermute | solution.py:98
  44.2 12.5 %collective-permute-start.4 = (bf16[64,3200]{1,0:T(8,128)(2,1)S(1)}, bf16[64,3200]{1,0:T(8,128)(2,1)S(1)}, u32[]{:S(2)}, u32[]{:S(2)}) collective-permute-start(bf16[64,3200]{1,0:T(8,128)(2,1)S(1)} %get-tuple-element.37), channel_id=1, source_target_pairs={{0,4},{1,3},{2,6},{3,1},{4,0},{5,7},{6,2},{7,5},{8,12},{9,11},{10,... | collective-permute-start | bytes 1228808 | tf_op jit(solution)/shard_map/ppermute | solution.py:98
  47.5 15.0 %collective-permute-start.7 = (bf16[64,3200]{1,0:T(8,128)(2,1)S(1)}, bf16[64,3200]{1,0:T(8,128)(2,1)S(1)}, u32[]{:S(2)}, u32[]{:S(2)}) collective-permute-start(bf16[64,3200]{1,0:T(8,128)(2,1)S(1)} %get-tuple-element.43), channel_id=1, source_target_pairs={{0,4},{1,3},{2,6},{3,1},{4,0},{5,7},{6,2},{7,5},{8,12},{9,11},{10,... | collective-permute-start | bytes 1228808 | tf_op jit(solution)/shard_map/ppermute | solution.py:98
  47.9 17.0 %collective-permute-start.9 = (bf16[480,256]{1,0:T(8,128)(2,1)S(1)}, bf16[480,256]{1,0:T(8,128)(2,1)S(1)}, u32[]{:S(2)}, u32[]{:S(2)}) collective-permute-start(bf16[480,256]{1,0:T(8,128)(2,1)S(1)} %get-tuple-element.70), channel_id=1, source_target_pairs={{0,16},{8,24},{16,0},{24,8},{1,17},{9,25},{17,1},{25,9},{2,18},{10... | collective-permute-start | bytes 737288 | tf_op jit(solution)/shard_map/ppermute | solution.py:98
  56.8 8.1 %collective-permute-start.5 = (bf16[32,3200]{1,0:T(8,128)(2,1)S(1)}, bf16[32,3200]{1,0:T(8,128)(2,1)S(1)}, u32[]{:S(2)}, u32[]{:S(2)}) collective-permute-start(bf16[32,3200]{1,0:T(8,128)(2,1)S(1)} %get-tuple-element.39), channel_id=1, source_target_pairs={{0,2},{1,5},{2,0},{3,7},{4,6},{5,1},{6,4},{7,3},{8,10},{9,13},{10,... | collective-permute-start | bytes 614408 | tf_op jit(solution)/shard_map/ppermute | solution.py:98
  62.6 7.6 %collective-permute-start.8 = (bf16[32,3200]{1,0:T(8,128)(2,1)S(1)}, bf16[32,3200]{1,0:T(8,128)(2,1)S(1)}, u32[]{:S(2)}, u32[]{:S(2)}) collective-permute-start(bf16[32,3200]{1,0:T(8,128)(2,1)S(1)} %get-tuple-element.45), channel_id=1, source_target_pairs={{0,2},{1,5},{2,0},{3,7},{4,6},{5,1},{6,4},{7,3},{8,10},{9,13},{10,... | collective-permute-start | bytes 614408 | tf_op jit(solution)/shard_map/ppermute | solution.py:98
  71.8 13.8 %collective-permute-start.10 = (bf16[4,32,1600]{2,1,0:T(8,128)(2,1)S(1)}, bf16[4,32,1600]{2,1,0:T(8,128)(2,1)S(1)}, u32[]{:S(2)}, u32[]{:S(2)}) collective-permute-start(bf16[4,32,1600]{2,1,0:T(8,128)(2,1)S(1)} %get-tuple-element.47.refs_3_), channel_id=1, source_target_pairs={{0,2},{1,5},{2,0},{3,7},{4,6},{5,1},{6,4},{7,3},{8,10},{9,13},{10,... | collective-permute-start | bytes 1228808 | tf_op jit(solution)/shard_map/ppermute | solution.py:98
  74.2 13.3 %collective-permute-start.11 = (bf16[4,32,1600]{2,1,0:T(8,128)(2,1)S(1)}, bf16[4,32,1600]{2,1,0:T(8,128)(2,1)S(1)}, u32[]{:S(2)}, u32[]{:S(2)}) collective-permute-start(bf16[4,32,1600]{2,1,0:T(8,128)(2,1)S(1)} %get-tuple-element.47.refs_3_), channel_id=1, source_target_pairs={{0,4},{1,3},{2,6},{3,1},{4,0},{5,7},{6,2},{7,5},{8,12},{9,11},{10,... | collective-permute-start | bytes 1228808 | tf_op jit(solution)/shard_map/ppermute | solution.py:98
  85.6 16.5 %collective-permute-start.12 = (bf16[4,32,1600]{2,1,0:T(8,128)(2,1)S(1)}, bf16[4,32,1600]{2,1,0:T(8,128)(2,1)S(1)}, u32[]{:S(2)}, u32[]{:S(2)}) collective-permute-start(bf16[4,32,1600]{2,1,0:T(8,128)(2,1)S(1)} %collective-permute-done.10.refs_4_), channel_id=1, source_target_pairs={{0,4},{1,3},{2,6},{3,1},{4,0},{5,7},{6,2},{7,5},{8,12},{9,11},{10,... | collective-permute-start | bytes 1228808 | tf_op jit(solution)/shard_map/ppermute | solution.py:98
  87.0 33.4 %collective-permute-start.13 = (bf16[4,32,1600]{2,1,0:T(8,128)(2,1)S(1)}, bf16[4,32,1600]{2,1,0:T(8,128)(2,1)S(1)}, u32[]{:S(2)}, u32[]{:S(2)}) collective-permute-start(bf16[4,32,1600]{2,1,0:T(8,128)(2,1)S(1)} %get-tuple-element.47.refs_3_), channel_id=1, source_target_pairs={{0,1},{1,0},{2,3},{3,2},{4,5},{5,4},{6,7},{7,6},{8,9},{9,8},{10,11... | collective-permute-start | bytes 1228808 | tf_op jit(solution)/shard_map/ppermute | solution.py:98
  87.0 33.4 %collective-permute-start.14 = (bf16[4,32,1600]{2,1,0:T(8,128)(2,1)S(1)}, bf16[4,32,1600]{2,1,0:T(8,128)(2,1)S(1)}, u32[]{:S(2)}, u32[]{:S(2)}) collective-permute-start(bf16[4,32,1600]{2,1,0:T(8,128)(2,1)S(1)} %collective-permute-done.10.refs_4_), channel_id=1, source_target_pairs={{0,1},{1,0},{2,3},{3,2},{4,5},{5,4},{6,7},{7,6},{8,9},{9,8},{10,11... | collective-permute-start | bytes 1228808 | tf_op jit(solution)/shard_map/ppermute | solution.py:98
  87.5 32.9 %collective-permute-start.15 = (bf16[4,32,1600]{2,1,0:T(8,128)(2,1)S(1)}, bf16[4,32,1600]{2,1,0:T(8,128)(2,1)S(1)}, u32[]{:S(2)}, u32[]{:S(2)}) collective-permute-start(bf16[4,32,1600]{2,1,0:T(8,128)(2,1)S(1)} %collective-permute-done.11.refs_5_), channel_id=1, source_target_pairs={{0,1},{1,0},{2,3},{3,2},{4,5},{5,4},{6,7},{7,6},{8,9},{9,8},{10,11... | collective-permute-start | bytes 1228808 | tf_op jit(solution)/shard_map/ppermute | solution.py:98
  102.1 18.3 %collective-permute-start.16 = (bf16[4,32,1600]{2,1,0:T(8,128)(2,1)S(1)}, bf16[4,32,1600]{2,1,0:T(8,128)(2,1)S(1)}, u32[]{:S(2)}, u32[]{:S(2)}) collective-permute-start(bf16[4,32,1600]{2,1,0:T(8,128)(2,1)S(1)} %collective-permute-done.12.refs_6_), channel_id=1, source_target_pairs={{0,1},{1,0},{2,3},{3,2},{4,5},{5,4},{6,7},{7,6},{8,9},{9,8},{10,11... | collective-permute-start | bytes 1228808 | tf_op jit(solution)/shard_map/ppermute | solution.py:98
  102.1 14.9 %collective-permute-start.17 = (bf16[496,256]{1,0:T(8,128)(2,1)S(1)}, bf16[496,256]{1,0:T(8,128)(2,1)S(1)}, u32[]{:S(2)}, u32[]{:S(2)}) collective-permute-start(bf16[496,256]{1,0:T(8,128)(2,1)S(1)} %pad_maximum_fusion), channel_id=1, source_target_pairs={{0,16},{8,24},{16,0},{24,8},{1,17},{9,25},{17,1},{25,9},{2,18},{10... | collective-permute-start | bytes 761864 | tf_op jit(solution)/shard_map/ppermute | solution.py:98
  117.1 12.5 %collective-permute-start.25 = (bf16[480,256]{1,0:T(8,128)(2,1)S(1)}, bf16[480,256]{1,0:T(8,128)(2,1)S(1)}, u32[]{:S(2)}, u32[]{:S(2)}) collective-permute-start(bf16[480,256]{1,0:T(8,128)(2,1)S(1)} %get-tuple-element.70), channel_id=1, source_target_pairs={{0,24},{8,16},{16,8},{24,0},{1,25},{9,17},{17,9},{25,1},{2,26},{10... | collective-permute-start | bytes 737288 | tf_op jit(solution)/shard_map/ppermute | solution.py:98
  126.0 5.6 %collective-permute-start.18 = (bf16[128,200]{1,0:T(8,128)(2,1)S(1)}, bf16[128,200]{1,0:T(8,128)(2,1)S(1)}, u32[]{:S(2)}, u32[]{:S(2)}) collective-permute-start(bf16[128,200]{1,0:T(8,128)(2,1)S(1)} %get-tuple-element.84), channel_id=1, source_target_pairs={{0,2},{1,5},{2,0},{3,7},{4,6},{5,1},{6,4},{7,3},{8,10},{9,13},{10,... | collective-permute-start | bytes 153608 | tf_op jit(solution)/shard_map/ppermute | solution.py:98
  127.2 4.6 %collective-permute-start.19 = (bf16[128,200]{1,0:T(8,128)(2,1)S(1)}, bf16[128,200]{1,0:T(8,128)(2,1)S(1)}, u32[]{:S(2)}, u32[]{:S(2)}) collective-permute-start(bf16[128,200]{1,0:T(8,128)(2,1)S(1)} %get-tuple-element.83), channel_id=1, source_target_pairs={{0,4},{1,3},{2,6},{3,1},{4,0},{5,7},{6,2},{7,5},{8,12},{9,11},{10,... | collective-permute-start | bytes 153608 | tf_op jit(solution)/shard_map/ppermute | solution.py:98
  128.2 5.2 %collective-permute-start.20 = (bf16[128,200]{1,0:T(8,128)(2,1)S(1)}, bf16[128,200]{1,0:T(8,128)(2,1)S(1)}, u32[]{:S(2)}, u32[]{:S(2)}) collective-permute-start(bf16[128,200]{1,0:T(8,128)(2,1)S(1)} %get-tuple-element.82), channel_id=1, source_target_pairs={{0,6},{1,7},{2,4},{3,5},{4,2},{5,3},{6,0},{7,1},{8,14},{9,15},{10,... | collective-permute-start | bytes 153608 | tf_op jit(solution)/shard_map/ppermute | solution.py:98
  129.6 3.7 %collective-permute-start.21 = (bf16[128,200]{1,0:T(8,128)(2,1)S(1)}, bf16[128,200]{1,0:T(8,128)(2,1)S(1)}, u32[]{:S(2)}, u32[]{:S(2)}) collective-permute-start(bf16[128,200]{1,0:T(8,128)(2,1)S(1)} %get-tuple-element.81), channel_id=1, source_target_pairs={{0,1},{1,0},{2,3},{3,2},{4,5},{5,4},{6,7},{7,6},{8,9},{9,8},{10,11... | collective-permute-start | bytes 153608 | tf_op jit(solution)/shard_map/ppermute | solution.py:98
  129.6 4.0 %collective-permute-start.22 = (bf16[128,200]{1,0:T(8,128)(2,1)S(1)}, bf16[128,200]{1,0:T(8,128)(2,1)S(1)}, u32[]{:S(2)}, u32[]{:S(2)}) collective-permute-start(bf16[128,200]{1,0:T(8,128)(2,1)S(1)} %get-tuple-element.80), channel_id=1, source_target_pairs={{0,5},{1,2},{2,7},{3,0},{4,1},{5,6},{6,3},{7,4},{8,13},{9,10},{10,... | collective-permute-start | bytes 153608 | tf_op jit(solution)/shard_map/ppermute | solution.py:98
  131.7 3.7 %collective-permute-start.23 = (bf16[128,200]{1,0:T(8,128)(2,1)S(1)}, bf16[128,200]{1,0:T(8,128)(2,1)S(1)}, u32[]{:S(2)}, u32[]{:S(2)}) collective-permute-start(bf16[128,200]{1,0:T(8,128)(2,1)S(1)} %get-tuple-element.79), channel_id=1, source_target_pairs={{0,3},{1,4},{2,1},{3,6},{4,7},{5,0},{6,5},{7,2},{8,11},{9,12},{10,... | collective-permute-start | bytes 153608 | tf_op jit(solution)/shard_map/ppermute | solution.py:98
  131.8 4.6 %collective-permute-start.24 = (bf16[128,200]{1,0:T(8,128)(2,1)S(1)}, bf16[128,200]{1,0:T(8,128)(2,1)S(1)}, u32[]{:S(2)}, u32[]{:S(2)}) collective-permute-start(bf16[128,200]{1,0:T(8,128)(2,1)S(1)} %get-tuple-element.78), channel_id=1, source_target_pairs={{0,7},{1,6},{2,5},{3,4},{4,3},{5,2},{6,1},{7,0},{8,15},{9,14},{10,... | collective-permute-start | bytes 153608 | tf_op jit(solution)/shard_map/ppermute | solution.py:98
  141.4 11.8 %collective-permute-start.26 = (bf16[4,32,1600]{2,1,0:T(8,128)(2,1)S(1)}, bf16[4,32,1600]{2,1,0:T(8,128)(2,1)S(1)}, u32[]{:S(2)}, u32[]{:S(2)}) collective-permute-start(bf16[4,32,1600]{2,1,0:T(8,128)(2,1)S(1)} %get-tuple-element.49.refs_3_), channel_id=1, source_target_pairs={{0,2},{1,5},{2,0},{3,7},{4,6},{5,1},{6,4},{7,3},{8,10},{9,13},{10,... | collective-permute-start | bytes 1228808 | tf_op jit(solution)/shard_map/ppermute | solution.py:98
  143.0 13.7 %collective-permute-start.27 = (bf16[4,32,1600]{2,1,0:T(8,128)(2,1)S(1)}, bf16[4,32,1600]{2,1,0:T(8,128)(2,1)S(1)}, u32[]{:S(2)}, u32[]{:S(2)}) collective-permute-start(bf16[4,32,1600]{2,1,0:T(8,128)(2,1)S(1)} %get-tuple-element.49.refs_3_), channel_id=1, source_target_pairs={{0,4},{1,3},{2,6},{3,1},{4,0},{5,7},{6,2},{7,5},{8,12},{9,11},{10,... | collective-permute-start | bytes 1228808 | tf_op jit(solution)/shard_map/ppermute | solution.py:98
  153.2 9.1 %collective-permute-start.28 = (bf16[4,32,1600]{2,1,0:T(8,128)(2,1)S(1)}, bf16[4,32,1600]{2,1,0:T(8,128)(2,1)S(1)}, u32[]{:S(2)}, u32[]{:S(2)}) collective-permute-start(bf16[4,32,1600]{2,1,0:T(8,128)(2,1)S(1)} %collective-permute-done.26.refs_4_), channel_id=1, source_target_pairs={{0,4},{1,3},{2,6},{3,1},{4,0},{5,7},{6,2},{7,5},{8,12},{9,11},{10,... | collective-permute-start | bytes 1228808 | tf_op jit(solution)/shard_map/ppermute | solution.py:98
  156.2 21.1 %collective-permute-start.29 = (bf16[4,32,1600]{2,1,0:T(8,128)(2,1)S(1)}, bf16[4,32,1600]{2,1,0:T(8,128)(2,1)S(1)}, u32[]{:S(2)}, u32[]{:S(2)}) collective-permute-start(bf16[4,32,1600]{2,1,0:T(8,128)(2,1)S(1)} %get-tuple-element.49.refs_3_), channel_id=1, source_target_pairs={{0,1},{1,0},{2,3},{3,2},{4,5},{5,4},{6,7},{7,6},{8,9},{9,8},{10,11... | collective-permute-start | bytes 1228808 | tf_op jit(solution)/shard_map/ppermute | solution.py:98
  156.2 21.2 %collective-permute-start.30 = (bf16[4,32,1600]{2,1,0:T(8,128)(2,1)S(1)}, bf16[4,32,1600]{2,1,0:T(8,128)(2,1)S(1)}, u32[]{:S(2)}, u32[]{:S(2)}) collective-permute-start(bf16[4,32,1600]{2,1,0:T(8,128)(2,1)S(1)} %collective-permute-done.26.refs_4_), channel_id=1, source_target_pairs={{0,1},{1,0},{2,3},{3,2},{4,5},{5,4},{6,7},{7,6},{8,9},{9,8},{10,11... | collective-permute-start | bytes 1228808 | tf_op jit(solution)/shard_map/ppermute | solution.py:98
  156.7 20.7 %collective-permute-start.31 = (bf16[4,32,1600]{2,1,0:T(8,128)(2,1)S(1)}, bf16[4,32,1600]{2,1,0:T(8,128)(2,1)S(1)}, u32[]{:S(2)}, u32[]{:S(2)}) collective-permute-start(bf16[4,32,1600]{2,1,0:T(8,128)(2,1)S(1)} %collective-permute-done.27.refs_5_), channel_id=1, source_target_pairs={{0,1},{1,0},{2,3},{3,2},{4,5},{5,4},{6,7},{7,6},{8,9},{9,8},{10,11... | collective-permute-start | bytes 1228808 | tf_op jit(solution)/shard_map/ppermute | solution.py:98
  162.3 15.1 %collective-permute-start.32 = (bf16[4,32,1600]{2,1,0:T(8,128)(2,1)S(1)}, bf16[4,32,1600]{2,1,0:T(8,128)(2,1)S(1)}, u32[]{:S(2)}, u32[]{:S(2)}) collective-permute-start(bf16[4,32,1600]{2,1,0:T(8,128)(2,1)S(1)} %collective-permute-done.28.refs_6_), channel_id=1, source_target_pairs={{0,1},{1,0},{2,3},{3,2},{4,5},{5,4},{6,7},{7,6},{8,9},{9,8},{10,11... | collective-permute-start | bytes 1228808 | tf_op jit(solution)/shard_map/ppermute | solution.py:98
  162.3 10.4 %collective-permute-start.33 = (bf16[496,256]{1,0:T(8,128)(2,1)S(1)}, bf16[496,256]{1,0:T(8,128)(2,1)S(1)}, u32[]{:S(2)}, u32[]{:S(2)}) collective-permute-start(bf16[496,256]{1,0:T(8,128)(2,1)S(1)} %copy-done.54), channel_id=1, source_target_pairs={{0,24},{8,16},{16,8},{24,0},{1,25},{9,17},{17,9},{25,1},{2,26},{10... | collective-permute-start | bytes 761864 | tf_op jit(solution)/shard_map/ppermute | solution.py:98
  172.7 14.4 %collective-permute-start.41 = (bf16[480,256]{1,0:T(8,128)(2,1)S(1)}, bf16[480,256]{1,0:T(8,128)(2,1)S(1)}, u32[]{:S(2)}, u32[]{:S(2)}) collective-permute-start(bf16[480,256]{1,0:T(8,128)(2,1)S(1)} %copy-done.56), channel_id=1, source_target_pairs={{0,8},{8,0},{16,24},{24,16},{1,9},{9,1},{17,25},{25,17},{2,10},{10... | collective-permute-start | bytes 737288 | tf_op jit(solution)/shard_map/ppermute | solution.py:98
  177.3 11.3 %collective-permute-start.42 = (bf16[496,256]{1,0:T(8,128)(2,1)S(1)}, bf16[496,256]{1,0:T(8,128)(2,1)S(1)}, u32[]{:S(2)}, u32[]{:S(2)}) collective-permute-start(bf16[496,256]{1,0:T(8,128)(2,1)S(1)} %copy-done.54), channel_id=1, source_target_pairs={{0,8},{8,0},{16,24},{24,16},{1,9},{9,1},{17,25},{25,17},{2,10},{10... | collective-permute-start | bytes 761864 | tf_op jit(solution)/shard_map/ppermute | solution.py:98
  183.7 6.1 %collective-permute-start.34 = (bf16[128,200]{1,0:T(8,128)(2,1)S(1)}, bf16[128,200]{1,0:T(8,128)(2,1)S(1)}, u32[]{:S(2)}, u32[]{:S(2)}) collective-permute-start(bf16[128,200]{1,0:T(8,128)(2,1)S(1)} %get-tuple-element.77), channel_id=1, source_target_pairs={{0,2},{1,5},{2,0},{3,7},{4,6},{5,1},{6,4},{7,3},{8,10},{9,13},{10,... | collective-permute-start | bytes 153608 | tf_op jit(solution)/shard_map/ppermute | solution.py:98
  184.7 6.3 %collective-permute-start.35 = (bf16[128,200]{1,0:T(8,128)(2,1)S(1)}, bf16[128,200]{1,0:T(8,128)(2,1)S(1)}, u32[]{:S(2)}, u32[]{:S(2)}) collective-permute-start(bf16[128,200]{1,0:T(8,128)(2,1)S(1)} %get-tuple-element.76), channel_id=1, source_target_pairs={{0,4},{1,3},{2,6},{3,1},{4,0},{5,7},{6,2},{7,5},{8,12},{9,11},{10,... | collective-permute-start | bytes 153608 | tf_op jit(solution)/shard_map/ppermute | solution.py:98
  184.9 6.8 %collective-permute-start.36 = (bf16[128,200]{1,0:T(8,128)(2,1)S(1)}, bf16[128,200]{1,0:T(8,128)(2,1)S(1)}, u32[]{:S(2)}, u32[]{:S(2)}) collective-permute-start(bf16[128,200]{1,0:T(8,128)(2,1)S(1)} %get-tuple-element.75), channel_id=1, source_target_pairs={{0,6},{1,7},{2,4},{3,5},{4,2},{5,3},{6,0},{7,1},{8,14},{9,15},{10,... | collective-permute-start | bytes 153608 | tf_op jit(solution)/shard_map/ppermute | solution.py:98
  187.9 4.4 %collective-permute-start.37 = (bf16[128,200]{1,0:T(8,128)(2,1)S(1)}, bf16[128,200]{1,0:T(8,128)(2,1)S(1)}, u32[]{:S(2)}, u32[]{:S(2)}) collective-permute-start(bf16[128,200]{1,0:T(8,128)(2,1)S(1)} %get-tuple-element.74), channel_id=1, source_target_pairs={{0,1},{1,0},{2,3},{3,2},{4,5},{5,4},{6,7},{7,6},{8,9},{9,8},{10,11... | collective-permute-start | bytes 153608 | tf_op jit(solution)/shard_map/ppermute | solution.py:98
  189.3 3.7 %collective-permute-start.38 = (bf16[128,200]{1,0:T(8,128)(2,1)S(1)}, bf16[128,200]{1,0:T(8,128)(2,1)S(1)}, u32[]{:S(2)}, u32[]{:S(2)}) collective-permute-start(bf16[128,200]{1,0:T(8,128)(2,1)S(1)} %get-tuple-element.73), channel_id=1, source_target_pairs={{0,5},{1,2},{2,7},{3,0},{4,1},{5,6},{6,3},{7,4},{8,13},{9,10},{10,... | collective-permute-start | bytes 153608 | tf_op jit(solution)/shard_map/ppermute | solution.py:98
  189.8 3.9 %collective-permute-start.39 = (bf16[128,200]{1,0:T(8,128)(2,1)S(1)}, bf16[128,200]{1,0:T(8,128)(2,1)S(1)}, u32[]{:S(2)}, u32[]{:S(2)}) collective-permute-start(bf16[128,200]{1,0:T(8,128)(2,1)S(1)} %get-tuple-element.72), channel_id=1, source_target_pairs={{0,3},{1,4},{2,1},{3,6},{4,7},{5,0},{6,5},{7,2},{8,11},{9,12},{10,... | collective-permute-start | bytes 153608 | tf_op jit(solution)/shard_map/ppermute | solution.py:98
  191.0 5.3 %collective-permute-start.40 = (bf16[128,200]{1,0:T(8,128)(2,1)S(1)}, bf16[128,200]{1,0:T(8,128)(2,1)S(1)}, u32[]{:S(2)}, u32[]{:S(2)}) collective-permute-start(bf16[128,200]{1,0:T(8,128)(2,1)S(1)} %get-tuple-element.71), channel_id=1, source_target_pairs={{0,7},{1,6},{2,5},{3,4},{4,3},{5,2},{6,1},{7,0},{8,15},{9,14},{10,... | collective-permute-start | bytes 153608 | tf_op jit(solution)/shard_map/ppermute | solution.py:98
  209.0 5.9 %collective-permute-start.43 = (bf16[32,1600]{1,0:T(8,128)(2,1)S(1)}, bf16[32,1600]{1,0:T(8,128)(2,1)S(1)}, u32[]{:S(2)}, u32[]{:S(2)}) collective-permute-start(bf16[32,1600]{1,0:T(8,128)(2,1)S(1)} %shard_map.149.refs_7_.refs_3_), channel_id=1, source_target_pairs={{0,2},{1,5},{2,0},{3,7},{4,6},{5,1},{6,4},{7,3},{8,10},{9,13},{10,... | collective-permute-start | bytes 307208 | tf_op jit(solution)/shard_map/ppermute | solution.py:98
  210.2 7.2 %collective-permute-start.44 = (bf16[32,1600]{1,0:T(8,128)(2,1)S(1)}, bf16[32,1600]{1,0:T(8,128)(2,1)S(1)}, u32[]{:S(2)}, u32[]{:S(2)}) collective-permute-start(bf16[32,1600]{1,0:T(8,128)(2,1)S(1)} %shard_map.149.refs_7_.refs_3_), channel_id=1, source_target_pairs={{0,4},{1,3},{2,6},{3,1},{4,0},{5,7},{6,2},{7,5},{8,12},{9,11},{10,... | collective-permute-start | bytes 307208 | tf_op jit(solution)/shard_map/ppermute | solution.py:98
  210.3 9.4 %collective-permute-start.46 = (bf16[32,1600]{1,0:T(8,128)(2,1)S(1)}, bf16[32,1600]{1,0:T(8,128)(2,1)S(1)}, u32[]{:S(2)}, u32[]{:S(2)}) collective-permute-start(bf16[32,1600]{1,0:T(8,128)(2,1)S(1)} %shard_map.149.refs_7_.refs_3_), channel_id=1, source_target_pairs={{0,1},{1,0},{2,3},{3,2},{4,5},{5,4},{6,7},{7,6},{8,9},{9,8},{10,11... | collective-permute-start | bytes 307208 | tf_op jit(solution)/shard_map/ppermute | solution.py:98
  210.3 9.4 %collective-permute-start.53 = (bf16[32,1600]{1,0:T(8,128)(2,1)S(1)}, bf16[32,1600]{1,0:T(8,128)(2,1)S(1)}, u32[]{:S(2)}, u32[]{:S(2)}) collective-permute-start(bf16[32,1600]{1,0:T(8,128)(2,1)S(1)} %shard_map.149.refs_7_.refs_3_), channel_id=1, source_target_pairs={{0,8},{8,0},{16,24},{24,16},{1,9},{9,1},{17,25},{25,17},{2,10},{10... | collective-permute-start | bytes 307208 | tf_op jit(solution)/shard_map/ppermute | solution.py:98
  214.9 5.4 %collective-permute-start.45 = (bf16[32,1600]{1,0:T(8,128)(2,1)S(1)}, bf16[32,1600]{1,0:T(8,128)(2,1)S(1)}, u32[]{:S(2)}, u32[]{:S(2)}) collective-permute-start(bf16[32,1600]{1,0:T(8,128)(2,1)S(1)} %collective-permute-done.43.refs_8_.refs_4_), channel_id=1, source_target_pairs={{0,4},{1,3},{2,6},{3,1},{4,0},{5,7},{6,2},{7,5},{8,12},{9,11},{10,... | collective-permute-start | bytes 307208 | tf_op jit(solution)/shard_map/ppermute | solution.py:98
  215.8 9.5 %collective-permute-start.54 = (bf16[32,1600]{1,0:T(8,128)(2,1)S(1)}, bf16[32,1600]{1,0:T(8,128)(2,1)S(1)}, u32[]{:S(2)}, u32[]{:S(2)}) collective-permute-start(bf16[32,1600]{1,0:T(8,128)(2,1)S(1)} %shard_map.149.refs_7_.refs_3_), channel_id=1, source_target_pairs={{0,16},{8,24},{16,0},{24,8},{1,17},{9,25},{17,1},{25,9},{2,18},{10... | collective-permute-start | bytes 307208 | tf_op jit(solution)/shard_map/ppermute | solution.py:98
  217.4 8.0 %collective-permute-start.55 = (bf16[32,1600]{1,0:T(8,128)(2,1)S(1)}, bf16[32,1600]{1,0:T(8,128)(2,1)S(1)}, u32[]{:S(2)}, u32[]{:S(2)}) collective-permute-start(bf16[32,1600]{1,0:T(8,128)(2,1)S(1)} %shard_map.149.refs_7_.refs_3_), channel_id=1, source_target_pairs={{0,24},{8,16},{16,8},{24,0},{1,25},{9,17},{17,9},{25,1},{2,26},{10... | collective-permute-start | bytes 307208 | tf_op jit(solution)/shard_map/ppermute | solution.py:98
  219.8 5.5 %collective-permute-start.47 = (bf16[32,1600]{1,0:T(8,128)(2,1)S(1)}, bf16[32,1600]{1,0:T(8,128)(2,1)S(1)}, u32[]{:S(2)}, u32[]{:S(2)}) collective-permute-start(bf16[32,1600]{1,0:T(8,128)(2,1)S(1)} %collective-permute-done.43.refs_8_.refs_4_), channel_id=1, source_target_pairs={{0,1},{1,0},{2,3},{3,2},{4,5},{5,4},{6,7},{7,6},{8,9},{9,8},{10,11... | collective-permute-start | bytes 307208 | tf_op jit(solution)/shard_map/ppermute | solution.py:98
  219.8 5.5 %collective-permute-start.48 = (bf16[32,1600]{1,0:T(8,128)(2,1)S(1)}, bf16[32,1600]{1,0:T(8,128)(2,1)S(1)}, u32[]{:S(2)}, u32[]{:S(2)}) collective-permute-start(bf16[32,1600]{1,0:T(8,128)(2,1)S(1)} %collective-permute-done.44.refs_9_.refs_5_), channel_id=1, source_target_pairs={{0,1},{1,0},{2,3},{3,2},{4,5},{5,4},{6,7},{7,6},{8,9},{9,8},{10,11... | collective-permute-start | bytes 307208 | tf_op jit(solution)/shard_map/ppermute | solution.py:98
  220.3 5.0 %collective-permute-start.49 = (bf16[32,1600]{1,0:T(8,128)(2,1)S(1)}, bf16[32,1600]{1,0:T(8,128)(2,1)S(1)}, u32[]{:S(2)}, u32[]{:S(2)}) collective-permute-start(bf16[32,1600]{1,0:T(8,128)(2,1)S(1)} %collective-permute-done.45.refs_10_.refs_6_), channel_id=1, source_target_pairs={{0,1},{1,0},{2,3},{3,2},{4,5},{5,4},{6,7},{7,6},{8,9},{9,8},{10,11... | collective-permute-start | bytes 307208 | tf_op jit(solution)/shard_map/ppermute | solution.py:98
  225.4 12.0 %collective-permute-start.56 = (bf16[3,32,1600]{2,1,0:T(8,128)(2,1)S(1)}, bf16[3,32,1600]{2,1,0:T(8,128)(2,1)S(1)}, u32[]{:S(2)}, u32[]{:S(2)}) collective-permute-start(bf16[3,32,1600]{2,1,0:T(8,128)(2,1)S(1)} %shard_map.153.refs_0_), channel_id=1, source_target_pairs={{0,2},{1,5},{2,0},{3,7},{4,6},{5,1},{6,4},{7,3},{8,10},{9,13},{10,... | collective-permute-start | bytes 921608 | tf_op jit(solution)/shard_map/ppermute | solution.py:98
  226.4 13.3 %collective-permute-start.57 = (bf16[3,32,1600]{2,1,0:T(8,128)(2,1)S(1)}, bf16[3,32,1600]{2,1,0:T(8,128)(2,1)S(1)}, u32[]{:S(2)}, u32[]{:S(2)}) collective-permute-start(bf16[3,32,1600]{2,1,0:T(8,128)(2,1)S(1)} %shard_map.153.refs_0_), channel_id=1, source_target_pairs={{0,4},{1,3},{2,6},{3,1},{4,0},{5,7},{6,2},{7,5},{8,12},{9,11},{10,... | collective-permute-start | bytes 921608 | tf_op jit(solution)/shard_map/ppermute | solution.py:98
  227.5 12.1 %collective-permute-start.58 = (bf16[3,32,1600]{2,1,0:T(8,128)(2,1)S(1)}, bf16[3,32,1600]{2,1,0:T(8,128)(2,1)S(1)}, u32[]{:S(2)}, u32[]{:S(2)}) collective-permute-start(bf16[3,32,1600]{2,1,0:T(8,128)(2,1)S(1)} %shard_map.153.refs_0_), channel_id=1, source_target_pairs={{0,6},{1,7},{2,4},{3,5},{4,2},{5,3},{6,0},{7,1},{8,14},{9,15},{10,... | collective-permute-start | bytes 921608 | tf_op jit(solution)/shard_map/ppermute | solution.py:98
  240.8 8.5 %collective-permute-start.59 = (bf16[4,3,32,1600]{3,2,1,0:T(8,128)(2,1)}, bf16[4,3,32,1600]{3,2,1,0:T(8,128)(2,1)}, u32[]{:S(2)}, u32[]{:S(2)}) collective-permute-start(bf16[4,3,32,1600]{3,2,1,0:T(8,128)(2,1)} %shard_map.154.refs_6_), channel_id=1, source_target_pairs={{0,1},{1,0},{2,3},{3,2},{4,5},{5,4},{6,7},{7,6},{8,9},{9,8},{10,11... | collective-permute-start | bytes 3686408 | tf_op jit(solution)/shard_map/ppermute | solution.py:98
  240.8 2.7 collective-permute-start.50
  243.6 4.6 %collective-permute-start.51 = (f32[72,256]{1,0:T(8,128)S(1)}, f32[72,256]{1,0:T(8,128)S(1)}, u32[]{:S(2)}, u32[]{:S(2)}) collective-permute-start(f32[72,256]{1,0:T(8,128)S(1)} %shard_map.151.refs_0_), channel_id=1, source_target_pairs={{0,2},{1,3},{2,0},{3,1},{4,6},{5,7},{6,4},{7,5},{8,10},{9,11},{10,... | collective-permute-start | bytes 221192 | tf_op jit(solution)/shard_map/ppermute | solution.py:98
  248.2 8.7 %collective-permute-start.52 = (f32[72,256]{1,0:T(8,128)S(1)}, f32[72,256]{1,0:T(8,128)S(1)}, u32[]{:S(2)}, u32[]{:S(2)}) collective-permute-start(f32[72,256]{1,0:T(8,128)S(1)} %shard_map.152.refs_0_), channel_id=1, source_target_pairs={{0,4},{1,5},{2,6},{3,7},{4,0},{5,1},{6,2},{7,3},{8,12},{9,13},{10,... | collective-permute-start | bytes 221192 | tf_op jit(solution)/shard_map/ppermute | solution.py:98
  257.0 22.0 %collective-permute-start.60 = (f32[72,256]{1,0:T(8,128)S(1)}, f32[72,256]{1,0:T(8,128)S(1)}, u32[]{:S(2)}, u32[]{:S(2)}) collective-permute-start(f32[72,256]{1,0:T(8,128)S(1)} %shard_map.156.refs_2_), channel_id=1, source_target_pairs={{0,8},{8,0},{16,24},{24,16},{1,9},{9,1},{17,25},{25,17},{2,10},{10... | collective-permute-start | bytes 221192 | tf_op jit(solution)/shard_map/ppermute | solution.py:98
  260.9 18.1 %collective-permute-start.61 = (f32[72,256]{1,0:T(8,128)S(1)}, f32[72,256]{1,0:T(8,128)S(1)}, u32[]{:S(2)}, u32[]{:S(2)}) collective-permute-start(f32[72,256]{1,0:T(8,128)S(1)} %shard_map.156.refs_2_), channel_id=1, source_target_pairs={{0,16},{8,24},{16,0},{24,8},{1,17},{9,25},{17,1},{25,9},{2,18},{10... | collective-permute-start | bytes 221192 | tf_op jit(solution)/shard_map/ppermute | solution.py:98
  260.9 18.1 %collective-permute-start.62 = (f32[72,256]{1,0:T(8,128)S(1)}, f32[72,256]{1,0:T(8,128)S(1)}, u32[]{:S(2)}, u32[]{:S(2)}) collective-permute-start(f32[72,256]{1,0:T(8,128)S(1)} %shard_map.156.refs_2_), channel_id=1, source_target_pairs={{0,24},{8,16},{16,8},{24,0},{1,25},{9,17},{17,9},{25,1},{2,26},{10... | collective-permute-start | bytes 221192 | tf_op jit(solution)/shard_map/ppermute | solution.py:98
  (62 other events, 618.6 us)
Sparse Core Ops, SparseCore 0:
  9.9 46.8 all-gather.4
  58.7 51.0 all-gather.2

commit v2 on v1

--- a/solution.py
+++ b/solution.py
@@ -209,14 +209,13 @@
             normed_ref[chunk * parts + at] = rms_rows(rows).astype(BF16)
 
 
-def to_rows(pairs, width, after):
+def to_rows(pairs, width):
     share, columns = pairs[0][0].shape
     shape = (len(pairs) * columns // width, share, width)
     return launch(
         functools.partial(rows_kernel, len(pairs)),
         [part for pair in pairs for part in pair],
         [WHOLE] * 2 * len(pairs),
-        after,
         out_shape=(shape_of(shape, F32), shape_of(shape, BF16)),
         out_specs=[WHOLE] * 2,
         cost_estimate=pl.CostEstimate(
@@ -272,7 +271,7 @@
             ]
 
 
-def attend(blocks, w_flat, ids, pieces, heads, head_width, after):
+def attend(blocks, w_flat, ids, pieces, heads, head_width):
     count = len(blocks)
     modules, share, width = blocks[0].shape
     rows = len(pieces[0]) * share
@@ -282,7 +281,6 @@
         functools.partial(attend_kernel, pieces, heads, head_width),
         (w_flat, *ids, *blocks),
         [WHOLE] * (3 + len(blocks)),
-        after,
         out_shape=shape_of((count, modules * share, used), BF16),
         out_specs=WHOLE,
         scratch_shapes=[pltpu.VMEM((every, width), BF16)] + [pltpu.VMEM((every, used), BF16)] * 3,
@@ -454,24 +452,21 @@
     )
 
 
-def far_kernel(keys, norm, genes_all, me_ref, first_ref, last_ref, col_ref, wm_ref, wd_ref, *refs):
+def far_kernel(keys, other, norm, genes_all, place_ref, seen_ref, col_ref, wm_ref, wd_ref, *refs):
     hids = refs[:2]
     high_ref, low_ref, hid_ref, table_ref = refs[2:]
     tile = wm_ref.shape[0]
-    first_steps = first_ref.shape[0] // tile
-    step = pl.program_id(0)
-    late = jnp.maximum(step - first_steps, 0)
-    early = jnp.minimum(step, first_steps - 1)
-    first = first_ref[pl.ds(pl.multiple_of(early * tile, 16), tile), :].astype(F32)
-    last = last_ref[pl.ds(pl.multiple_of(late * tile, 16), tile), :].astype(F32)
-    seen = jnp.where(step < first_steps, first, last)
-    lib = last_ref[last_ref.shape[0] - EXTRA :, :].astype(F32)
+    genes = seen_ref.shape[1] - EXTRA
+    block = place_ref[1] ^ other
+    at = pl.ds(pl.multiple_of(pl.program_id(0) * tile, 16), tile)
+    seen = seen_ref[block, at, :].astype(F32)
+    lib = seen_ref[block, genes:, :].astype(F32)
     panel_count = wd_ref.shape[0]
 
     @pl.when(pl.program_id(0) == 0)
     def _():
         blocks = [half[at, 0] for half in hids for at in range(half.shape[0])]
-        place_cells(keys, me_ref[0], blocks, hid_ref)
+        place_cells(keys, place_ref[0], blocks, hid_ref)
         table_ref[...] = panel_table(wd_ref, hid_ref[...], False)
 
     library = jnp.sum(lib, axis=0, keepdims=True)
@@ -485,19 +480,18 @@
     high_ref[...], low_ref[...] = split2(d_logit)
 
 
-def far_call(me, keys, other, seen, panel_col, w_mean_t, w_disp_t, hids, norm, genes_all):
+def far_call(place, keys, other, seen, panel_col, w_mean_t, w_disp_t, hids, norm, genes_all):
     genes, width = w_mean_t.shape
-    cells = seen[0].shape[1]
+    cells = seen.shape[2]
     panel_count = w_disp_t.shape[0]
     near, _, share, _ = hids[0].shape
-    tile = tile_of(genes, 16, min(256, genes // 2))
+    tile = tile_of(genes, 16, 256)
     by_gene = lambda columns: pl.BlockSpec((tile, columns), lambda i: (i, 0))
     return launch(
-        functools.partial(far_kernel, keys, norm, genes_all),
-        (me, *seen, panel_col, w_mean_t, w_disp_t, *hids),
+        functools.partial(far_kernel, keys, other + 1, norm, genes_all),
+        (place, seen, panel_col, w_mean_t, w_disp_t, *hids),
         [
             SCALAR,
-            WHOLE,
             WHOLE,
             by_gene(1),
             by_gene(width),
@@ -583,6 +577,26 @@
         out_shape=(shape_of((panel_count, width), F32), shape_of((1, cells), F32)),
         out_specs=[WHOLE] * 2,
         scratch_shapes=[pltpu.VMEM((len(sums), panel_count, width), F32)],
+    )
+
+
+def pack_kernel(counts_ref, library_ref, out_ref):
+    genes, cells = counts_ref.shape
+    out_ref[:genes, :] = counts_ref[...].astype(F32).astype(BF16)
+    parts = [part.astype(F32) for part in split3(library_ref[...])]
+    parts.append(jnp.zeros((EXTRA - len(parts), cells), F32))
+    out_ref[genes:, :] = jnp.concatenate(parts, axis=0).astype(BF16)
+
+
+def pack(counts_t, library, after):
+    genes, cells = counts_t.shape
+    return launch(
+        pack_kernel,
+        (counts_t, library),
+        [WHOLE] * 2,
+        after,
+        out_shape=shape_of((genes + EXTRA, cells), BF16),
+        out_specs=WHOLE,
     )
 
 
@@ -665,44 +679,32 @@
     flat_within = flat_qkv(w_qkv_within)
     flat_cross = flat_qkv(w_qkv_cross)
     out_within = lax.all_gather(flat_out(w_out_within), "gene")
-    out_cross = lax.all_gather(flat_out(w_out_cross), "gene")
-
     cell_ids = jnp.tile(jnp.arange(share, dtype=jnp.int32), modules)
     odd = (gene_me & 1) == 1
     owners = gene_me ^ jnp.where(odd, jnp.array([o for _, o in keys]), jnp.array([e for e, _ in keys]))
     group_ids = jnp.take(membership.reshape(gene_count, share), owners, axis=0).reshape(-1)
     cell_ids = (cell_ids.reshape(-1, 1), cell_ids.reshape(1, -1))
     group_ids = (group_ids.reshape(-1, 1), group_ids.reshape(1, -1))
-    tile = tile_of(genes_here, 16, min(256, genes_here // 2))
+    tile = tile_of(genes_here, 16, 256)
     panel_col = panels.reshape(genes_here, 1)
     panel_row = panels.reshape(genes_here // tile, 1, tile)
 
     halves = []
     for chunk in range(2):
-        early = [flat_within, flat_cross, *cell_ids, *group_ids, panel_col, panel_row]
+        early = [*cell_ids, *group_ids, panel_col, panel_row]
         keep, send = project(
             me, counts_t, TARGET / library, w_proj, keys, chunk, 2, early if chunk == 0 else []
         )
         halves.append((keep, hop(send, "gene", straight(1))))
-    parts = jnp.concatenate([p.astype(F32) for p in split3(library)], axis=0)
-    parts = jnp.pad(parts, ((0, EXTRA - parts.shape[0]), (0, 0)))
-    middle = genes_here // tile // 2 * tile
-    seen_parts = [
-        counts_t[:middle].astype(BF16),
-        jnp.concatenate([counts_t[middle:].astype(F32), parts], axis=0).astype(BF16),
-    ]
-    seen = [
-        [hop(part, "grp", straight(rel)) for part in seen_parts] for rel in range(1, grp_count)
-    ]
-    every = [part for pair in seen[1:] for part in pair]
-    waits = [every[at::4] for at in range(4)] + [seen[0]]
-    for key in far[::-1]:
+    seen = lax.all_gather(pack(counts_t, library, [halves[0][0]]), "grp")
+    laid = [flat_within, flat_cross]
+    for at, key in enumerate(far[::-1]):
         nexts = []
         for chunk, (keep, got) in enumerate(halves):
-            keep, send = halve(keep, got)
+            keep, send = halve(keep, got, laid[chunk : chunk + 1] if at == 1 else ())
             nexts.append((keep, hop(send, "gene", key)))
         halves = nexts
-    resid, normed = to_rows(halves, width, waits[0])
+    resid, normed = to_rows(halves, width)
 
     in_cell = [[(block, m) for m in range(modules)] for block in range(gene_count)]
     across = [[(block, m) for block in range(gene_count)] for m in range(modules)]
@@ -710,9 +712,10 @@
     def send_mixed(mixed):
         return [mixed] + [hop(mixed[at], "gene", keys[at]) for at in range(1, gene_count)]
 
-    mixed = attend(
-        spread(normed, "gene"), flat_within, cell_ids, in_cell, heads, head_width, waits[1]
-    )
+    blocks = spread(normed, "gene")
+    mixed = attend(blocks, flat_within, cell_ids, in_cell, heads, head_width)
+    out_cross = stack([flat_out(w_out_cross)], [mixed])[0]
+    out_cross = lax.all_gather(out_cross, "gene")
     rows = (modules, share, width)
     mid, normed = out_call(
         out_kernel,
@@ -722,7 +725,6 @@
         out_within,
         resid,
         [shape_of(rows, F32), shape_of(rows, BF16)],
-        waits[2],
     )
 
     mixed = attend(
@@ -732,10 +734,9 @@
         across,
         heads,
         head_width,
-        waits[3],
     )
     (hidden,) = out_call(
-        pool_kernel, me, keys, send_mixed(mixed), out_cross, mid, [shape_of((share, width), BF16)], waits[4]
+        pool_kernel, me, keys, send_mixed(mixed), out_cross, mid, [shape_of((share, width), BF16)], [seen]
     )
 
     hids = spread(hidden, "gene")
@@ -749,12 +750,12 @@
     far_hids.append(hop(far_hids[0], "gene", straight(1)))
     for other in range(grp_count - 1):
         high, low, hid = far_call(
-            me, keys, other, seen[other], panel_col, w_mean_t, w_disp_t, far_hids, norm, genes_all
+            place, keys, other, seen, panel_col, w_mean_t, w_disp_t, far_hids, norm, genes_all
         )
         groups.append((hid, high, low))
     bits = gene_count.bit_length() - 1
     for bit in range(bits):
-        after = [groups[1][1]] if bit == bits - 1 else []
+        after = [groups[min(bit, grp_count - 1)][1]]
         sums = add(sums, hop(sums, "gene", straight(1 << bit)), after)
     sums = [sums] + [hop(sums, "grp", straight(rel)) for rel in range(1, grp_count)]
     grad_mean = grad_mean_call(place, groups)

time: 293 us -> 275 us (0.939)
  waiting for transfers between devices: 104 us -> 80.3 us
  starting transfers between devices: 68.6 us -> 46.4 us
  local copies, waits for them, and re-layouts: 44.7 us -> 63 us
  Pallas kernels: 58.1 us -> 68.1 us
    ppermute x63 -> x57, waiting for transfers between devices: 104 us -> 80.3 us  [hop(): return lax.ppermute(value, axis, [(i, i ^ key[i & 1]) for i in range(size)])]
    ppermute x63 -> x57, starting transfers between devices: 68.5 us -> 46.1 us  [hop(): return lax.ppermute(value, axis, [(i, i ^ key[i & 1]) for i in range(size)])]
    unnamed x123 -> x139, local copies, waits for them, and re-layouts: 32.6 us -> 50.4 us
    pallas_call x22 -> x24, Pallas kernels: 58.1 us -> 68.1 us  [launch(): pl.pallas_call(body, in_specs=list(in_specs) + [UNREAD] * len(after), com...]
  transfers between devices with their start and end apart: 65 -> 60, of which waited for: 24 -> 24; matrix products, arithmetic and copies ran while one was open for 4% -> 4% of each run, Pallas kernels for 17% -> 22%
where the time goes in v2:
time: 275 us; the launch traced here: 273 us
  waiting for transfers between devices  80.3 us (29%)
  Pallas kernels  68.1 us (25%)
  local copies, waits for them, and re-layouts  63 us (23%)
  starting transfers between devices  46.4 us (17%)
  between operations  14.3 us (5%)
    ppermute x57, waiting for transfers between devices, hop(): return lax.ppermute(value, axis, [(i, i ^ key[i & 1]) for i in range(size)])  80.3 us
    pallas_call x24, Pallas kernels, launch(): pl.pallas_call(body, in_specs=list(in_specs) + [UNREAD] * len(after), com...  68.1 us
    unnamed x139, local copies, waits for them, and re-layouts  50.4 us
    ppermute x57, starting transfers between devices, hop(): return lax.ppermute(value, axis, [(i, i ^ key[i & 1]) for i in range(size)])  46.1 us
    reshape x2, local copies, waits for them, and re-layouts, flat_qkv(): return weights.transpose(2, 1, 0).reshape(-1, weights.shape[0])  7.35 us
  transfers between devices with their start and end apart: 60, of which 24 were waited for; matrix products, arithmetic and copies ran while one was open for 4% of the time, Pallas kernels for 22%

profile of v2, /device:TPU:0, one launch (start us, length us, event | category | flops | bytes accessed | tf_op | source)
XLA Modules:
  0.0 273.1 jit_solution(14725884761364194847)
XLA Ops:
  7.3 2.3 all_gather_reshape.3
  11.1 2.8 %collective-permute-start.1 = (f32[1,256]{1,0:T(1,128)S(1)}, f32[1,256]{1,0:T(1,128)S(1)}, u32[]{:S(2)}, u32[]{:S(2)}) collective-permute-start(f32[1,256]{1,0:T(1,128)S(1)} %add.19), channel_id=1, source_target_pairs={{0,2},{1,3},{2,0},{3,1},{4,6},{5,7},{6,4},{7,5},{8,10},{9,11},{10,... | collective-permute-start | bytes 3080 | tf_op jit(solution)/shard_map/ppermute | solution.py:98
  15.8 1.8 collective-permute-start.2
  19.4 4.9 %copy-done.1 = bf16[960,6400]{1,0:T(8,128)(2,1)S(1)} copy-done((bf16[960,6400]{1,0:T(8,128)(2,1)S(1)}, bf16[960,6400]{1,0:T(8,128)(2,1)}, u32[]{:S(2)}) %copy-start.1) | copy-done | bytes 12288024
  24.3 4.8 %shard_map.139 = (f32[128,3200]{1,0:T(8,128)S(1)}, f32[128,3200]{1,0:T(8,128)}) custom-call(s32[1]{0:T(128)} %bitcast.refs_0_, s32[960,256]{1,0:T(8,128)S(1)} %bitcast.51, f32[1,256]{1,0:T(1,128)S(1)} %get-tuple-element.67.refs_2_, bf16[960,6400]{1,0:T(8,128)(2,1)S(1)} %copy-done.1, s32[128,1]{1,0:T(8,128)S(1)} %reshape_tile.12.refs_4_.refs_1_, ...), custom_call_target="tpu_custom_call" | custom-call | flops 1572864000 | bytes 9420800 | tf_op jit(solution)/shard_map/pallas_call | solution.py:39
  29.1 4.8 %shard_map.142 = (f32[128,3200]{1,0:T(8,128)S(1)}, f32[128,3200]{1,0:T(8,128)}) custom-call(s32[1]{0:T(128)} %bitcast.refs_0_, s32[960,256]{1,0:T(8,128)S(1)} %bitcast.52, f32[1,256]{1,0:T(1,128)S(1)} %get-tuple-element.67.refs_2_, bf16[960,6400]{1,0:T(8,128)(2,1)S(1)} %copy-done.1), custom_call_target="tpu_custom_call" | custom-call | flops 1572864000 | bytes 9420800 | tf_op jit(solution)/shard_map/pallas_call | solution.py:39
  33.9 1.2 copy-done.23
  36.7 2.3 shard_map.140
  39.9 1.7 collective-permute-start.4
  41.6 1.4 copy-done.24
  43.1 2.4 shard_map.143
  47.3 4.3 %reshape.78.refs_2_.refs_0_ = bf16[600,1600]{1,0:T(8,128)(2,1)} reshape(bf16[150,4,1600]{2,1,0:T(4,128)(2,1)} %bitcast.60) | data formatting | bytes 3840000 | tf_op jit(solution)/shard_map/reshape | solution.py:635
  51.5 3.1 %reshape.80.refs_2_.refs_0_ = bf16[600,1600]{1,0:T(8,128)(2,1)S(1)} reshape(bf16[150,4,1600]{2,1,0:T(4,128)(2,1)} %bitcast.61) | data formatting | bytes 3840000 | tf_op jit(solution)/shard_map/reshape | solution.py:635
  54.7 2.0 collective-permute-done.4.refs_1_
  57.4 1.6 copy-done.11
  60.1 1.6 collective-permute-start.5
  62.7 1.1 collective-permute-start.8
  63.8 2.1 collective-permute-done.5.refs_1_
  65.9 2.6 collective-permute-done.8.refs_3_
  68.5 1.4 shard_map.145
  72.5 11.3 %collective-permute-done.9.refs_4_ = bf16[4,32,1600]{2,1,0:T(8,128)(2,1)S(1)} collective-permute-done((bf16[4,32,1600]{2,1,0:T(8,128)(2,1)}, bf16[4,32,1600]{2,1,0:T(8,128)(2,1)S(1)}, u32[]{:S(2)}, u32[]{:S(2)}) %collective-permute-start.9) | collective-permute-done | bytes 409632 | tf_op jit(solution)/shard_map/ppermute | solution.py:98
  84.4 7.6 %collective-permute-done.11.refs_6_ = bf16[4,32,1600]{2,1,0:T(8,128)(2,1)} collective-permute-done((bf16[4,32,1600]{2,1,0:T(8,128)(2,1)S(1)}, bf16[4,32,1600]{2,1,0:T(8,128)(2,1)}, u32[]{:S(2)}, u32[]{:S(2)}) %collective-permute-start.11) | collective-permute-done | bytes 409632 | tf_op jit(solution)/shard_map/ppermute | solution.py:98
  92.0 1.5 reshape.77.refs_0_
  94.2 1.6 copy-done.12
  96.7 7.3 %shard_map.146.refs_1_.refs_3_ = bf16[8,128,200]{2,1,0:T(8,128)(2,1)S(1)} custom-call(bf16[600,1600]{1,0:T(8,128)(2,1)S(1)} %copy-done.12, s32[128,1]{1,0:T(8,128)S(1)} %reshape_tile.12.refs_4_.refs_1_, s32[1,128]{1,0:T(1,128)S(1)} %reshape_tile.11.refs_5_.refs_2_, bf16[4,32,1600]{2,1,0:T(8,128)(2,1)} %get-tuple-element.46.refs_3_, ...), custom_call_target="tpu_custom_call" | custom-call | flops 2385510400 | bytes 5606400 | tf_op jit(solution)/shard_map/pallas_call | solution.py:39
  105.0 1.1 collective-permute-start.16
  106.2 2.4 collective-permute-start.18
  115.4 3.6 %collective-permute-done.22.refs_10_ = bf16[128,200]{1,0:T(8,128)(2,1)S(1)} collective-permute-done((bf16[128,200]{1,0:T(8,128)(2,1)S(1)}, bf16[128,200]{1,0:T(8,128)(2,1)S(1)}, u32[]{:S(2)}, u32[]{:S(2)}) %collective-permute-start.22) | collective-permute-done | bytes 51232 | tf_op jit(solution)/shard_map/ppermute | solution.py:98
  119.6 2.5 copy-done.13
  128.0 1.3 shard_map.148
  130.2 20.3 %collective-permute-done.23.refs_4_ = bf16[4,32,1600]{2,1,0:T(8,128)(2,1)S(1)} collective-permute-done((bf16[4,32,1600]{2,1,0:T(8,128)(2,1)S(1)}, bf16[4,32,1600]{2,1,0:T(8,128)(2,1)S(1)}, u32[]{:S(2)}, u32[]{:S(2)}) %collective-permute-start.23) | collective-permute-done | bytes 409632 | tf_op jit(solution)/shard_map/ppermute | solution.py:98
  151.3 8.5 %collective-permute-done.25.refs_6_ = bf16[4,32,1600]{2,1,0:T(8,128)(2,1)S(1)} collective-permute-done((bf16[4,32,1600]{2,1,0:T(8,128)(2,1)S(1)}, bf16[4,32,1600]{2,1,0:T(8,128)(2,1)S(1)}, u32[]{:S(2)}, u32[]{:S(2)}) %collective-permute-start.25) | collective-permute-done | bytes 409632 | tf_op jit(solution)/shard_map/ppermute | solution.py:98
  159.9 1.6 collective-permute-done.29.refs_10_
  161.6 5.3 %shard_map.149.refs_3_ = bf16[8,128,200]{2,1,0:T(8,128)(2,1)S(1)} custom-call(bf16[600,1600]{1,0:T(8,128)(2,1)S(1)} %reshape.80.refs_2_.refs_0_, s32[256,1]{1,0:T(8,128)S(1)} %select_n.43.refs_6_.refs_1_, s32[1,256]{1,0:T(1,128)S(1)} %select_n.42.refs_7_.refs_2_, bf16[4,32,1600]{2,1,0:T(8,128)(2,1)S(1)} %get-tuple-element.49.refs_3_, ...), custom_call_target="tpu_custom_call" | custom-call | flops 2804940800 | bytes 5606400 | tf_op jit(solution)/shard_map/pallas_call | solution.py:39
  169.2 2.1 collective-permute-start.32
  173.1 1.3 collective-permute-done.31.refs_5_
  177.2 1.8 collective-permute-done.36.refs_10_
  179.7 1.6 copy-done.2
  181.2 2.5 copy-done.14
  184.8 1.2 copy-done.30
  190.1 1.3 shard_map.151.refs_7_.refs_3_
  191.4 1.1 collective-permute-start.37
  192.5 1.5 collective-permute-start.46
  194.0 2.5 collective-permute-done.37.refs_8_.refs_4_
  196.9 2.5 collective-permute-start.47
  199.4 1.4 collective-permute-start.48
  201.5 5.4 %collective-permute-done.47.refs_1_ = bf16[32,1600]{1,0:T(8,128)(2,1)S(1)} collective-permute-done((bf16[32,1600]{1,0:T(8,128)(2,1)S(1)}, bf16[32,1600]{1,0:T(8,128)(2,1)S(1)}, u32[]{:S(2)}, u32[]{:S(2)}) %collective-permute-start.47) | collective-permute-done | bytes 102432 | tf_op jit(solution)/shard_map/ppermute | solution.py:98
  207.9 1.8 collective-permute-start.50
  210.5 8.5 %shard_map.152 = (bf16[960,256]{1,0:T(8,128)(2,1)S(1)}, bf16[960,256]{1,0:T(8,128)(2,1)S(1)}, f32[72,256]{1,0:T(8,128)S(1)}, bf16[256,1600]{1,0:T(8,128)(2,1)S(1)}) custom-call(s32[1]{0:T(128)} %bitcast.refs_0_, s32[960,256]{1,0:T(8,128)S(1)} %bitcast.54, s32[960,1]{1,0:T(8,128)S(1)} %copy-done.8, s32[4,1,240]{2,1,0:T(1,128)S(1)} %reshape.76.refs_9_.refs_3_, ...), custom_call_target="tpu_custom_call" | custom-call | flops 823296000 | bytes 5038080 | tf_op jit(solution)/shard_map/pallas_call | solution.py:39
  219.0 1.7 collective-permute-done.50.refs_2_
  221.3 1.1 shard_map.155.refs_5_
  223.8 2.1 collective-permute-done.44.refs_1_
  227.0 1.2 collective-permute-start.45
  228.2 1.6 copy-done.3
  230.8 4.7 %shard_map.156 = (bf16[960,256]{1,0:T(8,128)(2,1)S(1)}, bf16[960,256]{1,0:T(8,128)(2,1)S(1)}, bf16[256,1600]{1,0:T(8,128)(2,1)S(1)}) custom-call(s32[2]{0:T(128)S(1)} %pad_add_fusion.refs_0_, bf16[4,976,256]{2,1,0:T(8,128)(2,1)S(1)} %bitcast.48, s32[960,1]{1,0:T(8,128)S(1)} %copy-done.9, bf16[960,1600]{1,0:T(8,128)(2,1)S(1)} %bitcast.44, ...), custom_call_target="tpu_custom_call" | custom-call | flops 801177600 | bytes 4546560 | tf_op jit(solution)/shard_map/pallas_call | solution.py:39
  235.6 2.2 collective-permute-start.53
  237.8 4.6 %shard_map.160 = (bf16[960,256]{1,0:T(8,128)(2,1)S(1)}, bf16[960,256]{1,0:T(8,128)(2,1)S(1)}, bf16[256,1600]{1,0:T(8,128)(2,1)S(1)}) custom-call(s32[2]{0:T(128)S(1)} %pad_add_fusion.refs_0_, bf16[4,976,256]{2,1,0:T(8,128)(2,1)S(1)} %bitcast.49, s32[960,1]{1,0:T(8,128)S(1)} %copy-done.10, bf16[960,1600]{1,0:T(8,128)(2,1)S(1)} %bitcast.45, ...), custom_call_target="tpu_custom_call" | custom-call | flops 801177600 | bytes 4546560 | tf_op jit(solution)/shard_map/pallas_call | solution.py:39
  242.4 4.8 %shard_map.158 = (bf16[960,256]{1,0:T(8,128)(2,1)S(1)}, bf16[960,256]{1,0:T(8,128)(2,1)S(1)}, bf16[256,1600]{1,0:T(8,128)(2,1)S(1)}) custom-call(s32[2]{0:T(128)S(1)} %pad_add_fusion.refs_0_, bf16[4,976,256]{2,1,0:T(8,128)(2,1)S(1)} %bitcast.50, s32[960,1]{1,0:T(8,128)S(1)} %copy-done.10, bf16[960,1600]{1,0:T(8,128)(2,1)S(1)} %bitcast.46, ...), custom_call_target="tpu_custom_call" | custom-call | flops 801177600 | bytes 4546560 | tf_op jit(solution)/shard_map/pallas_call | solution.py:39
  247.2 3.2 %collective-permute-start.54 = (f32[72,256]{1,0:T(8,128)S(1)}, f32[72,256]{1,0:T(8,128)S(1)}, u32[]{:S(2)}, u32[]{:S(2)}) collective-permute-start(f32[72,256]{1,0:T(8,128)S(1)} %shard_map.159.refs_2_), channel_id=1, source_target_pairs={{0,8},{8,0},{16,24},{24,16},{1,9},{9,1},{17,25},{25,17},{2,10},{10... | collective-permute-start | bytes 221192 | tf_op jit(solution)/shard_map/ppermute | solution.py:98
  250.4 2.0 collective-permute-start.55
  252.4 1.4 collective-permute-start.56
  253.8 6.3 %shard_map.161.refs_10_ = f32[400,960]{1,0:T(8,128)} custom-call(s32[2]{0:T(128)S(1)} %pad_add_fusion.refs_0_, bf16[256,1600]{1,0:T(8,128)(2,1)S(1)} %copy-done.28, bf16[960,256]{1,0:T(8,128)(2,1)S(1)} %copy-done.19, bf16[960,256]{1,0:T(8,128)(2,1)S(1)} %copy-done.62, bf16[256,1600]{1,0:T(8,128)(2,1)S(1)} %get-tuple-element.55.refs_4_.refs_7_, ...), custom_call_target="tpu_custom_call" | custom-call | flops 2883584000 | bytes 8744960 | tf_op jit(solution)/shard_map/pallas_call | solution.py:39
  260.1 1.4 copy-done.22
  261.5 5.1 %shard_map.162 = (f32[64,1600]{1,0:T(8,128)}, f32[1,256]{1,0:T(1,128)}) custom-call(s32[2]{0:T(128)S(1)} %pad_add_fusion.refs_0_, bf16[64,1600]{1,0:T(8,128)(2,1)S(1)} %bitcast.59, f32[72,256]{1,0:T(8,128)S(1)} %shard_map.159.refs_2_, f32[72,256]{1,0:T(8,128)S(1)} %collective-permute-done.54.refs_3_, f32[72,256]{1,0:T(8,128)S(1)} %collective-permute-done.55.refs_4_, ...), custom_call_target="tpu_custom_call" | custom-call | tf_op jit(solution)/shard_map/pallas_call | solution.py:39
  (248 shorter events, 52.9 us)
Async XLA Ops:
  7.2 112.4 %all-gather.7.cloned.1.call-start = ((), (), s32[]{:S(2)}) async-start(), calls=%async_computation.1 | async-start | bytes 5990400 | tf_op jit(solution)/shard_map/all_gather | solution.py:681
  9.6 164.8 %all-gather.9.cloned.1.call-start = ((), (), s32[]{:S(2)}) async-start(), calls=%async_computation.2 | async-start | bytes 2498560 | tf_op jit(solution)/shard_map/all_gather | solution.py:699
  9.8 1.3 collective-permute-start
  11.1 4.6 %collective-permute-start.1 = (f32[1,256]{1,0:T(1,128)S(1)}, f32[1,256]{1,0:T(1,128)S(1)}, u32[]{:S(2)}, u32[]{:S(2)}) collective-permute-start(f32[1,256]{1,0:T(1,128)S(1)} %add.19), channel_id=1, source_target_pairs={{0,2},{1,3},{2,0},{3,1},{4,6},{5,7},{6,4},{7,5},{8,10},{9,11},{10,... | collective-permute-start | bytes 3080 | tf_op jit(solution)/shard_map/ppermute | solution.py:98
  15.8 3.6 %collective-permute-start.2 = (f32[1,256]{1,0:T(1,128)S(1)}, f32[1,256]{1,0:T(1,128)S(1)}, u32[]{:S(2)}, u32[]{:S(2)}) collective-permute-start(f32[1,256]{1,0:T(1,128)S(1)} %add.20), channel_id=1, source_target_pairs={{0,4},{1,5},{2,6},{3,7},{4,0},{5,1},{6,2},{7,3},{8,12},{9,13},{10,... | collective-permute-start | bytes 3080 | tf_op jit(solution)/shard_map/ppermute | solution.py:98
  29.1 7.6 %collective-permute-start.3 = (f32[128,3200]{1,0:T(8,128)}, f32[128,3200]{1,0:T(8,128)}, u32[]{:S(2)}, u32[]{:S(2)}) collective-permute-start(f32[128,3200]{1,0:T(8,128)} %get-tuple-element.35), channel_id=1, source_target_pairs={{0,1},{1,0},{2,3},{3,2},{4,5},{5,4},{6,7},{7,6},{8,9},{9,8},{10,11... | collective-permute-start | bytes 4915208 | tf_op jit(solution)/shard_map/ppermute | solution.py:98
  35.1 6.6 %collective-permute-start.6 = (f32[128,3200]{1,0:T(8,128)}, f32[128,3200]{1,0:T(8,128)}, u32[]{:S(2)}, u32[]{:S(2)}) collective-permute-start(f32[128,3200]{1,0:T(8,128)} %get-tuple-element.41), channel_id=1, source_target_pairs={{0,1},{1,0},{2,3},{3,2},{4,5},{5,4},{6,7},{7,6},{8,9},{9,8},{10,11... | collective-permute-start | bytes 4915208 | tf_op jit(solution)/shard_map/ppermute | solution.py:98
  36.4 143.2 %all-gather.5.cloned.1.call-start = ((), (), s32[]{:S(2)}) async-start(), calls=%async_computation | async-start | bytes 5990400 | tf_op jit(solution)/shard_map/all_gather | solution.py:718
  39.9 16.7 %collective-permute-start.4 = (bf16[64,3200]{1,0:T(8,128)(2,1)}, bf16[64,3200]{1,0:T(8,128)(2,1)S(1)}, u32[]{:S(2)}, u32[]{:S(2)}) collective-permute-start(bf16[64,3200]{1,0:T(8,128)(2,1)} %get-tuple-element.37), channel_id=1, source_target_pairs={{0,4},{1,3},{2,6},{3,1},{4,0},{5,7},{6,2},{7,5},{8,12},{9,11},{10,... | collective-permute-start | bytes 1228808 | tf_op jit(solution)/shard_map/ppermute | solution.py:98
  46.3 15.3 %collective-permute-start.7 = (bf16[64,3200]{1,0:T(8,128)(2,1)}, bf16[64,3200]{1,0:T(8,128)(2,1)}, u32[]{:S(2)}, u32[]{:S(2)}) collective-permute-start(bf16[64,3200]{1,0:T(8,128)(2,1)} %get-tuple-element.43), channel_id=1, source_target_pairs={{0,4},{1,3},{2,6},{3,1},{4,0},{5,7},{6,2},{7,5},{8,12},{9,11},{10,... | collective-permute-start | bytes 1228808 | tf_op jit(solution)/shard_map/ppermute | solution.py:98
  60.1 5.8 %collective-permute-start.5 = (bf16[32,3200]{1,0:T(8,128)(2,1)S(1)}, bf16[32,3200]{1,0:T(8,128)(2,1)S(1)}, u32[]{:S(2)}, u32[]{:S(2)}) collective-permute-start(bf16[32,3200]{1,0:T(8,128)(2,1)S(1)} %get-tuple-element.39), channel_id=1, source_target_pairs={{0,2},{1,5},{2,0},{3,7},{4,6},{5,1},{6,4},{7,3},{8,10},{9,13},{10,... | collective-permute-start | bytes 614408 | tf_op jit(solution)/shard_map/ppermute | solution.py:98
  62.7 5.8 %collective-permute-start.8 = (bf16[32,3200]{1,0:T(8,128)(2,1)S(1)}, bf16[32,3200]{1,0:T(8,128)(2,1)S(1)}, u32[]{:S(2)}, u32[]{:S(2)}) collective-permute-start(bf16[32,3200]{1,0:T(8,128)(2,1)S(1)} %get-tuple-element.45), channel_id=1, source_target_pairs={{0,2},{1,5},{2,0},{3,7},{4,6},{5,1},{6,4},{7,3},{8,10},{9,13},{10,... | collective-permute-start | bytes 614408 | tf_op jit(solution)/shard_map/ppermute | solution.py:98
  70.9 12.9 %collective-permute-start.9 = (bf16[4,32,1600]{2,1,0:T(8,128)(2,1)}, bf16[4,32,1600]{2,1,0:T(8,128)(2,1)S(1)}, u32[]{:S(2)}, u32[]{:S(2)}) collective-permute-start(bf16[4,32,1600]{2,1,0:T(8,128)(2,1)} %get-tuple-element.46.refs_3_), channel_id=1, source_target_pairs={{0,2},{1,5},{2,0},{3,7},{4,6},{5,1},{6,4},{7,3},{8,10},{9,13},{10,... | collective-permute-start | bytes 1228808 | tf_op jit(solution)/shard_map/ppermute | solution.py:98
  71.9 12.4 %collective-permute-start.10 = (bf16[4,32,1600]{2,1,0:T(8,128)(2,1)}, bf16[4,32,1600]{2,1,0:T(8,128)(2,1)}, u32[]{:S(2)}, u32[]{:S(2)}) collective-permute-start(bf16[4,32,1600]{2,1,0:T(8,128)(2,1)} %get-tuple-element.46.refs_3_), channel_id=1, source_target_pairs={{0,4},{1,3},{2,6},{3,1},{4,0},{5,7},{6,2},{7,5},{8,12},{9,11},{10,... | collective-permute-start | bytes 1228808 | tf_op jit(solution)/shard_map/ppermute | solution.py:98
  83.8 8.2 %collective-permute-start.11 = (bf16[4,32,1600]{2,1,0:T(8,128)(2,1)S(1)}, bf16[4,32,1600]{2,1,0:T(8,128)(2,1)}, u32[]{:S(2)}, u32[]{:S(2)}) collective-permute-start(bf16[4,32,1600]{2,1,0:T(8,128)(2,1)S(1)} %collective-permute-done.9.refs_4_), channel_id=1, source_target_pairs={{0,4},{1,3},{2,6},{3,1},{4,0},{5,7},{6,2},{7,5},{8,12},{9,11},{10,... | collective-permute-start | bytes 1228808 | tf_op jit(solution)/shard_map/ppermute | solution.py:98
  83.8 9.7 %collective-permute-start.12 = (bf16[4,32,1600]{2,1,0:T(8,128)(2,1)}, bf16[4,32,1600]{2,1,0:T(8,128)(2,1)}, u32[]{:S(2)}, u32[]{:S(2)}) collective-permute-start(bf16[4,32,1600]{2,1,0:T(8,128)(2,1)} %get-tuple-element.46.refs_3_), channel_id=1, source_target_pairs={{0,1},{1,0},{2,3},{3,2},{4,5},{5,4},{6,7},{7,6},{8,9},{9,8},{10,11... | collective-permute-start | bytes 1228808 | tf_op jit(solution)/shard_map/ppermute | solution.py:98
  83.8 9.7 %collective-permute-start.13 = (bf16[4,32,1600]{2,1,0:T(8,128)(2,1)S(1)}, bf16[4,32,1600]{2,1,0:T(8,128)(2,1)}, u32[]{:S(2)}, u32[]{:S(2)}) collective-permute-start(bf16[4,32,1600]{2,1,0:T(8,128)(2,1)S(1)} %collective-permute-done.9.refs_4_), channel_id=1, source_target_pairs={{0,1},{1,0},{2,3},{3,2},{4,5},{5,4},{6,7},{7,6},{8,9},{9,8},{10,11... | collective-permute-start | bytes 1228808 | tf_op jit(solution)/shard_map/ppermute | solution.py:98
  84.3 9.2 %collective-permute-start.14 = (bf16[4,32,1600]{2,1,0:T(8,128)(2,1)}, bf16[4,32,1600]{2,1,0:T(8,128)(2,1)}, u32[]{:S(2)}, u32[]{:S(2)}) collective-permute-start(bf16[4,32,1600]{2,1,0:T(8,128)(2,1)} %collective-permute-done.10.refs_5_), channel_id=1, source_target_pairs={{0,1},{1,0},{2,3},{3,2},{4,5},{5,4},{6,7},{7,6},{8,9},{9,8},{10,11... | collective-permute-start | bytes 1228808 | tf_op jit(solution)/shard_map/ppermute | solution.py:98
  92.0 2.1 collective-permute-start.15
  105.0 4.3 %collective-permute-start.16 = (bf16[128,200]{1,0:T(8,128)(2,1)S(1)}, bf16[128,200]{1,0:T(8,128)(2,1)S(1)}, u32[]{:S(2)}, u32[]{:S(2)}) collective-permute-start(bf16[128,200]{1,0:T(8,128)(2,1)S(1)} %get-tuple-element.82), channel_id=1, source_target_pairs={{0,2},{1,5},{2,0},{3,7},{4,6},{5,1},{6,4},{7,3},{8,10},{9,13},{10,... | collective-permute-start | bytes 153608 | tf_op jit(solution)/shard_map/ppermute | solution.py:98
  106.2 5.7 %collective-permute-start.17 = (bf16[128,200]{1,0:T(8,128)(2,1)S(1)}, bf16[128,200]{1,0:T(8,128)(2,1)S(1)}, u32[]{:S(2)}, u32[]{:S(2)}) collective-permute-start(bf16[128,200]{1,0:T(8,128)(2,1)S(1)} %get-tuple-element.81), channel_id=1, source_target_pairs={{0,4},{1,3},{2,6},{3,1},{4,0},{5,7},{6,2},{7,5},{8,12},{9,11},{10,... | collective-permute-start | bytes 153608 | tf_op jit(solution)/shard_map/ppermute | solution.py:98
  106.2 6.7 %collective-permute-start.18 = (bf16[128,200]{1,0:T(8,128)(2,1)S(1)}, bf16[128,200]{1,0:T(8,128)(2,1)S(1)}, u32[]{:S(2)}, u32[]{:S(2)}) collective-permute-start(bf16[128,200]{1,0:T(8,128)(2,1)S(1)} %get-tuple-element.80), channel_id=1, source_target_pairs={{0,6},{1,7},{2,4},{3,5},{4,2},{5,3},{6,0},{7,1},{8,14},{9,15},{10,... | collective-permute-start | bytes 153608 | tf_op jit(solution)/shard_map/ppermute | solution.py:98
  108.6 4.9 %collective-permute-start.19 = (bf16[128,200]{1,0:T(8,128)(2,1)S(1)}, bf16[128,200]{1,0:T(8,128)(2,1)S(1)}, u32[]{:S(2)}, u32[]{:S(2)}) collective-permute-start(bf16[128,200]{1,0:T(8,128)(2,1)S(1)} %get-tuple-element.79), channel_id=1, source_target_pairs={{0,1},{1,0},{2,3},{3,2},{4,5},{5,4},{6,7},{7,6},{8,9},{9,8},{10,11... | collective-permute-start | bytes 153608 | tf_op jit(solution)/shard_map/ppermute | solution.py:98
  108.6 5.5 %collective-permute-start.20 = (bf16[128,200]{1,0:T(8,128)(2,1)S(1)}, bf16[128,200]{1,0:T(8,128)(2,1)S(1)}, u32[]{:S(2)}, u32[]{:S(2)}) collective-permute-start(bf16[128,200]{1,0:T(8,128)(2,1)S(1)} %get-tuple-element.78), channel_id=1, source_target_pairs={{0,5},{1,2},{2,7},{3,0},{4,1},{5,6},{6,3},{7,4},{8,13},{9,10},{10,... | collective-permute-start | bytes 153608 | tf_op jit(solution)/shard_map/ppermute | solution.py:98
  110.0 4.8 %collective-permute-start.21 = (bf16[128,200]{1,0:T(8,128)(2,1)S(1)}, bf16[128,200]{1,0:T(8,128)(2,1)S(1)}, u32[]{:S(2)}, u32[]{:S(2)}) collective-permute-start(bf16[128,200]{1,0:T(8,128)(2,1)S(1)} %get-tuple-element.77), channel_id=1, source_target_pairs={{0,3},{1,4},{2,1},{3,6},{4,7},{5,0},{6,5},{7,2},{8,11},{9,12},{10,... | collective-permute-start | bytes 153608 | tf_op jit(solution)/shard_map/ppermute | solution.py:98
  112.4 6.6 %collective-permute-start.22 = (bf16[128,200]{1,0:T(8,128)(2,1)S(1)}, bf16[128,200]{1,0:T(8,128)(2,1)S(1)}, u32[]{:S(2)}, u32[]{:S(2)}) collective-permute-start(bf16[128,200]{1,0:T(8,128)(2,1)S(1)} %get-tuple-element.76), channel_id=1, source_target_pairs={{0,7},{1,6},{2,5},{3,4},{4,3},{5,2},{6,1},{7,0},{8,15},{9,14},{10,... | collective-permute-start | bytes 153608 | tf_op jit(solution)/shard_map/ppermute | solution.py:98
  129.3 37.6 %copy-start.29 = (f32[4,32,1600]{2,1,0:T(8,128)}, f32[4,32,1600]{2,1,0:T(8,128)S(1)}, u32[]{:S(2)}) copy-start(f32[4,32,1600]{2,1,0:T(8,128)S(1)} %get-tuple-element.48.refs_2_) | copy-start | bytes 2457604
  129.3 21.2 %collective-permute-start.23 = (bf16[4,32,1600]{2,1,0:T(8,128)(2,1)S(1)}, bf16[4,32,1600]{2,1,0:T(8,128)(2,1)S(1)}, u32[]{:S(2)}, u32[]{:S(2)}) collective-permute-start(bf16[4,32,1600]{2,1,0:T(8,128)(2,1)S(1)} %get-tuple-element.49.refs_3_), channel_id=1, source_target_pairs={{0,2},{1,5},{2,0},{3,7},{4,6},{5,1},{6,4},{7,3},{8,10},{9,13},{10,... | collective-permute-start | bytes 1228808 | tf_op jit(solution)/shard_map/ppermute | solution.py:98
  130.2 21.1 %collective-permute-start.24 = (bf16[4,32,1600]{2,1,0:T(8,128)(2,1)S(1)}, bf16[4,32,1600]{2,1,0:T(8,128)(2,1)S(1)}, u32[]{:S(2)}, u32[]{:S(2)}) collective-permute-start(bf16[4,32,1600]{2,1,0:T(8,128)(2,1)S(1)} %get-tuple-element.49.refs_3_), channel_id=1, source_target_pairs={{0,4},{1,3},{2,6},{3,1},{4,0},{5,7},{6,2},{7,5},{8,12},{9,11},{10,... | collective-permute-start | bytes 1228808 | tf_op jit(solution)/shard_map/ppermute | solution.py:98
  150.5 9.3 %collective-permute-start.25 = (bf16[4,32,1600]{2,1,0:T(8,128)(2,1)S(1)}, bf16[4,32,1600]{2,1,0:T(8,128)(2,1)S(1)}, u32[]{:S(2)}, u32[]{:S(2)}) collective-permute-start(bf16[4,32,1600]{2,1,0:T(8,128)(2,1)S(1)} %collective-permute-done.23.refs_4_), channel_id=1, source_target_pairs={{0,4},{1,3},{2,6},{3,1},{4,0},{5,7},{6,2},{7,5},{8,12},{9,11},{10,... | collective-permute-start | bytes 1228808 | tf_op jit(solution)/shard_map/ppermute | solution.py:98
  150.5 9.4 %collective-permute-start.26 = (bf16[4,32,1600]{2,1,0:T(8,128)(2,1)S(1)}, bf16[4,32,1600]{2,1,0:T(8,128)(2,1)S(1)}, u32[]{:S(2)}, u32[]{:S(2)}) collective-permute-start(bf16[4,32,1600]{2,1,0:T(8,128)(2,1)S(1)} %get-tuple-element.49.refs_3_), channel_id=1, source_target_pairs={{0,1},{1,0},{2,3},{3,2},{4,5},{5,4},{6,7},{7,6},{8,9},{9,8},{10,11... | collective-permute-start | bytes 1228808 | tf_op jit(solution)/shard_map/ppermute | solution.py:98
  150.5 9.4 %collective-permute-start.27 = (bf16[4,32,1600]{2,1,0:T(8,128)(2,1)S(1)}, bf16[4,32,1600]{2,1,0:T(8,128)(2,1)S(1)}, u32[]{:S(2)}, u32[]{:S(2)}) collective-permute-start(bf16[4,32,1600]{2,1,0:T(8,128)(2,1)S(1)} %collective-permute-done.23.refs_4_), channel_id=1, source_target_pairs={{0,1},{1,0},{2,3},{3,2},{4,5},{5,4},{6,7},{7,6},{8,9},{9,8},{10,11... | collective-permute-start | bytes 1228808 | tf_op jit(solution)/shard_map/ppermute | solution.py:98
  151.3 8.6 %collective-permute-start.28 = (bf16[4,32,1600]{2,1,0:T(8,128)(2,1)S(1)}, bf16[4,32,1600]{2,1,0:T(8,128)(2,1)S(1)}, u32[]{:S(2)}, u32[]{:S(2)}) collective-permute-start(bf16[4,32,1600]{2,1,0:T(8,128)(2,1)S(1)} %collective-permute-done.24.refs_5_), channel_id=1, source_target_pairs={{0,1},{1,0},{2,3},{3,2},{4,5},{5,4},{6,7},{7,6},{8,9},{9,8},{10,11... | collective-permute-start | bytes 1228808 | tf_op jit(solution)/shard_map/ppermute | solution.py:98
  159.8 1.8 collective-permute-start.29
  167.8 4.3 %collective-permute-start.30 = (bf16[128,200]{1,0:T(8,128)(2,1)S(1)}, bf16[128,200]{1,0:T(8,128)(2,1)S(1)}, u32[]{:S(2)}, u32[]{:S(2)}) collective-permute-start(bf16[128,200]{1,0:T(8,128)(2,1)S(1)} %get-tuple-element.75), channel_id=1, source_target_pairs={{0,2},{1,5},{2,0},{3,7},{4,6},{5,1},{6,4},{7,3},{8,10},{9,13},{10,... | collective-permute-start | bytes 153608 | tf_op jit(solution)/shard_map/ppermute | solution.py:98
  168.9 5.5 %collective-permute-start.31 = (bf16[128,200]{1,0:T(8,128)(2,1)S(1)}, bf16[128,200]{1,0:T(8,128)(2,1)S(1)}, u32[]{:S(2)}, u32[]{:S(2)}) collective-permute-start(bf16[128,200]{1,0:T(8,128)(2,1)S(1)} %get-tuple-element.74), channel_id=1, source_target_pairs={{0,4},{1,3},{2,6},{3,1},{4,0},{5,7},{6,2},{7,5},{8,12},{9,11},{10,... | collective-permute-start | bytes 153608 | tf_op jit(solution)/shard_map/ppermute | solution.py:98
  169.2 5.6 %collective-permute-start.32 = (bf16[128,200]{1,0:T(8,128)(2,1)S(1)}, bf16[128,200]{1,0:T(8,128)(2,1)S(1)}, u32[]{:S(2)}, u32[]{:S(2)}) collective-permute-start(bf16[128,200]{1,0:T(8,128)(2,1)S(1)} %get-tuple-element.73), channel_id=1, source_target_pairs={{0,6},{1,7},{2,4},{3,5},{4,2},{5,3},{6,0},{7,1},{8,14},{9,15},{10,... | collective-permute-start | bytes 153608 | tf_op jit(solution)/shard_map/ppermute | solution.py:98
  171.3 4.1 %collective-permute-start.33 = (bf16[128,200]{1,0:T(8,128)(2,1)S(1)}, bf16[128,200]{1,0:T(8,128)(2,1)S(1)}, u32[]{:S(2)}, u32[]{:S(2)}) collective-permute-start(bf16[128,200]{1,0:T(8,128)(2,1)S(1)} %get-tuple-element.72), channel_id=1, source_target_pairs={{0,1},{1,0},{2,3},{3,2},{4,5},{5,4},{6,7},{7,6},{8,9},{9,8},{10,11... | collective-permute-start | bytes 153608 | tf_op jit(solution)/shard_map/ppermute | solution.py:98
  171.3 4.7 %collective-permute-start.34 = (bf16[128,200]{1,0:T(8,128)(2,1)S(1)}, bf16[128,200]{1,0:T(8,128)(2,1)S(1)}, u32[]{:S(2)}, u32[]{:S(2)}) collective-permute-start(bf16[128,200]{1,0:T(8,128)(2,1)S(1)} %get-tuple-element.71), channel_id=1, source_target_pairs={{0,5},{1,2},{2,7},{3,0},{4,1},{5,6},{6,3},{7,4},{8,13},{9,10},{10,... | collective-permute-start | bytes 153608 | tf_op jit(solution)/shard_map/ppermute | solution.py:98
  172.1 4.5 %collective-permute-start.35 = (bf16[128,200]{1,0:T(8,128)(2,1)S(1)}, bf16[128,200]{1,0:T(8,128)(2,1)S(1)}, u32[]{:S(2)}, u32[]{:S(2)}) collective-permute-start(bf16[128,200]{1,0:T(8,128)(2,1)S(1)} %get-tuple-element.70), channel_id=1, source_target_pairs={{0,3},{1,4},{2,1},{3,6},{4,7},{5,0},{6,5},{7,2},{8,11},{9,12},{10,... | collective-permute-start | bytes 153608 | tf_op jit(solution)/shard_map/ppermute | solution.py:98
  174.4 4.7 %collective-permute-start.36 = (bf16[128,200]{1,0:T(8,128)(2,1)S(1)}, bf16[128,200]{1,0:T(8,128)(2,1)S(1)}, u32[]{:S(2)}, u32[]{:S(2)}) collective-permute-start(bf16[128,200]{1,0:T(8,128)(2,1)S(1)} %get-tuple-element.69), channel_id=1, source_target_pairs={{0,7},{1,6},{2,5},{3,4},{4,3},{5,2},{6,1},{7,0},{8,15},{9,14},{10,... | collective-permute-start | bytes 153608 | tf_op jit(solution)/shard_map/ppermute | solution.py:98
  190.1 20.3 %copy-start = (bf16[1600,960]{0,1:T(8,128)(2,1)S(1)}, bf16[1600,960]{0,1:T(8,128)(2,1)}, u32[]{:S(2)}) copy-start(bf16[1600,960]{0,1:T(8,128)(2,1)} %param.20) | copy-start | bytes 9216004
  190.1 20.3 %copy-start.8 = (s32[960,1]{1,0:T(8,128)S(1)}, s32[960,1]{1,0:T(8,128)}, u32[]{:S(2)}) copy-start(s32[960,1]{1,0:T(8,128)} %copy-done.7) | copy-start | bytes 11524
  190.1 20.3 %copy-start.15 = (bf16[1600,64]{0,1:T(8,128)(2,1)S(1)}, bf16[1600,64]{0,1:T(8,128)(2,1)}, u32[]{:S(2)}) copy-start(bf16[1600,64]{0,1:T(8,128)(2,1)} %param.21) | copy-start | bytes 614404
  191.4 5.1 %collective-permute-start.37 = (bf16[32,1600]{1,0:T(8,128)(2,1)S(1)}, bf16[32,1600]{1,0:T(8,128)(2,1)S(1)}, u32[]{:S(2)}, u32[]{:S(2)}) collective-permute-start(bf16[32,1600]{1,0:T(8,128)(2,1)S(1)} %shard_map.151.refs_7_.refs_3_), channel_id=1, source_target_pairs={{0,2},{1,5},{2,0},{3,7},{4,6},{5,1},{6,4},{7,3},{8,10},{9,13},{10,... | collective-permute-start | bytes 307208 | tf_op jit(solution)/shard_map/ppermute | solution.py:98
  192.5 6.9 %collective-permute-start.38 = (bf16[32,1600]{1,0:T(8,128)(2,1)S(1)}, bf16[32,1600]{1,0:T(8,128)(2,1)S(1)}, u32[]{:S(2)}, u32[]{:S(2)}) collective-permute-start(bf16[32,1600]{1,0:T(8,128)(2,1)S(1)} %shard_map.151.refs_7_.refs_3_), channel_id=1, source_target_pairs={{0,4},{1,3},{2,6},{3,1},{4,0},{5,7},{6,2},{7,5},{8,12},{9,11},{10,... | collective-permute-start | bytes 307208 | tf_op jit(solution)/shard_map/ppermute | solution.py:98
  192.5 8.3 %collective-permute-start.40 = (bf16[32,1600]{1,0:T(8,128)(2,1)S(1)}, bf16[32,1600]{1,0:T(8,128)(2,1)S(1)}, u32[]{:S(2)}, u32[]{:S(2)}) collective-permute-start(bf16[32,1600]{1,0:T(8,128)(2,1)S(1)} %shard_map.151.refs_7_.refs_3_), channel_id=1, source_target_pairs={{0,1},{1,0},{2,3},{3,2},{4,5},{5,4},{6,7},{7,6},{8,9},{9,8},{10,11... | collective-permute-start | bytes 307208 | tf_op jit(solution)/shard_map/ppermute | solution.py:98
  192.5 8.3 %collective-permute-start.46 = (bf16[32,1600]{1,0:T(8,128)(2,1)S(1)}, bf16[32,1600]{1,0:T(8,128)(2,1)S(1)}, u32[]{:S(2)}, u32[]{:S(2)}) collective-permute-start(bf16[32,1600]{1,0:T(8,128)(2,1)S(1)} %shard_map.151.refs_7_.refs_3_), channel_id=1, source_target_pairs={{0,8},{8,0},{16,24},{24,16},{1,9},{9,1},{17,25},{25,17},{2,10},{10... | collective-permute-start | bytes 307208 | tf_op jit(solution)/shard_map/ppermute | solution.py:98
  196.6 4.8 %collective-permute-start.39 = (bf16[32,1600]{1,0:T(8,128)(2,1)S(1)}, bf16[32,1600]{1,0:T(8,128)(2,1)S(1)}, u32[]{:S(2)}, u32[]{:S(2)}) collective-permute-start(bf16[32,1600]{1,0:T(8,128)(2,1)S(1)} %collective-permute-done.37.refs_8_.refs_4_), channel_id=1, source_target_pairs={{0,4},{1,3},{2,6},{3,1},{4,0},{5,7},{6,2},{7,5},{8,12},{9,11},{10,... | collective-permute-start | bytes 307208 | tf_op jit(solution)/shard_map/ppermute | solution.py:98
  196.9 9.9 %collective-permute-start.47 = (bf16[32,1600]{1,0:T(8,128)(2,1)S(1)}, bf16[32,1600]{1,0:T(8,128)(2,1)S(1)}, u32[]{:S(2)}, u32[]{:S(2)}) collective-permute-start(bf16[32,1600]{1,0:T(8,128)(2,1)S(1)} %shard_map.151.refs_7_.refs_3_), channel_id=1, source_target_pairs={{0,16},{8,24},{16,0},{24,8},{1,17},{9,25},{17,1},{25,9},{2,18},{10... | collective-permute-start | bytes 307208 | tf_op jit(solution)/shard_map/ppermute | solution.py:98
  199.4 7.4 %collective-permute-start.48 = (bf16[32,1600]{1,0:T(8,128)(2,1)S(1)}, bf16[32,1600]{1,0:T(8,128)(2,1)S(1)}, u32[]{:S(2)}, u32[]{:S(2)}) collective-permute-start(bf16[32,1600]{1,0:T(8,128)(2,1)S(1)} %shard_map.151.refs_7_.refs_3_), channel_id=1, source_target_pairs={{0,24},{8,16},{16,8},{24,0},{1,25},{9,17},{17,9},{25,1},{2,26},{10... | collective-permute-start | bytes 307208 | tf_op jit(solution)/shard_map/ppermute | solution.py:98
  200.9 6.0 %collective-permute-start.41 = (bf16[32,1600]{1,0:T(8,128)(2,1)S(1)}, bf16[32,1600]{1,0:T(8,128)(2,1)S(1)}, u32[]{:S(2)}, u32[]{:S(2)}) collective-permute-start(bf16[32,1600]{1,0:T(8,128)(2,1)S(1)} %collective-permute-done.37.refs_8_.refs_4_), channel_id=1, source_target_pairs={{0,1},{1,0},{2,3},{3,2},{4,5},{5,4},{6,7},{7,6},{8,9},{9,8},{10,11... | collective-permute-start | bytes 307208 | tf_op jit(solution)/shard_map/ppermute | solution.py:98
  200.9 6.0 %collective-permute-start.42 = (bf16[32,1600]{1,0:T(8,128)(2,1)S(1)}, bf16[32,1600]{1,0:T(8,128)(2,1)S(1)}, u32[]{:S(2)}, u32[]{:S(2)}) collective-permute-start(bf16[32,1600]{1,0:T(8,128)(2,1)S(1)} %collective-permute-done.38.refs_9_.refs_5_), channel_id=1, source_target_pairs={{0,1},{1,0},{2,3},{3,2},{4,5},{5,4},{6,7},{7,6},{8,9},{9,8},{10,11... | collective-permute-start | bytes 307208 | tf_op jit(solution)/shard_map/ppermute | solution.py:98
  201.4 5.5 %collective-permute-start.43 = (bf16[32,1600]{1,0:T(8,128)(2,1)S(1)}, bf16[32,1600]{1,0:T(8,128)(2,1)S(1)}, u32[]{:S(2)}, u32[]{:S(2)}) collective-permute-start(bf16[32,1600]{1,0:T(8,128)(2,1)S(1)} %collective-permute-done.39.refs_10_.refs_6_), channel_id=1, source_target_pairs={{0,1},{1,0},{2,3},{3,2},{4,5},{5,4},{6,7},{7,6},{8,9},{9,8},{10,11... | collective-permute-start | bytes 307208 | tf_op jit(solution)/shard_map/ppermute | solution.py:98
  206.9 12.1 %collective-permute-start.49 = (bf16[3,32,1600]{2,1,0:T(8,128)(2,1)S(1)}, bf16[3,32,1600]{2,1,0:T(8,128)(2,1)S(1)}, u32[]{:S(2)}, u32[]{:S(2)}) collective-permute-start(bf16[3,32,1600]{2,1,0:T(8,128)(2,1)S(1)} %shard_map.154.refs_0_), channel_id=1, source_target_pairs={{0,2},{1,5},{2,0},{3,7},{4,6},{5,1},{6,4},{7,3},{8,10},{9,13},{10,... | collective-permute-start | bytes 921608 | tf_op jit(solution)/shard_map/ppermute | solution.py:98
  207.9 12.8 %collective-permute-start.50 = (bf16[3,32,1600]{2,1,0:T(8,128)(2,1)S(1)}, bf16[3,32,1600]{2,1,0:T(8,128)(2,1)S(1)}, u32[]{:S(2)}, u32[]{:S(2)}) collective-permute-start(bf16[3,32,1600]{2,1,0:T(8,128)(2,1)S(1)} %shard_map.154.refs_0_), channel_id=1, source_target_pairs={{0,4},{1,3},{2,6},{3,1},{4,0},{5,7},{6,2},{7,5},{8,12},{9,11},{10,... | collective-permute-start | bytes 921608 | tf_op jit(solution)/shard_map/ppermute | solution.py:98
  209.6 11.7 %collective-permute-start.51 = (bf16[3,32,1600]{2,1,0:T(8,128)(2,1)S(1)}, bf16[3,32,1600]{2,1,0:T(8,128)(2,1)S(1)}, u32[]{:S(2)}, u32[]{:S(2)}) collective-permute-start(bf16[3,32,1600]{2,1,0:T(8,128)(2,1)S(1)} %shard_map.154.refs_0_), channel_id=1, source_target_pairs={{0,6},{1,7},{2,4},{3,5},{4,2},{5,3},{6,0},{7,1},{8,14},{9,15},{10,... | collective-permute-start | bytes 921608 | tf_op jit(solution)/shard_map/ppermute | solution.py:98
  223.3 4.9 %collective-permute-start.52 = (bf16[4,3,32,1600]{3,2,1,0:T(8,128)(2,1)}, bf16[4,3,32,1600]{3,2,1,0:T(8,128)(2,1)}, u32[]{:S(2)}, u32[]{:S(2)}) collective-permute-start(bf16[4,3,32,1600]{3,2,1,0:T(8,128)(2,1)} %shard_map.155.refs_5_), channel_id=1, source_target_pairs={{0,1},{1,0},{2,3},{3,2},{4,5},{5,4},{6,7},{7,6},{8,9},{9,8},{10,11... | collective-permute-start | bytes 3686408 | tf_op jit(solution)/shard_map/ppermute | solution.py:98
  223.3 2.7 collective-permute-start.44
  227.0 8.5 %collective-permute-start.45 = (f32[72,256]{1,0:T(8,128)S(1)}, f32[72,256]{1,0:T(8,128)S(1)}, u32[]{:S(2)}, u32[]{:S(2)}) collective-permute-start(f32[72,256]{1,0:T(8,128)S(1)} %shard_map.153.refs_0_), channel_id=1, source_target_pairs={{0,2},{1,3},{2,0},{3,1},{4,6},{5,7},{6,4},{7,5},{8,10},{9,11},{10,... | collective-permute-start | bytes 221192 | tf_op jit(solution)/shard_map/ppermute | solution.py:98
  235.6 11.6 %collective-permute-start.53 = (f32[72,256]{1,0:T(8,128)S(1)}, f32[72,256]{1,0:T(8,128)S(1)}, u32[]{:S(2)}, u32[]{:S(2)}) collective-permute-start(f32[72,256]{1,0:T(8,128)S(1)} %shard_map.157.refs_0_), channel_id=1, source_target_pairs={{0,4},{1,5},{2,6},{3,7},{4,0},{5,1},{6,2},{7,3},{8,12},{9,13},{10,... | collective-permute-start | bytes 221192 | tf_op jit(solution)/shard_map/ppermute | solution.py:98
  247.2 12.9 %collective-permute-start.54 = (f32[72,256]{1,0:T(8,128)S(1)}, f32[72,256]{1,0:T(8,128)S(1)}, u32[]{:S(2)}, u32[]{:S(2)}) collective-permute-start(f32[72,256]{1,0:T(8,128)S(1)} %shard_map.159.refs_2_), channel_id=1, source_target_pairs={{0,8},{8,0},{16,24},{24,16},{1,9},{9,1},{17,25},{25,17},{2,10},{10... | collective-permute-start | bytes 221192 | tf_op jit(solution)/shard_map/ppermute | solution.py:98
  250.4 9.7 %collective-permute-start.55 = (f32[72,256]{1,0:T(8,128)S(1)}, f32[72,256]{1,0:T(8,128)S(1)}, u32[]{:S(2)}, u32[]{:S(2)}) collective-permute-start(f32[72,256]{1,0:T(8,128)S(1)} %shard_map.159.refs_2_), channel_id=1, source_target_pairs={{0,16},{8,24},{16,0},{24,8},{1,17},{9,25},{17,1},{25,9},{2,18},{10... | collective-permute-start | bytes 221192 | tf_op jit(solution)/shard_map/ppermute | solution.py:98
  252.4 7.7 %collective-permute-start.56 = (f32[72,256]{1,0:T(8,128)S(1)}, f32[72,256]{1,0:T(8,128)S(1)}, u32[]{:S(2)}, u32[]{:S(2)}) collective-permute-start(f32[72,256]{1,0:T(8,128)S(1)} %shard_map.159.refs_2_), channel_id=1, source_target_pairs={{0,24},{8,16},{16,8},{24,0},{1,25},{9,17},{17,9},{25,1},{2,26},{10... | collective-permute-start | bytes 221192 | tf_op jit(solution)/shard_map/ppermute | solution.py:98
  (65 other events, 197.4 us)
Sparse Core Ops, SparseCore 0:
  9.9 48.8 all-gather.6
  60.4 43.8 all-gather.8
  106.2 52.1 all-gather.4

commit v3 on v2

--- a/solution.py
+++ b/solution.py
@@ -23,7 +23,11 @@
 LARGE = pltpu.CompilerParams(vmem_limit_bytes=20 * 1024 * 1024)
 WHOLE = pl.BlockSpec(memory_space=pltpu.VMEM)
 SCALAR = pl.BlockSpec(memory_space=pltpu.SMEM)
-UNREAD = pl.BlockSpec(memory_space=pl.ANY)
+ANYWHERE = pl.BlockSpec(memory_space=pl.ANY)
+
+
+def in_hbm(array):
+    return pltpu.with_memory_space_constraint(array, pltpu.HBM)
 
 
 def shape_of(shape, dtype):
@@ -38,7 +42,7 @@
 
     return pl.pallas_call(
         body,
-        in_specs=list(in_specs) + [UNREAD] * len(after),
+        in_specs=list(in_specs) + [ANYWHERE] * len(after),
         compiler_params=params,
         **options,
     )(*args, *after)
@@ -70,12 +74,6 @@
 
 def softplus(value):
     return jnp.maximum(value, 0.0) + jnp.log1p(jnp.exp(-jnp.abs(value)))
-
-
-def softplus_pair(value):
-    small = jnp.exp(-jnp.abs(value))
-    soft = jnp.maximum(value, 0.0) + jnp.log1p(small)
-    return soft, jnp.where(value >= 0.0, 1.0, small) / (1.0 + small)
 
 
 def sigmoid(value):
@@ -154,7 +152,7 @@
     out = shape_of((half, columns), F32)
     return launch(
         functools.partial(project_kernel, keys),
-        (me, counts_t, scale, w_proj),
+        (me, counts_t, scale, in_hbm(w_proj)),
         [
             SCALAR,
             fixed(genes, cells),
@@ -178,21 +176,22 @@
     half = stay_ref.shape[0]
     total = keep_ref[...] + got_ref[...].astype(F32)
     stay_ref[...] = total[:half]
-    go_ref[...] = total[half:].astype(BF16)
-
-
-def halve(keep, got, after=()):
-    rows, columns = keep.shape
-    out = (rows // 2, columns)
+    go_ref[...] = total[half:].astype(go_ref.dtype)
+
+
+def halve(keep, got, after=(), dtype=BF16):
+    rows, *columns = keep.shape
+    out = (rows // 2, *columns)
+    size = keep.size
     return launch(
         halve_kernel,
         (keep, got),
         [WHOLE] * 2,
         after,
-        out_shape=(shape_of(out, F32), shape_of(out, BF16)),
+        out_shape=(shape_of(out, F32), shape_of(out, dtype)),
         out_specs=[WHOLE] * 2,
         cost_estimate=pl.CostEstimate(
-            flops=rows * columns, bytes_accessed=rows * columns * 11, transcendentals=0
+            flops=size, bytes_accessed=size * 11, transcendentals=0
         ),
     )
 
@@ -224,11 +223,18 @@
     )
 
 
-def attend_kernel(pieces, heads, head_width, w_ref, row_ref, col_ref, *refs):
-    blocks = refs[:-5]
-    out_ref, x_ref, query_ref, keys_ref, values_ref = refs[-5:]
-    modules, share, _ = blocks[0].shape
+def attend_kernel(pieces, heads, head_width, outs, w_ref, row_ref, col_ref, *refs):
+    blocks = refs[: -4 - outs]
+    out_refs, refs = refs[-4 - outs : -4], refs[-4:]
+    x_ref, query_ref, keys_ref, values_ref = refs
+    if outs == 2:
+        blocks, blocks_out = blocks[:-1], blocks[-1]
     used = heads * head_width
+    _, share, _ = blocks[0].shape
+    rows = len(pieces[0]) * share
+    places = [spot for piece in pieces for spot in piece]
+    for at, (block, module) in enumerate(places):
+        x_ref[at * share : (at + 1) * share, :] = blocks[block][module]
     lane = lax.broadcasted_iota(jnp.int32, (1, used), 1)
     picks = [(lax.rem(lane, heads) == h).astype(F32).astype(BF16) for h in range(heads)]
     down = lax.rem(lax.broadcasted_iota(jnp.int32, (used, used), 0), heads)
@@ -240,12 +246,6 @@
         mean = (dot_nn(high, same_head) + dot_nn(low, same_head)) * (1.0 / head_width)
         return (values * lax.rsqrt(jnp.maximum(mean, FLOOR))).astype(BF16)
 
-    rows = len(pieces[0]) * share
-    for at, piece in enumerate(pieces):
-        for place, (block, module) in enumerate(piece):
-            x_ref[at * rows + place * share : at * rows + (place + 1) * share, :] = blocks[block][
-                module
-            ]
     every = x_ref.shape[0]
     step = min(every, 256)
     for at in range(0, every, step):
@@ -256,6 +256,7 @@
         values_ref[part, :] = qkv[:, 2 * used :].astype(BF16)
     same = row_ref[...] == col_ref[...]
     scale = head_width ** (-0.5) * LOG2_E
+    summed = None
     for at, piece in enumerate(pieces):
         part = slice(at * rows, (at + 1) * rows)
         query, keys, values = query_ref[part, :], keys_ref[part, :], values_ref[part, :]
@@ -265,24 +266,40 @@
             probs = weights * (1.0 / jnp.sum(weights, axis=-1, keepdims=True))
             mixed = mixed + dot_nn(probs.astype(BF16), values * pick)
         mixed = mixed.astype(BF16)
-        for place, (block, module) in enumerate(piece):
-            out_ref[block, module * share : (module + 1) * share, :] = mixed[
-                place * share : (place + 1) * share
-            ]
-
-
-def attend(blocks, w_flat, ids, pieces, heads, head_width):
+        if outs == 1:
+            for place, (block, module) in enumerate(piece):
+                out_refs[0][block, module * share : (module + 1) * share, :] = mixed[
+                    place * share : (place + 1) * share
+                ]
+        else:
+            mixed = mixed.astype(F32)
+            summed = mixed if summed is None else summed + mixed
+    if outs == 2:
+        w_out = blocks_out[...]
+        high, middle, low = split3(summed * (1.0 / len(pieces)))
+        total = dot_nn(high, w_out) + dot_nn(middle, w_out) + dot_nn(low, w_out)
+        for at in range(rows // share):
+            half = rows // share // 2
+            out_refs[at // half][at % half] = total[at * share : (at + 1) * share]
+
+
+def attend(blocks, w_flat, ids, pieces, heads, head_width, w_out=None, after=()):
     count = len(blocks)
     modules, share, width = blocks[0].shape
     rows = len(pieces[0]) * share
     every = len(pieces) * rows
     used = heads * head_width
-    return launch(
-        functools.partial(attend_kernel, pieces, heads, head_width),
-        (w_flat, *ids, *blocks),
-        [WHOLE] * (3 + len(blocks)),
-        out_shape=shape_of((count, modules * share, used), BF16),
-        out_specs=WHOLE,
+    if w_out is None:
+        last, out_shape = [], [shape_of((count, modules * share, used), BF16)]
+    else:
+        last, out_shape = [w_out], [shape_of((count // 2, share, width), F32)] * 2
+    return launch(
+        functools.partial(attend_kernel, pieces, heads, head_width, len(out_shape)),
+        (w_flat, *ids, *blocks, *last),
+        [WHOLE] * (3 + len(blocks) + len(last)),
+        after,
+        out_shape=out_shape,
+        out_specs=[WHOLE] * len(out_shape),
         scratch_shapes=[pltpu.VMEM((every, width), BF16)] + [pltpu.VMEM((every, used), BF16)] * 3,
         cost_estimate=pl.CostEstimate(
             flops=2 * every * (width * 3 * used + 2 * heads * rows * used),
@@ -292,44 +309,80 @@
     )
 
 
-def add_mixed(places, keys, me_ref, w_ref, resid_ref, mixed_refs):
+def add_mixed(places, keys, me_ref, w_hbm, resid_hbm, mixed_hbm, scratch):
+    mixed_ref, w_ref, resid_ref, sems = scratch
     modules, share, _ = resid_ref.shape
+    count = len(keys)
+    copies = []
+    for at, (place, key) in enumerate(zip(places, keys)):
+        source = mixed_hbm[0].at[0] if place == 0 else mixed_hbm[place]
+        pair = [
+            pltpu.make_async_copy(source, mixed_ref.at[at], sems.at[2 * at]),
+            pltpu.make_async_copy(
+                w_hbm.at[holder(me_ref[0], key)], w_ref.at[at], sems.at[2 * at + 1]
+            ),
+        ]
+        for copy in pair:
+            copy.start()
+        copies.append(pair)
+    resid_copy = pltpu.make_async_copy(resid_hbm, resid_ref, sems.at[2 * count])
+    resid_copy.start()
     total = None
-    for place, key in zip(places, keys):
-        mixed = mixed_refs[0][0] if place == 0 else mixed_refs[place][...]
-        term = dot_nn(mixed, w_ref[holder(me_ref[0], key)])
+    for at, pair in enumerate(copies):
+        for copy in pair:
+            copy.wait()
+        term = dot_nn(mixed_ref[at], w_ref[at])
         total = term if total is None else total + term
+    resid_copy.wait()
     return [resid_ref[m] + total[m * share : (m + 1) * share] for m in range(modules)]
 
 
-def out_kernel(places, keys, me_ref, w_ref, resid_ref, *refs):
-    mid_ref, normed_ref = refs[-2:]
-    for m, rows in enumerate(add_mixed(places, keys, me_ref, w_ref, resid_ref, refs[:-2])):
+def out_kernel(places, keys, me_ref, w_hbm, resid_hbm, *refs):
+    mixed, (mid_ref, normed_ref), scratch = refs[:-6], refs[-6:-4], refs[-4:]
+    modules = add_mixed(places, keys, me_ref, w_hbm, resid_hbm, mixed, scratch)
+    for m, rows in enumerate(modules):
         mid_ref[m] = rows
         normed_ref[m] = rms_rows(rows).astype(BF16)
 
 
-def pool_kernel(places, keys, me_ref, w_ref, resid_ref, *refs):
-    modules = add_mixed(places, keys, me_ref, w_ref, resid_ref, refs[:-1])
-    pooled = functools.reduce(jnp.add, modules) * (1.0 / len(modules))
-    refs[-1][...] = rms_rows(pooled).astype(BF16)
+def pool_kernel(resid_ref, keep_ref, got_ref, hidden_ref):
+    modules = resid_ref.shape[0]
+    total = functools.reduce(jnp.add, [resid_ref[m] for m in range(modules)])
+    pooled = total * (1.0 / modules) + (keep_ref[0] + got_ref[0])
+    hidden_ref[...] = rms_rows(pooled).astype(BF16)
+
+
+def pool(resid, keep, got):
+    return launch(
+        pool_kernel,
+        (resid, keep, got),
+        [WHOLE] * 3,
+        out_shape=shape_of(keep.shape[1:], BF16),
+        out_specs=WHOLE,
+    )
 
 
 def out_call(kernel, me, keys, mixed, w_all, resid, out_shape, after=()):
     back = [(o, e) if e & 1 else (e, o) for e, o in keys]
     _, rows, inner = mixed[0].shape
     width = w_all.shape[-1]
+    count = len(keys)
     return launch(
         functools.partial(kernel, [back.index(key) for key in keys], keys),
-        (me, w_all, resid, *mixed),
-        [SCALAR, WHOLE, WHOLE, fixed(1, rows, inner)] + [WHOLE] * (len(mixed) - 1),
+        (me, in_hbm(w_all), resid, *mixed),
+        [SCALAR, ANYWHERE, ANYWHERE] + [ANYWHERE] * len(mixed),
         after,
-        grid=(1,),
         out_shape=out_shape,
         out_specs=[WHOLE] * len(out_shape),
+        scratch_shapes=[
+            pltpu.VMEM((count, rows, inner), BF16),
+            pltpu.VMEM(w_all.shape, BF16),
+            pltpu.VMEM(resid.shape, F32),
+            pltpu.SemaphoreType.DMA((2 * count + 1,)),
+        ],
         cost_estimate=pl.CostEstimate(
-            flops=2 * rows * len(keys) * inner * width,
-            bytes_accessed=len(keys) * inner * (width + rows) * 2 + rows * width * 10,
+            flops=2 * rows * count * inner * width,
+            bytes_accessed=count * inner * (width + rows) * 2 + rows * width * 10,
             transcendentals=0,
         ),
     )
@@ -356,10 +409,12 @@
 
 
 def rate_terms(logit, rate_scale, theta, seen, norm):
-    soft, d_soft = softplus_pair(logit)
+    small = jnp.exp(-jnp.abs(logit))
+    soft = jnp.maximum(logit, 0.0) + jnp.log1p(small)
     rate = rate_scale * soft
     total = theta + rate
-    d_logit = theta * (rate - seen) * norm * d_soft / (soft * total)
+    above = theta * (rate - seen) * jnp.where(logit >= 0.0, norm, norm * small)
+    d_logit = above / (soft * total * (1.0 + small))
     return rate, total, d_logit
 
 
@@ -421,7 +476,7 @@
             panel_col,
             panel_row,
             rate_scale,
-            w_mean_t,
+            in_hbm(w_mean_t),
             w_disp_t,
             *hids,
         ),
@@ -489,7 +544,7 @@
     by_gene = lambda columns: pl.BlockSpec((tile, columns), lambda i: (i, 0))
     return launch(
         functools.partial(far_kernel, keys, other + 1, norm, genes_all),
-        (place, seen, panel_col, w_mean_t, w_disp_t, *hids),
+        (place, seen, panel_col, in_hbm(w_mean_t), w_disp_t, *hids),
         [
             SCALAR,
             WHOLE,
@@ -555,9 +610,12 @@
     for other in range(count):
         hidden = hids[other][...]
         d_disp = sums[other][:panel_count] * sigmoid(dot_nt(wd_ref[...], hidden)) * norm
-        high, middle, low = split3(d_disp)
+        parts = jnp.concatenate([part.astype(F32) for part in split3(d_disp)], axis=0)
+        three = dot_nn(parts.astype(BF16), hidden)
         term_ref[place_ref[1] ^ other] = (
-            dot_nn(high, hidden) + dot_nn(middle, hidden) + dot_nn(low, hidden)
+            three[:panel_count]
+            + three[panel_count : 2 * panel_count]
+            + three[2 * panel_count :]
         )
     total = term_ref[0]
     for block in range(1, count):
@@ -678,7 +736,8 @@
     library = 1.0 + library
     flat_within = flat_qkv(w_qkv_within)
     flat_cross = flat_qkv(w_qkv_cross)
-    out_within = lax.all_gather(flat_out(w_out_within), "gene")
+    out_within = in_hbm(lax.all_gather(flat_out(w_out_within), "gene"))
+    out_cross = flat_out(w_out_cross)
     cell_ids = jnp.tile(jnp.arange(share, dtype=jnp.int32), modules)
     odd = (gene_me & 1) == 1
     owners = gene_me ^ jnp.where(odd, jnp.array([o for _, o in keys]), jnp.array([e for e, _ in keys]))
@@ -690,22 +749,24 @@
     panel_row = panels.reshape(genes_here // tile, 1, tile)
 
     halves = []
+    early = [*cell_ids, *group_ids, panel_col, panel_row]
     for chunk in range(2):
-        early = [*cell_ids, *group_ids, panel_col, panel_row]
-        keep, send = project(
-            me, counts_t, TARGET / library, w_proj, keys, chunk, 2, early if chunk == 0 else []
-        )
+        keep, send = project(me, counts_t, TARGET / library, w_proj, keys, chunk, 2, early)
+        early = []
         halves.append((keep, hop(send, "gene", straight(1))))
-    seen = lax.all_gather(pack(counts_t, library, [halves[0][0]]), "grp")
-    laid = [flat_within, flat_cross]
+    laid = [[flat_within], [flat_cross, out_cross]]
     for at, key in enumerate(far[::-1]):
         nexts = []
         for chunk, (keep, got) in enumerate(halves):
-            keep, send = halve(keep, got, laid[chunk : chunk + 1] if at == 1 else ())
+            keep, send = halve(keep, got, laid[chunk] if at == 1 else ())
             nexts.append((keep, hop(send, "gene", key)))
         halves = nexts
     resid, normed = to_rows(halves, width)
 
+    packed = pack(counts_t, library, [resid])
+    seen = in_hbm(lax.all_gather(packed, "grp"))
+    normed = stack([normed], [out_within, packed])[0]
+
     in_cell = [[(block, m) for m in range(modules)] for block in range(gene_count)]
     across = [[(block, m) for block in range(gene_count)] for m in range(modules)]
 
@@ -713,9 +774,7 @@
         return [mixed] + [hop(mixed[at], "gene", keys[at]) for at in range(1, gene_count)]
 
     blocks = spread(normed, "gene")
-    mixed = attend(blocks, flat_within, cell_ids, in_cell, heads, head_width)
-    out_cross = stack([flat_out(w_out_cross)], [mixed])[0]
-    out_cross = lax.all_gather(out_cross, "gene")
+    (mixed,) = attend(blocks, flat_within, cell_ids, in_cell, heads, head_width)
     rows = (modules, share, width)
     mid, normed = out_call(
         out_kernel,
@@ -727,17 +786,16 @@
         [shape_of(rows, F32), shape_of(rows, BF16)],
     )
 
-    mixed = attend(
-        spread(normed, "gene"),
-        flat_cross,
-        group_ids,
-        across,
-        heads,
-        head_width,
-    )
-    (hidden,) = out_call(
-        pool_kernel, me, keys, send_mixed(mixed), out_cross, mid, [shape_of((share, width), BF16)], [seen]
-    )
+    normed = stack([normed], [seen])[0]
+
+    keep, send = attend(
+        spread(normed, "gene"), flat_cross, group_ids, across, heads, head_width, out_cross
+    )
+    got = hop(send, "gene", straight(1))
+    for key in far[::-1]:
+        keep, send = halve(keep, got, dtype=F32)
+        got = hop(send, "gene", key)
+    hidden = pool(mid, keep, got)
 
     hids = spread(hidden, "gene")
     far_hids = [stack([hop(hidden, "grp", straight(rel)) for rel in range(1, grp_count)], hids)]
@@ -758,7 +816,7 @@
         after = [groups[min(bit, grp_count - 1)][1]]
         sums = add(sums, hop(sums, "gene", straight(1 << bit)), after)
     sums = [sums] + [hop(sums, "grp", straight(rel)) for rel in range(1, grp_count)]
-    grad_mean = grad_mean_call(place, groups)
+    grad_mean = in_hbm(grad_mean_call(place, groups))
     grad_disp, loss = disp_call(
         place, sums, [group[0] for group in groups], w_disp_t, norm, genes_all, [grad_mean]
     )

time: 275 us -> 245 us (0.89)
  local copies, waits for them, and re-layouts: 63 us -> 24.2 us
  waiting for transfers between devices: 80.3 us -> 87 us
  Pallas kernels: 68.1 us -> 72.3 us
    unnamed x139 -> x51, local copies, waits for them, and re-layouts: 50.4 us -> 10.4 us
    ppermute x57 -> x53, waiting for transfers between devices: 80.3 us -> 86.9 us  [hop(): return lax.ppermute(value, axis, [(i, i ^ key[i & 1]) for i in range(size)])]
    pallas_call x24 -> x27, Pallas kernels: 68.1 us -> 72.3 us  [launch(): pl.pallas_call(body, in_specs=list(in_specs) + [ANYWHERE] * len(after), c...]
    ppermute x57 -> x53, starting transfers between devices: 46.1 us -> 45.3 us  [hop(): return lax.ppermute(value, axis, [(i, i ^ key[i & 1]) for i in range(size)])]
  transfers between devices with their start and end apart: 60 -> 55, of which waited for: 24 -> 24; matrix products, arithmetic and copies ran while one was open for 4% -> 5% of each run, Pallas kernels for 22% -> 25%
where the time goes in v3:
time: 245 us; the launch traced here: 244 us
  waiting for transfers between devices  87 us (36%)
  Pallas kernels  72.3 us (30%)
  starting transfers between devices  45.3 us (18%)
  local copies, waits for them, and re-layouts  24.2 us (10%)
  between operations  14.5 us (6%)
    ppermute x53, waiting for transfers between devices, hop(): return lax.ppermute(value, axis, [(i, i ^ key[i & 1]) for i in range(size)])  86.9 us
    pallas_call x27, Pallas kernels, launch(): pl.pallas_call(body, in_specs=list(in_specs) + [ANYWHERE] * len(after), c...  72.3 us
    ppermute x53, starting transfers between devices, hop(): return lax.ppermute(value, axis, [(i, i ^ key[i & 1]) for i in range(size)])  45.3 us
    unnamed x51, local copies, waits for them, and re-layouts  10.4 us
    reshape x2, local copies, waits for them, and re-layouts, flat_qkv(): return weights.transpose(2, 1, 0).reshape(-1, weights.shape[0])  8.55 us
  transfers between devices with their start and end apart: 55, of which 24 were waited for; matrix products, arithmetic and copies ran while one was open for 5% of the time, Pallas kernels for 25%

profile of v3, /device:TPU:0, one launch (start us, length us, event | category | flops | bytes accessed | tf_op | source)
XLA Modules:
  0.0 244.3 jit_solution(3159753014083179048)
XLA Ops:
  7.3 2.4 all_gather_reshape.3
  11.2 2.8 %collective-permute-start.1 = (f32[1,256]{1,0:T(1,128)S(1)}, f32[1,256]{1,0:T(1,128)S(1)}, u32[]{:S(2)}, u32[]{:S(2)}) collective-permute-start(f32[1,256]{1,0:T(1,128)S(1)} %add.19), channel_id=1, source_target_pairs={{0,2},{1,3},{2,0},{3,1},{4,6},{5,7},{6,4},{7,5},{8,10},{9,11},{10,... | collective-permute-start | bytes 3080 | tf_op jit(solution)/shard_map/ppermute | solution.py:96
  15.8 1.8 collective-permute-start.2
  18.4 1.1 collective-permute-done.2
  19.5 6.4 %shard_map.139 = (f32[128,3200]{1,0:T(8,128)S(1)}, f32[128,3200]{1,0:T(8,128)S(1)}) custom-call(s32[1]{0:T(128)} %bitcast.refs_0_, s32[960,256]{1,0:T(8,128)S(1)} %bitcast.31, f32[1,256]{1,0:T(1,128)S(1)} %get-tuple-element.79.refs_2_, bf16[960,6400]{1,0:T(8,128)(2,1)} %refs_3_.3, s32[128,1]{1,0:T(8,128)S(1)} %reshape_tile.12.refs_4_.refs_1_, ...), custom_call_target="tpu_custom_call" | custom-call | flops 1572864000 | bytes 9420800 | tf_op jit(solution)/shard_map/pallas_call | solution.py:43
  25.9 6.3 %shard_map.142 = (f32[128,3200]{1,0:T(8,128)S(1)}, f32[128,3200]{1,0:T(8,128)S(1)}) custom-call(s32[1]{0:T(128)} %bitcast.refs_0_, s32[960,256]{1,0:T(8,128)S(1)} %bitcast.32, f32[1,256]{1,0:T(1,128)S(1)} %get-tuple-element.79.refs_2_, bf16[960,6400]{1,0:T(8,128)(2,1)} %refs_3_.3), custom_call_target="tpu_custom_call" | custom-call | flops 1572864000 | bytes 9420800 | tf_op jit(solution)/shard_map/pallas_call | solution.py:43
  32.7 0.9 shard_map.140
  33.7 1.7 collective-permute-start.4
  35.9 0.9 shard_map.143
  37.7 1.7 collective-permute-start.7
  39.4 4.2 %reshape.78.refs_2_.refs_0_ = bf16[600,1600]{1,0:T(8,128)(2,1)} reshape(bf16[150,4,1600]{2,1,0:T(4,128)(2,1)} %bitcast.56) | data formatting | bytes 3840000 | tf_op jit(solution)/shard_map/reshape | solution.py:693
  43.6 4.3 %reshape.79.refs_2_.refs_0_ = bf16[600,1600]{1,0:T(8,128)(2,1)} reshape(bf16[150,4,1600]{2,1,0:T(4,128)(2,1)} %bitcast.57) | data formatting | bytes 3840000 | tf_op jit(solution)/shard_map/reshape | solution.py:693
  47.9 1.5 reshape.80.refs_3_.refs_11_
  49.6 1.7 copy-done.3
  51.2 1.1 shard_map.141
  52.4 1.9 collective-permute-start.5
  54.3 8.4 %collective-permute-done.7.refs_1_ = bf16[64,3200]{1,0:T(8,128)(2,1)} collective-permute-done((bf16[64,3200]{1,0:T(8,128)(2,1)}, bf16[64,3200]{1,0:T(8,128)(2,1)}, u32[]{:S(2)}, u32[]{:S(2)}) %collective-permute-start.7) | collective-permute-done | bytes 409632 | tf_op jit(solution)/shard_map/ppermute | solution.py:96
  62.8 1.1 shard_map.144
  63.9 1.7 collective-permute-start.8
  65.6 4.1 %collective-permute-done.8.refs_3_ = bf16[32,3200]{1,0:T(8,128)(2,1)S(1)} collective-permute-done((bf16[32,3200]{1,0:T(8,128)(2,1)S(1)}, bf16[32,3200]{1,0:T(8,128)(2,1)S(1)}, u32[]{:S(2)}, u32[]{:S(2)}) %collective-permute-start.8) | collective-permute-done | bytes 204832 | tf_op jit(solution)/shard_map/ppermute | solution.py:96
  72.0 1.0 copy-done.16
  73.1 1.7 collective-permute-start.9
  74.8 1.0 collective-permute-start.10
  75.8 9.5 %collective-permute-done.9.refs_4_ = bf16[4,32,1600]{2,1,0:T(8,128)(2,1)S(1)} collective-permute-done((bf16[4,32,1600]{2,1,0:T(8,128)(2,1)S(1)}, bf16[4,32,1600]{2,1,0:T(8,128)(2,1)S(1)}, u32[]{:S(2)}, u32[]{:S(2)}) %collective-permute-start.9) | collective-permute-done | bytes 409632 | tf_op jit(solution)/shard_map/ppermute | solution.py:96
  85.9 7.6 %collective-permute-done.11.refs_6_ = bf16[4,32,1600]{2,1,0:T(8,128)(2,1)S(1)} collective-permute-done((bf16[4,32,1600]{2,1,0:T(8,128)(2,1)S(1)}, bf16[4,32,1600]{2,1,0:T(8,128)(2,1)S(1)}, u32[]{:S(2)}, u32[]{:S(2)}) %collective-permute-start.11) | collective-permute-done | bytes 409632 | tf_op jit(solution)/shard_map/ppermute | solution.py:96
  93.5 1.7 collective-permute-done.15.refs_10_
  95.2 5.6 %shard_map.148.refs_3_ = bf16[8,128,200]{2,1,0:T(8,128)(2,1)S(1)} custom-call(bf16[600,1600]{1,0:T(8,128)(2,1)S(1)} %copy-done.4, s32[128,1]{1,0:T(8,128)S(1)} %reshape_tile.12.refs_4_.refs_1_, s32[1,128]{1,0:T(1,128)S(1)} %reshape_tile.11.refs_5_.refs_2_, bf16[4,32,1600]{2,1,0:T(8,128)(2,1)S(1)} %bitcast.43, ...), custom_call_target="tpu_custom_call" | custom-call | flops 2385510400 | bytes 5606400 | tf_op jit(solution)/shard_map/pallas_call | solution.py:43
  100.9 1.8 collective-permute-start.16
  102.8 1.7 collective-permute-start.18
  105.2 1.1 collective-permute-start.21
  106.3 1.5 collective-permute-done.17.refs_5_
  108.8 1.0 collective-permute-done.21.refs_9_
  109.8 2.6 %collective-permute-done.22.refs_10_ = bf16[128,200]{1,0:T(8,128)(2,1)S(1)} collective-permute-done((bf16[128,200]{1,0:T(8,128)(2,1)S(1)}, bf16[128,200]{1,0:T(8,128)(2,1)S(1)}, u32[]{:S(2)}, u32[]{:S(2)}) %collective-permute-start.22) | collective-permute-done | bytes 51232 | tf_op jit(solution)/shard_map/ppermute | solution.py:96
  112.5 3.8 %shard_map.149 = (f32[4,32,1600]{2,1,0:T(8,128)S(1)}, bf16[4,32,1600]{2,1,0:T(8,128)(2,1)S(1)}) custom-call(s32[1]{0:T(128)} %bitcast.refs_0_, bf16[8,200,1600]{2,1,0:T(8,128)(2,1)} %all-gather.4.cloned.1.call-done.refs_1_, f32[4,32,1600]{2,1,0:T(8,128)S(1)} %get-tuple-element.52.refs_2_, bf16[8,128,200]{2,1,0:T(8,128)(2,1)S(1)} %shard_map.148.refs_3_, ...), custom_call_target="tpu_custom_call" | custom-call | flops 655360000 | bytes 7577600 | tf_op jit(solution)/shard_map/pallas_call | solution.py:43
  116.3 0.9 copy-done.11
  117.9 1.1 copy-done.18
  119.6 1.5 collective-permute-start.24
  121.1 10.7 %collective-permute-done.23.refs_4_ = bf16[4,32,1600]{2,1,0:T(8,128)(2,1)S(1)} collective-permute-done((bf16[4,32,1600]{2,1,0:T(8,128)(2,1)S(1)}, bf16[4,32,1600]{2,1,0:T(8,128)(2,1)S(1)}, u32[]{:S(2)}, u32[]{:S(2)}) %collective-permute-start.23) | collective-permute-done | bytes 409632 | tf_op jit(solution)/shard_map/ppermute | solution.py:96
  132.5 7.5 %collective-permute-done.25.refs_6_ = bf16[4,32,1600]{2,1,0:T(8,128)(2,1)S(1)} collective-permute-done((bf16[4,32,1600]{2,1,0:T(8,128)(2,1)S(1)}, bf16[4,32,1600]{2,1,0:T(8,128)(2,1)S(1)}, u32[]{:S(2)}, u32[]{:S(2)}) %collective-permute-start.25) | collective-permute-done | bytes 409632 | tf_op jit(solution)/shard_map/ppermute | solution.py:96
  140.0 1.7 collective-permute-done.29.refs_10_
  141.7 6.2 %shard_map.151 = (f32[4,32,1600]{2,1,0:T(8,128)S(1)}, f32[4,32,1600]{2,1,0:T(8,128)S(1)}) custom-call(bf16[600,1600]{1,0:T(8,128)(2,1)S(1)} %copy-done.2, s32[256,1]{1,0:T(8,128)S(1)} %select_n.43.refs_6_.refs_1_, s32[1,256]{1,0:T(1,128)S(1)} %select_n.42.refs_7_.refs_2_, bf16[4,32,1600]{2,1,0:T(8,128)(2,1)S(1)} %bitcast.47, ...), custom_call_target="tpu_custom_call" | custom-call | flops 2804940800 | bytes 5606400 | tf_op jit(solution)/shard_map/pallas_call | solution.py:43
  148.1 2.2 collective-permute-done.30.refs_1_
  150.7 8.0 %collective-permute-done.31.refs_1_ = f32[2,32,1600]{2,1,0:T(8,128)S(1)} collective-permute-done((f32[2,32,1600]{2,1,0:T(8,128)S(1)}, f32[2,32,1600]{2,1,0:T(8,128)S(1)}, u32[]{:S(2)}, u32[]{:S(2)}) %collective-permute-start.31) | collective-permute-done | bytes 409632 | tf_op jit(solution)/shard_map/ppermute | solution.py:96
  159.0 5.7 %collective-permute-done.32.refs_2_ = f32[1,32,1600]{2,1,0:T(8,128)S(1)} collective-permute-done((f32[1,32,1600]{2,1,0:T(8,128)S(1)}, f32[1,32,1600]{2,1,0:T(8,128)S(1)}, u32[]{:S(2)}, u32[]{:S(2)}) %collective-permute-start.32) | collective-permute-done | bytes 204832 | tf_op jit(solution)/shard_map/ppermute | solution.py:96
  165.1 1.7 collective-permute-start.34
  167.2 2.3 collective-permute-done.33.refs_8_.refs_4_
  169.9 3.0 %collective-permute-start.43 = (bf16[32,1600]{1,0:T(8,128)(2,1)S(1)}, bf16[32,1600]{1,0:T(8,128)(2,1)S(1)}, u32[]{:S(2)}, u32[]{:S(2)}) collective-permute-start(bf16[32,1600]{1,0:T(8,128)(2,1)S(1)} %shard_map.154.refs_7_.refs_3_), channel_id=1, source_target_pairs={{0,16},{8,24},{16,0},{24,8},{1,17},{9,25},{17,1},{25,9},{2,18},{10... | collective-permute-start | bytes 307208 | tf_op jit(solution)/shard_map/ppermute | solution.py:96
  172.9 1.4 collective-permute-start.44
  174.9 5.4 %collective-permute-done.43.refs_1_ = bf16[32,1600]{1,0:T(8,128)(2,1)S(1)} collective-permute-done((bf16[32,1600]{1,0:T(8,128)(2,1)S(1)}, bf16[32,1600]{1,0:T(8,128)(2,1)S(1)}, u32[]{:S(2)}, u32[]{:S(2)}) %collective-permute-start.43) | collective-permute-done | bytes 102432 | tf_op jit(solution)/shard_map/ppermute | solution.py:96
  180.3 1.3 collective-permute-start.45
  181.6 1.6 collective-permute-start.46
  183.9 9.3 %shard_map.155 = (bf16[960,256]{1,0:T(8,128)(2,1)S(1)}, bf16[960,256]{1,0:T(8,128)(2,1)S(1)}, f32[72,256]{1,0:T(8,128)S(1)}, bf16[256,1600]{1,0:T(8,128)(2,1)S(1)}) custom-call(s32[1]{0:T(128)} %bitcast.refs_0_, s32[960,256]{1,0:T(8,128)S(1)} %bitcast.34, s32[960,1]{1,0:T(8,128)S(1)} %copy.31.refs_8_.refs_2_, s32[4,1,240]{2,1,0:T(1,128)S(1)} %reshape.76.refs_9_.refs_3_, ...), custom_call_target="tpu_custom_call" | custom-call | flops 823296000 | bytes 5038080 | tf_op jit(solution)/shard_map/pallas_call | solution.py:43
  194.1 1.3 collective-permute-done.47.refs_3_
  196.9 2.5 %collective-permute-done.40.refs_1_ = f32[72,256]{1,0:T(8,128)S(1)} collective-permute-done((f32[72,256]{1,0:T(8,128)S(1)}, f32[72,256]{1,0:T(8,128)S(1)}, u32[]{:S(2)}, u32[]{:S(2)}) %collective-permute-start.40) | collective-permute-done | bytes 73760 | tf_op jit(solution)/shard_map/ppermute | solution.py:96
  199.4 1.0 copy-done.7
  201.1 5.7 %shard_map.159 = (bf16[960,256]{1,0:T(8,128)(2,1)S(1)}, bf16[960,256]{1,0:T(8,128)(2,1)S(1)}, bf16[256,1600]{1,0:T(8,128)(2,1)S(1)}) custom-call(s32[2]{0:T(128)S(1)} %pad_add_fusion.refs_0_, bf16[4,976,256]{2,1,0:T(8,128)(2,1)} %bitcast.53, s32[960,1]{1,0:T(8,128)S(1)} %copy.31.refs_8_.refs_2_, bf16[960,1600]{1,0:T(8,128)(2,1)} %bitcast.49, ...), custom_call_target="tpu_custom_call" | custom-call | flops 801177600 | bytes 4546560 | tf_op jit(solution)/shard_map/pallas_call | solution.py:43
  206.9 2.2 collective-permute-start.49
  209.1 5.7 %shard_map.163 = (bf16[960,256]{1,0:T(8,128)(2,1)S(1)}, bf16[960,256]{1,0:T(8,128)(2,1)S(1)}, bf16[256,1600]{1,0:T(8,128)(2,1)S(1)}) custom-call(s32[2]{0:T(128)S(1)} %pad_add_fusion.refs_0_, bf16[4,976,256]{2,1,0:T(8,128)(2,1)} %bitcast.54, s32[960,1]{1,0:T(8,128)S(1)} %copy.31.refs_8_.refs_2_, bf16[960,1600]{1,0:T(8,128)(2,1)} %bitcast.50, ...), custom_call_target="tpu_custom_call" | custom-call | flops 801177600 | bytes 4546560 | tf_op jit(solution)/shard_map/pallas_call | solution.py:43
  214.8 5.8 %shard_map.161 = (bf16[960,256]{1,0:T(8,128)(2,1)S(1)}, bf16[960,256]{1,0:T(8,128)(2,1)S(1)}, bf16[256,1600]{1,0:T(8,128)(2,1)S(1)}) custom-call(s32[2]{0:T(128)S(1)} %pad_add_fusion.refs_0_, bf16[4,976,256]{2,1,0:T(8,128)(2,1)} %bitcast.55, s32[960,1]{1,0:T(8,128)S(1)} %copy.31.refs_8_.refs_2_, bf16[960,1600]{1,0:T(8,128)(2,1)} %bitcast.51, ...), custom_call_target="tpu_custom_call" | custom-call | flops 801177600 | bytes 4546560 | tf_op jit(solution)/shard_map/pallas_call | solution.py:43
  220.7 2.9 %collective-permute-start.50 = (f32[72,256]{1,0:T(8,128)S(1)}, f32[72,256]{1,0:T(8,128)S(1)}, u32[]{:S(2)}, u32[]{:S(2)}) collective-permute-start(f32[72,256]{1,0:T(8,128)S(1)} %shard_map.162.refs_2_), channel_id=1, source_target_pairs={{0,8},{8,0},{16,24},{24,16},{1,9},{9,1},{17,25},{25,17},{2,10},{10... | collective-permute-start | bytes 221192 | tf_op jit(solution)/shard_map/ppermute | solution.py:96
  223.6 0.9 collective-permute-start.51
  224.5 1.5 collective-permute-start.52
  226.1 6.3 %shard_map.164.refs_10_ = f32[400,960]{1,0:T(8,128)} custom-call(s32[2]{0:T(128)S(1)} %pad_add_fusion.refs_0_, bf16[256,1600]{1,0:T(8,128)(2,1)S(1)} %copy-done.10, bf16[960,256]{1,0:T(8,128)(2,1)S(1)} %copy-done.8, bf16[960,256]{1,0:T(8,128)(2,1)S(1)} %copy-done.20, bf16[256,1600]{1,0:T(8,128)(2,1)S(1)} %get-tuple-element.67.refs_4_.refs_7_, ...), custom_call_target="tpu_custom_call" | custom-call | flops 2883584000 | bytes 8744960 | tf_op jit(solution)/shard_map/pallas_call | solution.py:43
  232.4 5.1 %shard_map.165 = (f32[64,1600]{1,0:T(8,128)}, f32[1,256]{1,0:T(1,128)}) custom-call(s32[2]{0:T(128)S(1)} %pad_add_fusion.refs_0_, bf16[64,1600]{1,0:T(8,128)(2,1)S(1)} %bitcast.39, f32[72,256]{1,0:T(8,128)S(1)} %shard_map.162.refs_2_, f32[72,256]{1,0:T(8,128)S(1)} %collective-permute-done.50.refs_3_, f32[72,256]{1,0:T(8,128)S(1)} %collective-permute-done.51.refs_4_, ...), custom_call_target="tpu_custom_call" | custom-call | tf_op jit(solution)/shard_map/pallas_call | solution.py:43
  (151 shorter events, 19.6 us)
Async XLA Ops:
  7.2 64.8 %all-gather.4.cloned.1.call-start = ((), (), s32[]{:S(2)}) async-start(), calls=%async_computation | async-start | bytes 5990400 | tf_op jit(solution)/shard_map/all_gather | solution.py:739
  9.7 108.3 %all-gather.6.cloned.1.call-start = ((), (), s32[]{:S(2)}) async-start(), calls=%async_computation.1 | async-start | bytes 2498560 | tf_op jit(solution)/shard_map/all_gather | solution.py:767
  9.9 1.3 collective-permute-start
  11.2 4.6 %collective-permute-start.1 = (f32[1,256]{1,0:T(1,128)S(1)}, f32[1,256]{1,0:T(1,128)S(1)}, u32[]{:S(2)}, u32[]{:S(2)}) collective-permute-start(f32[1,256]{1,0:T(1,128)S(1)} %add.19), channel_id=1, source_target_pairs={{0,2},{1,3},{2,0},{3,1},{4,6},{5,7},{6,4},{7,5},{8,10},{9,11},{10,... | collective-permute-start | bytes 3080 | tf_op jit(solution)/shard_map/ppermute | solution.py:96
  15.8 3.6 %collective-permute-start.2 = (f32[1,256]{1,0:T(1,128)S(1)}, f32[1,256]{1,0:T(1,128)S(1)}, u32[]{:S(2)}, u32[]{:S(2)}) collective-permute-start(f32[1,256]{1,0:T(1,128)S(1)} %add.20), channel_id=1, source_target_pairs={{0,4},{1,5},{2,6},{3,7},{4,0},{5,1},{6,2},{7,3},{8,12},{9,13},{10,... | collective-permute-start | bytes 3080 | tf_op jit(solution)/shard_map/ppermute | solution.py:96
  25.9 6.9 %collective-permute-start.3 = (f32[128,3200]{1,0:T(8,128)S(1)}, f32[128,3200]{1,0:T(8,128)S(1)}, u32[]{:S(2)}, u32[]{:S(2)}) collective-permute-start(f32[128,3200]{1,0:T(8,128)S(1)} %get-tuple-element.41), channel_id=1, source_target_pairs={{0,1},{1,0},{2,3},{3,2},{4,5},{5,4},{6,7},{7,6},{8,9},{9,8},{10,11... | collective-permute-start | bytes 4915208 | tf_op jit(solution)/shard_map/ppermute | solution.py:96
  32.2 3.7 %collective-permute-start.6 = (f32[128,3200]{1,0:T(8,128)S(1)}, f32[128,3200]{1,0:T(8,128)S(1)}, u32[]{:S(2)}, u32[]{:S(2)}) collective-permute-start(f32[128,3200]{1,0:T(8,128)S(1)} %get-tuple-element.47), channel_id=1, source_target_pairs={{0,1},{1,0},{2,3},{3,2},{4,5},{5,4},{6,7},{7,6},{8,9},{9,8},{10,11... | collective-permute-start | bytes 4915208 | tf_op jit(solution)/shard_map/ppermute | solution.py:96
  33.7 15.9 %collective-permute-start.4 = (bf16[64,3200]{1,0:T(8,128)(2,1)}, bf16[64,3200]{1,0:T(8,128)(2,1)}, u32[]{:S(2)}, u32[]{:S(2)}) collective-permute-start(bf16[64,3200]{1,0:T(8,128)(2,1)} %get-tuple-element.43), channel_id=1, source_target_pairs={{0,4},{1,3},{2,6},{3,1},{4,0},{5,7},{6,2},{7,5},{8,12},{9,11},{10,... | collective-permute-start | bytes 1228808 | tf_op jit(solution)/shard_map/ppermute | solution.py:96
  37.7 25.1 %collective-permute-start.7 = (bf16[64,3200]{1,0:T(8,128)(2,1)}, bf16[64,3200]{1,0:T(8,128)(2,1)}, u32[]{:S(2)}, u32[]{:S(2)}) collective-permute-start(bf16[64,3200]{1,0:T(8,128)(2,1)} %get-tuple-element.49), channel_id=1, source_target_pairs={{0,4},{1,3},{2,6},{3,1},{4,0},{5,7},{6,2},{7,5},{8,12},{9,11},{10,... | collective-permute-start | bytes 1228808 | tf_op jit(solution)/shard_map/ppermute | solution.py:96
  49.4 13.4 %copy-start.1 = (bf16[600,1600]{1,0:T(8,128)(2,1)S(1)}, bf16[600,1600]{1,0:T(8,128)(2,1)}, u32[]{:S(2)}) copy-start(bf16[600,1600]{1,0:T(8,128)(2,1)} %reshape.79.refs_2_.refs_0_) | copy-start | bytes 5760004
  51.2 11.5 %copy-start.14 = (f32[64,3200]{1,0:T(8,128)S(1)}, f32[64,3200]{1,0:T(8,128)}, u32[]{:S(2)}) copy-start(f32[64,3200]{1,0:T(8,128)} %copy-done.13) | copy-start | bytes 2457604
  52.4 13.2 %collective-permute-start.5 = (bf16[32,3200]{1,0:T(8,128)(2,1)S(1)}, bf16[32,3200]{1,0:T(8,128)(2,1)S(1)}, u32[]{:S(2)}, u32[]{:S(2)}) collective-permute-start(bf16[32,3200]{1,0:T(8,128)(2,1)S(1)} %get-tuple-element.45), channel_id=1, source_target_pairs={{0,2},{1,5},{2,0},{3,7},{4,6},{5,1},{6,4},{7,3},{8,10},{9,13},{10,... | collective-permute-start | bytes 614408 | tf_op jit(solution)/shard_map/ppermute | solution.py:96
  63.9 5.8 %collective-permute-start.8 = (bf16[32,3200]{1,0:T(8,128)(2,1)S(1)}, bf16[32,3200]{1,0:T(8,128)(2,1)S(1)}, u32[]{:S(2)}, u32[]{:S(2)}) collective-permute-start(bf16[32,3200]{1,0:T(8,128)(2,1)S(1)} %get-tuple-element.51), channel_id=1, source_target_pairs={{0,2},{1,5},{2,0},{3,7},{4,6},{5,1},{6,4},{7,3},{8,10},{9,13},{10,... | collective-permute-start | bytes 614408 | tf_op jit(solution)/shard_map/ppermute | solution.py:96
  73.0 22.2 %copy-start.4 = (bf16[600,1600]{1,0:T(8,128)(2,1)S(1)}, bf16[600,1600]{1,0:T(8,128)(2,1)}, u32[]{:S(2)}) copy-start(bf16[600,1600]{1,0:T(8,128)(2,1)} %reshape.78.refs_2_.refs_0_) | copy-start | bytes 5760004
  73.1 12.3 %collective-permute-start.9 = (bf16[4,32,1600]{2,1,0:T(8,128)(2,1)S(1)}, bf16[4,32,1600]{2,1,0:T(8,128)(2,1)S(1)}, u32[]{:S(2)}, u32[]{:S(2)}) collective-permute-start(bf16[4,32,1600]{2,1,0:T(8,128)(2,1)S(1)} %bitcast.40), channel_id=1, source_target_pairs={{0,2},{1,5},{2,0},{3,7},{4,6},{5,1},{6,4},{7,3},{8,10},{9,13},{10,... | collective-permute-start | bytes 1228808 | tf_op jit(solution)/shard_map/ppermute | solution.py:96
  74.8 11.1 %collective-permute-start.10 = (bf16[4,32,1600]{2,1,0:T(8,128)(2,1)S(1)}, bf16[4,32,1600]{2,1,0:T(8,128)(2,1)S(1)}, u32[]{:S(2)}, u32[]{:S(2)}) collective-permute-start(bf16[4,32,1600]{2,1,0:T(8,128)(2,1)S(1)} %bitcast.41), channel_id=1, source_target_pairs={{0,4},{1,3},{2,6},{3,1},{4,0},{5,7},{6,2},{7,5},{8,12},{9,11},{10,... | collective-permute-start | bytes 1228808 | tf_op jit(solution)/shard_map/ppermute | solution.py:96
  85.3 8.1 %collective-permute-start.11 = (bf16[4,32,1600]{2,1,0:T(8,128)(2,1)S(1)}, bf16[4,32,1600]{2,1,0:T(8,128)(2,1)S(1)}, u32[]{:S(2)}, u32[]{:S(2)}) collective-permute-start(bf16[4,32,1600]{2,1,0:T(8,128)(2,1)S(1)} %collective-permute-done.9.refs_4_), channel_id=1, source_target_pairs={{0,4},{1,3},{2,6},{3,1},{4,0},{5,7},{6,2},{7,5},{8,12},{9,11},{10,... | collective-permute-start | bytes 1228808 | tf_op jit(solution)/shard_map/ppermute | solution.py:96
  85.4 8.1 %collective-permute-start.12 = (bf16[4,32,1600]{2,1,0:T(8,128)(2,1)S(1)}, bf16[4,32,1600]{2,1,0:T(8,128)(2,1)S(1)}, u32[]{:S(2)}, u32[]{:S(2)}) collective-permute-start(bf16[4,32,1600]{2,1,0:T(8,128)(2,1)S(1)} %bitcast.42), channel_id=1, source_target_pairs={{0,1},{1,0},{2,3},{3,2},{4,5},{5,4},{6,7},{7,6},{8,9},{9,8},{10,11... | collective-permute-start | bytes 1228808 | tf_op jit(solution)/shard_map/ppermute | solution.py:96
  85.4 8.1 %collective-permute-start.13 = (bf16[4,32,1600]{2,1,0:T(8,128)(2,1)S(1)}, bf16[4,32,1600]{2,1,0:T(8,128)(2,1)S(1)}, u32[]{:S(2)}, u32[]{:S(2)}) collective-permute-start(bf16[4,32,1600]{2,1,0:T(8,128)(2,1)S(1)} %collective-permute-done.9.refs_4_), channel_id=1, source_target_pairs={{0,1},{1,0},{2,3},{3,2},{4,5},{5,4},{6,7},{7,6},{8,9},{9,8},{10,11... | collective-permute-start | bytes 1228808 | tf_op jit(solution)/shard_map/ppermute | solution.py:96
  85.9 7.6 %collective-permute-start.14 = (bf16[4,32,1600]{2,1,0:T(8,128)(2,1)S(1)}, bf16[4,32,1600]{2,1,0:T(8,128)(2,1)S(1)}, u32[]{:S(2)}, u32[]{:S(2)}) collective-permute-start(bf16[4,32,1600]{2,1,0:T(8,128)(2,1)S(1)} %collective-permute-done.10.refs_5_), channel_id=1, source_target_pairs={{0,1},{1,0},{2,3},{3,2},{4,5},{5,4},{6,7},{7,6},{8,9},{9,8},{10,11... | collective-permute-start | bytes 1228808 | tf_op jit(solution)/shard_map/ppermute | solution.py:96
  93.5 1.8 collective-permute-start.15
  100.9 4.3 %collective-permute-start.16 = (bf16[128,200]{1,0:T(8,128)(2,1)S(1)}, bf16[128,200]{1,0:T(8,128)(2,1)S(1)}, u32[]{:S(2)}, u32[]{:S(2)}) collective-permute-start(bf16[128,200]{1,0:T(8,128)(2,1)S(1)} %get-tuple-element.87), channel_id=1, source_target_pairs={{0,2},{1,5},{2,0},{3,7},{4,6},{5,1},{6,4},{7,3},{8,10},{9,13},{10,... | collective-permute-start | bytes 153608 | tf_op jit(solution)/shard_map/ppermute | solution.py:96
  102.7 5.1 %collective-permute-start.17 = (bf16[128,200]{1,0:T(8,128)(2,1)S(1)}, bf16[128,200]{1,0:T(8,128)(2,1)S(1)}, u32[]{:S(2)}, u32[]{:S(2)}) collective-permute-start(bf16[128,200]{1,0:T(8,128)(2,1)S(1)} %get-tuple-element.86), channel_id=1, source_target_pairs={{0,4},{1,3},{2,6},{3,1},{4,0},{5,7},{6,2},{7,5},{8,12},{9,11},{10,... | collective-permute-start | bytes 153608 | tf_op jit(solution)/shard_map/ppermute | solution.py:96
  102.8 5.8 %collective-permute-start.18 = (bf16[128,200]{1,0:T(8,128)(2,1)S(1)}, bf16[128,200]{1,0:T(8,128)(2,1)S(1)}, u32[]{:S(2)}, u32[]{:S(2)}) collective-permute-start(bf16[128,200]{1,0:T(8,128)(2,1)S(1)} %get-tuple-element.85), channel_id=1, source_target_pairs={{0,6},{1,7},{2,4},{3,5},{4,2},{5,3},{6,0},{7,1},{8,14},{9,15},{10,... | collective-permute-start | bytes 153608 | tf_op jit(solution)/shard_map/ppermute | solution.py:96
  104.5 4.2 %collective-permute-start.19 = (bf16[128,200]{1,0:T(8,128)(2,1)S(1)}, bf16[128,200]{1,0:T(8,128)(2,1)S(1)}, u32[]{:S(2)}, u32[]{:S(2)}) collective-permute-start(bf16[128,200]{1,0:T(8,128)(2,1)S(1)} %get-tuple-element.84), channel_id=1, source_target_pairs={{0,1},{1,0},{2,3},{3,2},{4,5},{5,4},{6,7},{7,6},{8,9},{9,8},{10,11... | collective-permute-start | bytes 153608 | tf_op jit(solution)/shard_map/ppermute | solution.py:96
  104.5 4.3 %collective-permute-start.20 = (bf16[128,200]{1,0:T(8,128)(2,1)S(1)}, bf16[128,200]{1,0:T(8,128)(2,1)S(1)}, u32[]{:S(2)}, u32[]{:S(2)}) collective-permute-start(bf16[128,200]{1,0:T(8,128)(2,1)S(1)} %get-tuple-element.83), channel_id=1, source_target_pairs={{0,5},{1,2},{2,7},{3,0},{4,1},{5,6},{6,3},{7,4},{8,13},{9,10},{10,... | collective-permute-start | bytes 153608 | tf_op jit(solution)/shard_map/ppermute | solution.py:96
  105.2 4.6 %collective-permute-start.21 = (bf16[128,200]{1,0:T(8,128)(2,1)S(1)}, bf16[128,200]{1,0:T(8,128)(2,1)S(1)}, u32[]{:S(2)}, u32[]{:S(2)}) collective-permute-start(bf16[128,200]{1,0:T(8,128)(2,1)S(1)} %get-tuple-element.82), channel_id=1, source_target_pairs={{0,3},{1,4},{2,1},{3,6},{4,7},{5,0},{6,5},{7,2},{8,11},{9,12},{10,... | collective-permute-start | bytes 153608 | tf_op jit(solution)/shard_map/ppermute | solution.py:96
  107.9 4.6 %collective-permute-start.22 = (bf16[128,200]{1,0:T(8,128)(2,1)S(1)}, bf16[128,200]{1,0:T(8,128)(2,1)S(1)}, u32[]{:S(2)}, u32[]{:S(2)}) collective-permute-start(bf16[128,200]{1,0:T(8,128)(2,1)S(1)} %get-tuple-element.81), channel_id=1, source_target_pairs={{0,7},{1,6},{2,5},{3,4},{4,3},{5,2},{6,1},{7,0},{8,15},{9,14},{10,... | collective-permute-start | bytes 153608 | tf_op jit(solution)/shard_map/ppermute | solution.py:96
  117.9 23.8 %copy-start.2 = (bf16[600,1600]{1,0:T(8,128)(2,1)S(1)}, bf16[600,1600]{1,0:T(8,128)(2,1)}, u32[]{:S(2)}) copy-start(bf16[600,1600]{1,0:T(8,128)(2,1)} %reshape.79.refs_2_.refs_0_) | copy-start | bytes 5760004
  119.1 12.7 %collective-permute-start.23 = (bf16[4,32,1600]{2,1,0:T(8,128)(2,1)S(1)}, bf16[4,32,1600]{2,1,0:T(8,128)(2,1)S(1)}, u32[]{:S(2)}, u32[]{:S(2)}) collective-permute-start(bf16[4,32,1600]{2,1,0:T(8,128)(2,1)S(1)} %bitcast.44), channel_id=1, source_target_pairs={{0,2},{1,5},{2,0},{3,7},{4,6},{5,1},{6,4},{7,3},{8,10},{9,13},{10,... | collective-permute-start | bytes 1228808 | tf_op jit(solution)/shard_map/ppermute | solution.py:96
  119.6 12.8 %collective-permute-start.24 = (bf16[4,32,1600]{2,1,0:T(8,128)(2,1)S(1)}, bf16[4,32,1600]{2,1,0:T(8,128)(2,1)S(1)}, u32[]{:S(2)}, u32[]{:S(2)}) collective-permute-start(bf16[4,32,1600]{2,1,0:T(8,128)(2,1)S(1)} %bitcast.45), channel_id=1, source_target_pairs={{0,4},{1,3},{2,6},{3,1},{4,0},{5,7},{6,2},{7,5},{8,12},{9,11},{10,... | collective-permute-start | bytes 1228808 | tf_op jit(solution)/shard_map/ppermute | solution.py:96
  131.8 8.1 %collective-permute-start.25 = (bf16[4,32,1600]{2,1,0:T(8,128)(2,1)S(1)}, bf16[4,32,1600]{2,1,0:T(8,128)(2,1)S(1)}, u32[]{:S(2)}, u32[]{:S(2)}) collective-permute-start(bf16[4,32,1600]{2,1,0:T(8,128)(2,1)S(1)} %collective-permute-done.23.refs_4_), channel_id=1, source_target_pairs={{0,4},{1,3},{2,6},{3,1},{4,0},{5,7},{6,2},{7,5},{8,12},{9,11},{10,... | collective-permute-start | bytes 1228808 | tf_op jit(solution)/shard_map/ppermute | solution.py:96
  131.9 8.0 %collective-permute-start.26 = (bf16[4,32,1600]{2,1,0:T(8,128)(2,1)S(1)}, bf16[4,32,1600]{2,1,0:T(8,128)(2,1)S(1)}, u32[]{:S(2)}, u32[]{:S(2)}) collective-permute-start(bf16[4,32,1600]{2,1,0:T(8,128)(2,1)S(1)} %bitcast.46), channel_id=1, source_target_pairs={{0,1},{1,0},{2,3},{3,2},{4,5},{5,4},{6,7},{7,6},{8,9},{9,8},{10,11... | collective-permute-start | bytes 1228808 | tf_op jit(solution)/shard_map/ppermute | solution.py:96
  132.0 8.0 %collective-permute-start.27 = (bf16[4,32,1600]{2,1,0:T(8,128)(2,1)S(1)}, bf16[4,32,1600]{2,1,0:T(8,128)(2,1)S(1)}, u32[]{:S(2)}, u32[]{:S(2)}) collective-permute-start(bf16[4,32,1600]{2,1,0:T(8,128)(2,1)S(1)} %collective-permute-done.23.refs_4_), channel_id=1, source_target_pairs={{0,1},{1,0},{2,3},{3,2},{4,5},{5,4},{6,7},{7,6},{8,9},{9,8},{10,11... | collective-permute-start | bytes 1228808 | tf_op jit(solution)/shard_map/ppermute | solution.py:96
  132.5 7.5 %collective-permute-start.28 = (bf16[4,32,1600]{2,1,0:T(8,128)(2,1)S(1)}, bf16[4,32,1600]{2,1,0:T(8,128)(2,1)S(1)}, u32[]{:S(2)}, u32[]{:S(2)}) collective-permute-start(bf16[4,32,1600]{2,1,0:T(8,128)(2,1)S(1)} %collective-permute-done.24.refs_5_), channel_id=1, source_target_pairs={{0,1},{1,0},{2,3},{3,2},{4,5},{5,4},{6,7},{7,6},{8,9},{9,8},{10,11... | collective-permute-start | bytes 1228808 | tf_op jit(solution)/shard_map/ppermute | solution.py:96
  139.9 1.8 collective-permute-start.29
  147.9 16.7 %copy-start.12 = (f32[4,32,1600]{2,1,0:T(8,128)S(1)}, f32[4,32,1600]{2,1,0:T(8,128)}, u32[]{:S(2)}) copy-start(f32[4,32,1600]{2,1,0:T(8,128)} %copy-done.11) | copy-start | bytes 2457604
  147.9 2.4 %collective-permute-start.30 = (f32[4,32,1600]{2,1,0:T(8,128)S(1)}, f32[4,32,1600]{2,1,0:T(8,128)S(1)}, u32[]{:S(2)}, u32[]{:S(2)}) collective-permute-start(f32[4,32,1600]{2,1,0:T(8,128)S(1)} %get-tuple-element.57), channel_id=1, source_target_pairs={{0,1},{1,0},{2,3},{3,2},{4,5},{5,4},{6,7},{7,6},{8,9},{9,8},{10,11... | collective-permute-start | bytes 2457608 | tf_op jit(solution)/shard_map/ppermute | solution.py:96
  150.5 8.2 %collective-permute-start.31 = (f32[2,32,1600]{2,1,0:T(8,128)S(1)}, f32[2,32,1600]{2,1,0:T(8,128)S(1)}, u32[]{:S(2)}, u32[]{:S(2)}) collective-permute-start(f32[2,32,1600]{2,1,0:T(8,128)S(1)} %get-tuple-element.59), channel_id=1, source_target_pairs={{0,4},{1,3},{2,6},{3,1},{4,0},{5,7},{6,2},{7,5},{8,12},{9,11},{10,... | collective-permute-start | bytes 1228808 | tf_op jit(solution)/shard_map/ppermute | solution.py:96
  158.7 25.2 %copy-start.5 = (bf16[1600,64]{0,1:T(8,128)(2,1)S(1)}, bf16[1600,64]{0,1:T(8,128)(2,1)}, u32[]{:S(2)}) copy-start(bf16[1600,64]{0,1:T(8,128)(2,1)} %param.21) | copy-start | bytes 614404
  158.7 5.9 %collective-permute-start.32 = (f32[1,32,1600]{2,1,0:T(8,128)S(1)}, f32[1,32,1600]{2,1,0:T(8,128)S(1)}, u32[]{:S(2)}, u32[]{:S(2)}) collective-permute-start(f32[1,32,1600]{2,1,0:T(8,128)S(1)} %get-tuple-element.61), channel_id=1, source_target_pairs={{0,2},{1,5},{2,0},{3,7},{4,6},{5,1},{6,4},{7,3},{8,10},{9,13},{10,... | collective-permute-start | bytes 614408 | tf_op jit(solution)/shard_map/ppermute | solution.py:96
  164.8 4.8 %collective-permute-start.33 = (bf16[32,1600]{1,0:T(8,128)(2,1)S(1)}, bf16[32,1600]{1,0:T(8,128)(2,1)S(1)}, u32[]{:S(2)}, u32[]{:S(2)}) collective-permute-start(bf16[32,1600]{1,0:T(8,128)(2,1)S(1)} %shard_map.154.refs_7_.refs_3_), channel_id=1, source_target_pairs={{0,2},{1,5},{2,0},{3,7},{4,6},{5,1},{6,4},{7,3},{8,10},{9,13},{10,... | collective-permute-start | bytes 307208 | tf_op jit(solution)/shard_map/ppermute | solution.py:96
  165.1 7.8 %collective-permute-start.34 = (bf16[32,1600]{1,0:T(8,128)(2,1)S(1)}, bf16[32,1600]{1,0:T(8,128)(2,1)S(1)}, u32[]{:S(2)}, u32[]{:S(2)}) collective-permute-start(bf16[32,1600]{1,0:T(8,128)(2,1)S(1)} %shard_map.154.refs_7_.refs_3_), channel_id=1, source_target_pairs={{0,4},{1,3},{2,6},{3,1},{4,0},{5,7},{6,2},{7,5},{8,12},{9,11},{10,... | collective-permute-start | bytes 307208 | tf_op jit(solution)/shard_map/ppermute | solution.py:96
  166.8 7.5 %collective-permute-start.36 = (bf16[32,1600]{1,0:T(8,128)(2,1)S(1)}, bf16[32,1600]{1,0:T(8,128)(2,1)S(1)}, u32[]{:S(2)}, u32[]{:S(2)}) collective-permute-start(bf16[32,1600]{1,0:T(8,128)(2,1)S(1)} %shard_map.154.refs_7_.refs_3_), channel_id=1, source_target_pairs={{0,1},{1,0},{2,3},{3,2},{4,5},{5,4},{6,7},{7,6},{8,9},{9,8},{10,11... | collective-permute-start | bytes 307208 | tf_op jit(solution)/shard_map/ppermute | solution.py:96
  166.8 7.6 %collective-permute-start.42 = (bf16[32,1600]{1,0:T(8,128)(2,1)S(1)}, bf16[32,1600]{1,0:T(8,128)(2,1)S(1)}, u32[]{:S(2)}, u32[]{:S(2)}) collective-permute-start(bf16[32,1600]{1,0:T(8,128)(2,1)S(1)} %shard_map.154.refs_7_.refs_3_), channel_id=1, source_target_pairs={{0,8},{8,0},{16,24},{24,16},{1,9},{9,1},{17,25},{25,17},{2,10},{10... | collective-permute-start | bytes 307208 | tf_op jit(solution)/shard_map/ppermute | solution.py:96
  169.6 5.3 %collective-permute-start.35 = (bf16[32,1600]{1,0:T(8,128)(2,1)S(1)}, bf16[32,1600]{1,0:T(8,128)(2,1)S(1)}, u32[]{:S(2)}, u32[]{:S(2)}) collective-permute-start(bf16[32,1600]{1,0:T(8,128)(2,1)S(1)} %collective-permute-done.33.refs_8_.refs_4_), channel_id=1, source_target_pairs={{0,4},{1,3},{2,6},{3,1},{4,0},{5,7},{6,2},{7,5},{8,12},{9,11},{10,... | collective-permute-start | bytes 307208 | tf_op jit(solution)/shard_map/ppermute | solution.py:96
  169.9 10.3 %collective-permute-start.43 = (bf16[32,1600]{1,0:T(8,128)(2,1)S(1)}, bf16[32,1600]{1,0:T(8,128)(2,1)S(1)}, u32[]{:S(2)}, u32[]{:S(2)}) collective-permute-start(bf16[32,1600]{1,0:T(8,128)(2,1)S(1)} %shard_map.154.refs_7_.refs_3_), channel_id=1, source_target_pairs={{0,16},{8,24},{16,0},{24,8},{1,17},{9,25},{17,1},{25,9},{2,18},{10... | collective-permute-start | bytes 307208 | tf_op jit(solution)/shard_map/ppermute | solution.py:96
  172.9 7.4 %collective-permute-start.44 = (bf16[32,1600]{1,0:T(8,128)(2,1)S(1)}, bf16[32,1600]{1,0:T(8,128)(2,1)S(1)}, u32[]{:S(2)}, u32[]{:S(2)}) collective-permute-start(bf16[32,1600]{1,0:T(8,128)(2,1)S(1)} %shard_map.154.refs_7_.refs_3_), channel_id=1, source_target_pairs={{0,24},{8,16},{16,8},{24,0},{1,25},{9,17},{17,9},{25,1},{2,26},{10... | collective-permute-start | bytes 307208 | tf_op jit(solution)/shard_map/ppermute | solution.py:96
  174.3 6.0 %collective-permute-start.37 = (bf16[32,1600]{1,0:T(8,128)(2,1)S(1)}, bf16[32,1600]{1,0:T(8,128)(2,1)S(1)}, u32[]{:S(2)}, u32[]{:S(2)}) collective-permute-start(bf16[32,1600]{1,0:T(8,128)(2,1)S(1)} %collective-permute-done.33.refs_8_.refs_4_), channel_id=1, source_target_pairs={{0,1},{1,0},{2,3},{3,2},{4,5},{5,4},{6,7},{7,6},{8,9},{9,8},{10,11... | collective-permute-start | bytes 307208 | tf_op jit(solution)/shard_map/ppermute | solution.py:96
  174.3 5.9 %collective-permute-start.38 = (bf16[32,1600]{1,0:T(8,128)(2,1)S(1)}, bf16[32,1600]{1,0:T(8,128)(2,1)S(1)}, u32[]{:S(2)}, u32[]{:S(2)}) collective-permute-start(bf16[32,1600]{1,0:T(8,128)(2,1)S(1)} %collective-permute-done.34.refs_9_.refs_5_), channel_id=1, source_target_pairs={{0,1},{1,0},{2,3},{3,2},{4,5},{5,4},{6,7},{7,6},{8,9},{9,8},{10,11... | collective-permute-start | bytes 307208 | tf_op jit(solution)/shard_map/ppermute | solution.py:96
  174.8 5.4 %collective-permute-start.39 = (bf16[32,1600]{1,0:T(8,128)(2,1)S(1)}, bf16[32,1600]{1,0:T(8,128)(2,1)S(1)}, u32[]{:S(2)}, u32[]{:S(2)}) collective-permute-start(bf16[32,1600]{1,0:T(8,128)(2,1)S(1)} %collective-permute-done.35.refs_10_.refs_6_), channel_id=1, source_target_pairs={{0,1},{1,0},{2,3},{3,2},{4,5},{5,4},{6,7},{7,6},{8,9},{9,8},{10,11... | collective-permute-start | bytes 307208 | tf_op jit(solution)/shard_map/ppermute | solution.py:96
  180.3 13.8 %collective-permute-start.45 = (bf16[3,32,1600]{2,1,0:T(8,128)(2,1)S(1)}, bf16[3,32,1600]{2,1,0:T(8,128)(2,1)S(1)}, u32[]{:S(2)}, u32[]{:S(2)}) collective-permute-start(bf16[3,32,1600]{2,1,0:T(8,128)(2,1)S(1)} %shard_map.157.refs_0_), channel_id=1, source_target_pairs={{0,2},{1,5},{2,0},{3,7},{4,6},{5,1},{6,4},{7,3},{8,10},{9,13},{10,... | collective-permute-start | bytes 921608 | tf_op jit(solution)/shard_map/ppermute | solution.py:96
  181.6 12.5 %collective-permute-start.46 = (bf16[3,32,1600]{2,1,0:T(8,128)(2,1)S(1)}, bf16[3,32,1600]{2,1,0:T(8,128)(2,1)S(1)}, u32[]{:S(2)}, u32[]{:S(2)}) collective-permute-start(bf16[3,32,1600]{2,1,0:T(8,128)(2,1)S(1)} %shard_map.157.refs_0_), channel_id=1, source_target_pairs={{0,4},{1,3},{2,6},{3,1},{4,0},{5,7},{6,2},{7,5},{8,12},{9,11},{10,... | collective-permute-start | bytes 921608 | tf_op jit(solution)/shard_map/ppermute | solution.py:96
  183.2 12.2 %collective-permute-start.47 = (bf16[3,32,1600]{2,1,0:T(8,128)(2,1)S(1)}, bf16[3,32,1600]{2,1,0:T(8,128)(2,1)S(1)}, u32[]{:S(2)}, u32[]{:S(2)}) collective-permute-start(bf16[3,32,1600]{2,1,0:T(8,128)(2,1)S(1)} %shard_map.157.refs_0_), channel_id=1, source_target_pairs={{0,6},{1,7},{2,4},{3,5},{4,2},{5,3},{6,0},{7,1},{8,14},{9,15},{10,... | collective-permute-start | bytes 921608 | tf_op jit(solution)/shard_map/ppermute | solution.py:96
  196.3 4.8 %collective-permute-start.48 = (bf16[4,3,32,1600]{3,2,1,0:T(8,128)(2,1)S(1)}, bf16[4,3,32,1600]{3,2,1,0:T(8,128)(2,1)S(1)}, u32[]{:S(2)}, u32[]{:S(2)}) collective-permute-start(bf16[4,3,32,1600]{3,2,1,0:T(8,128)(2,1)S(1)} %shard_map.158.refs_5_), channel_id=1, source_target_pairs={{0,1},{1,0},{2,3},{3,2},{4,5},{5,4},{6,7},{7,6},{8,9},{9,8},{10,11... | collective-permute-start | bytes 3686408 | tf_op jit(solution)/shard_map/ppermute | solution.py:96
  196.3 3.1 %collective-permute-start.40 = (f32[72,256]{1,0:T(8,128)S(1)}, f32[72,256]{1,0:T(8,128)S(1)}, u32[]{:S(2)}, u32[]{:S(2)}) collective-permute-start(f32[72,256]{1,0:T(8,128)S(1)} %get-tuple-element.62.refs_0_), channel_id=1, source_target_pairs={{0,1},{1,0},{2,3},{3,2},{4,5},{5,4},{6,7},{7,6},{8,9},{9,8},{10,11... | collective-permute-start | bytes 221192 | tf_op jit(solution)/shard_map/ppermute | solution.py:96
  200.4 6.4 %collective-permute-start.41 = (f32[72,256]{1,0:T(8,128)S(1)}, f32[72,256]{1,0:T(8,128)S(1)}, u32[]{:S(2)}, u32[]{:S(2)}) collective-permute-start(f32[72,256]{1,0:T(8,128)S(1)} %shard_map.156.refs_0_), channel_id=1, source_target_pairs={{0,2},{1,3},{2,0},{3,1},{4,6},{5,7},{6,4},{7,5},{8,10},{9,11},{10,... | collective-permute-start | bytes 221192 | tf_op jit(solution)/shard_map/ppermute | solution.py:96
  206.9 13.8 %collective-permute-start.49 = (f32[72,256]{1,0:T(8,128)S(1)}, f32[72,256]{1,0:T(8,128)S(1)}, u32[]{:S(2)}, u32[]{:S(2)}) collective-permute-start(f32[72,256]{1,0:T(8,128)S(1)} %shard_map.160.refs_0_), channel_id=1, source_target_pairs={{0,4},{1,5},{2,6},{3,7},{4,0},{5,1},{6,2},{7,3},{8,12},{9,13},{10,... | collective-permute-start | bytes 221192 | tf_op jit(solution)/shard_map/ppermute | solution.py:96
  214.8 11.3 %copy-start.8 = (bf16[960,256]{1,0:T(8,128)(2,1)S(1)}, bf16[960,256]{1,0:T(8,128)(2,1)}, u32[]{:S(2)}) copy-start(bf16[960,256]{1,0:T(8,128)(2,1)} %copy-done.6) | copy-start | bytes 1474564
  214.8 11.3 %copy-start.10 = (bf16[256,1600]{1,0:T(8,128)(2,1)S(1)}, bf16[256,1600]{1,0:T(8,128)(2,1)}, u32[]{:S(2)}) copy-start(bf16[256,1600]{1,0:T(8,128)(2,1)} %copy-done.9) | copy-start | bytes 2457604
  214.8 11.2 %copy-start.20 = (bf16[960,256]{1,0:T(8,128)(2,1)S(1)}, bf16[960,256]{1,0:T(8,128)(2,1)}, u32[]{:S(2)}) copy-start(bf16[960,256]{1,0:T(8,128)(2,1)} %copy-done.19) | copy-start | bytes 1474564
  220.7 11.6 %collective-permute-start.50 = (f32[72,256]{1,0:T(8,128)S(1)}, f32[72,256]{1,0:T(8,128)S(1)}, u32[]{:S(2)}, u32[]{:S(2)}) collective-permute-start(f32[72,256]{1,0:T(8,128)S(1)} %shard_map.162.refs_2_), channel_id=1, source_target_pairs={{0,8},{8,0},{16,24},{24,16},{1,9},{9,1},{17,25},{25,17},{2,10},{10... | collective-permute-start | bytes 221192 | tf_op jit(solution)/shard_map/ppermute | solution.py:96
  223.6 8.7 %collective-permute-start.51 = (f32[72,256]{1,0:T(8,128)S(1)}, f32[72,256]{1,0:T(8,128)S(1)}, u32[]{:S(2)}, u32[]{:S(2)}) collective-permute-start(f32[72,256]{1,0:T(8,128)S(1)} %shard_map.162.refs_2_), channel_id=1, source_target_pairs={{0,16},{8,24},{16,0},{24,8},{1,17},{9,25},{17,1},{25,9},{2,18},{10... | collective-permute-start | bytes 221192 | tf_op jit(solution)/shard_map/ppermute | solution.py:96
  224.5 7.8 %collective-permute-start.52 = (f32[72,256]{1,0:T(8,128)S(1)}, f32[72,256]{1,0:T(8,128)S(1)}, u32[]{:S(2)}, u32[]{:S(2)}) collective-permute-start(f32[72,256]{1,0:T(8,128)S(1)} %shard_map.162.refs_2_), channel_id=1, source_target_pairs={{0,24},{8,16},{16,8},{24,0},{1,25},{9,17},{17,9},{25,1},{2,26},{10... | collective-permute-start | bytes 221192 | tf_op jit(solution)/shard_map/ppermute | solution.py:96
  (16 other events, 38.1 us)
Sparse Core Ops, SparseCore 0:
  9.9 52.8 all-gather.3
  72.1 44.7 all-gather.5

commit v4 on v3

--- a/solution.py
+++ b/solution.py
@@ -115,9 +115,11 @@
 def spread(own, axis):
     size = lax.axis_size(axis)
     blocks = [own]
-    for key in far_keys(size) + [straight(1)]:
+    for at, key in enumerate(far_keys(size)):
+        if at:
+            blocks[0] = stack([own], blocks[1:])[0]
         blocks += [hop(block, axis, key) for block in blocks]
-    return blocks
+    return blocks + [hop(block, axis, straight(1)) for block in blocks]
 
 
 def holder(me, key):
@@ -345,19 +347,35 @@
         normed_ref[m] = rms_rows(rows).astype(BF16)
 
 
-def pool_kernel(resid_ref, keep_ref, got_ref, hidden_ref):
+def add_split_kernel(keep_ref, got_ref, *out_refs):
+    for at, out_ref in enumerate(out_refs):
+        out_ref[...] = keep_ref[at] + got_ref[at]
+
+
+def add_split(keep, got):
+    count, *rest = keep.shape
+    return launch(
+        add_split_kernel,
+        (keep, got),
+        [WHOLE] * 2,
+        out_shape=[shape_of(tuple(rest), F32)] * count,
+        out_specs=[WHOLE] * count,
+    )
+
+
+def pool_kernel(resid_ref, *refs):
     modules = resid_ref.shape[0]
     total = functools.reduce(jnp.add, [resid_ref[m] for m in range(modules)])
-    pooled = total * (1.0 / modules) + (keep_ref[0] + got_ref[0])
-    hidden_ref[...] = rms_rows(pooled).astype(BF16)
-
-
-def pool(resid, keep, got):
+    parts = functools.reduce(jnp.add, [ref[...] for ref in refs[:-1]])
+    refs[-1][...] = rms_rows(total * (1.0 / modules) + parts).astype(BF16)
+
+
+def pool(resid, parts):
     return launch(
         pool_kernel,
-        (resid, keep, got),
-        [WHOLE] * 3,
-        out_shape=shape_of(keep.shape[1:], BF16),
+        (resid, *parts),
+        [WHOLE] * (1 + len(parts)),
+        out_shape=shape_of(parts[0].shape, BF16),
         out_specs=WHOLE,
     )
 
@@ -507,15 +525,11 @@
     )
 
 
-def far_kernel(keys, other, norm, genes_all, place_ref, seen_ref, col_ref, wm_ref, wd_ref, *refs):
+def far_kernel(keys, norm, genes_all, place_ref, seen_ref, lib_ref, col_ref, wm_ref, wd_ref, *refs):
     hids = refs[:2]
     high_ref, low_ref, hid_ref, table_ref = refs[2:]
-    tile = wm_ref.shape[0]
-    genes = seen_ref.shape[1] - EXTRA
-    block = place_ref[1] ^ other
-    at = pl.ds(pl.multiple_of(pl.program_id(0) * tile, 16), tile)
-    seen = seen_ref[block, at, :].astype(F32)
-    lib = seen_ref[block, genes:, :].astype(F32)
+    seen = seen_ref[0].astype(F32)
+    lib = lib_ref[0].astype(F32)
     panel_count = wd_ref.shape[0]
 
     @pl.when(pl.program_id(0) == 0)
@@ -541,32 +555,41 @@
     panel_count = w_disp_t.shape[0]
     near, _, share, _ = hids[0].shape
     tile = tile_of(genes, 16, 256)
-    by_gene = lambda columns: pl.BlockSpec((tile, columns), lambda i: (i, 0))
-    return launch(
-        functools.partial(far_kernel, keys, other + 1, norm, genes_all),
-        (place, seen, panel_col, in_hbm(w_mean_t), w_disp_t, *hids),
-        [
-            SCALAR,
-            WHOLE,
-            by_gene(1),
-            by_gene(width),
-            fixed(panel_count, width),
-        ]
-        + [pl.BlockSpec((near, 1, share, width), lambda i: (0, other, 0, 0))] * len(hids),
-        grid=(genes // tile,),
+    by_gene = lambda columns: pl.BlockSpec((tile, columns), lambda i, at: (i, 0))
+    last = genes // EXTRA
+    return pl.pallas_call(
+        functools.partial(far_kernel, keys, norm, genes_all),
+        grid_spec=pltpu.PrefetchScalarGridSpec(
+            num_scalar_prefetch=1,
+            grid=(genes // tile,),
+            in_specs=[
+                pl.BlockSpec((1, tile, cells), lambda i, at: (at[1] ^ other, i, 0)),
+                pl.BlockSpec((1, EXTRA, cells), lambda i, at: (at[1] ^ other, last, 0)),
+                by_gene(1),
+                by_gene(width),
+                pl.BlockSpec((panel_count, width), lambda i, at: (0, 0)),
+            ]
+            + [pl.BlockSpec((near, 1, share, width), lambda i, at: (0, other - 1, 0, 0))]
+            * len(hids),
+            out_specs=[
+                by_gene(cells),
+                by_gene(cells),
+                pl.BlockSpec((cells, width), lambda i, at: (0, 0)),
+            ],
+            scratch_shapes=[pltpu.VMEM((3 * panel_count, cells), BF16)],
+        ),
         out_shape=(
             shape_of((genes, cells), BF16),
             shape_of((genes, cells), BF16),
             shape_of((cells, width), BF16),
         ),
-        out_specs=[by_gene(cells), by_gene(cells), fixed(cells, width)],
-        scratch_shapes=[pltpu.VMEM((3 * panel_count, cells), BF16)],
+        compiler_params=PARAMS,
         cost_estimate=pl.CostEstimate(
             flops=2 * genes * cells * width + 60 * genes * cells,
             bytes_accessed=genes * (width * 2 + cells * 6),
             transcendentals=4 * genes * cells,
         ),
-    )
+    )(place, seen, seen, panel_col, in_hbm(w_mean_t), w_disp_t, *hids)
 
 
 def grad_kernel(place_ref, *refs):
@@ -792,12 +815,12 @@
         spread(normed, "gene"), flat_cross, group_ids, across, heads, head_width, out_cross
     )
     got = hop(send, "gene", straight(1))
-    for key in far[::-1]:
-        keep, send = halve(keep, got, dtype=F32)
-        got = hop(send, "gene", key)
-    hidden = pool(mid, keep, got)
-
-    hids = spread(hidden, "gene")
+    parts = list(add_split(keep, got))
+    parts = parts[:1] + [hop(part, "gene", key) for part, key in zip(parts[1:], keys[1:])]
+    hidden = pool(mid, parts)
+
+    hids = [hidden] + [hop(hidden, "gene", key) for key in keys[1 : gene_count // 2]]
+    hids += [hop(block, "gene", straight(1)) for block in hids]
     far_hids = [stack([hop(hidden, "grp", straight(rel)) for rel in range(1, grp_count)], hids)]
     far_hids += [hop(far_hids[0], "gene", key) for key in keys[1 : gene_count // 2]]
     high, low, sums, own_hid = decode(
@@ -806,7 +829,7 @@
     groups = [(own_hid, high, low)]
     far_hids = [stack(far_hids, [high])]
     far_hids.append(hop(far_hids[0], "gene", straight(1)))
-    for other in range(grp_count - 1):
+    for other in range(1, grp_count):
         high, low, hid = far_call(
             place, keys, other, seen, panel_col, w_mean_t, w_disp_t, far_hids, norm, genes_all
         )

time: 245 us -> 244 us (level)
  waiting for transfers between devices: 87 us -> 83.8 us
    pallas_call x0 -> x3, Pallas kernels: none -> 17.3 us  [far_call(): pl.pallas_call(functools.partial(far_kernel, keys, norm, genes_all), grid...]
    pallas_call x27 -> x25, Pallas kernels: 72.3 us -> 55.4 us  [launch(): pl.pallas_call(body, in_specs=list(in_specs) + [ANYWHERE] * len(after), c...]
    ppermute x53 -> x54, waiting for transfers between devices: 86.9 us -> 83.8 us  [hop(): return lax.ppermute(value, axis, [(i, i ^ key[i & 1]) for i in range(size)])]
    ppermute x53 -> x54, starting transfers between devices: 45.3 us -> 47.5 us  [hop(): return lax.ppermute(value, axis, [(i, i ^ key[i & 1]) for i in range(size)])]
  transfers between devices with their start and end apart: 55 -> 56, of which waited for: 24 -> 28; matrix products, arithmetic and copies ran while one was open for 5% -> 5% of each run, Pallas kernels for 25% -> 25%
where the time goes in v4:
time: 244 us
  waiting for transfers between devices  83.8 us (34%)
  Pallas kernels  72.6 us (30%)
  starting transfers between devices  47.6 us (20%)
  local copies, waits for them, and re-layouts  24 us (10%)
  between operations  14.5 us (6%)
    ppermute x54, waiting for transfers between devices, hop(): return lax.ppermute(value, axis, [(i, i ^ key[i & 1]) for i in range(size)])  83.8 us
    pallas_call x25, Pallas kernels, launch(): pl.pallas_call(body, in_specs=list(in_specs) + [ANYWHERE] * len(after), c...  55.4 us
    ppermute x54, starting transfers between devices, hop(): return lax.ppermute(value, axis, [(i, i ^ key[i & 1]) for i in range(size)])  47.5 us
    pallas_call x3, Pallas kernels, far_call(): pl.pallas_call(functools.partial(far_kernel, keys, norm, genes_all), grid...  17.3 us
    unnamed x51, local copies, waits for them, and re-layouts  10.3 us
    reshape x2, local copies, waits for them, and re-layouts, flat_qkv(): return weights.transpose(2, 1, 0).reshape(-1, weights.shape[0])  8.55 us
  transfers between devices with their start and end apart: 56, of which 28 were waited for; matrix products, arithmetic and copies ran while one was open for 5% of the time, Pallas kernels for 25%

profile of v4, /device:TPU:0, one launch (start us, length us, event | category | flops | bytes accessed | tf_op | source)
XLA Modules:
  0.0 243.5 jit_solution(17154546222719829681)
XLA Ops:
  7.3 2.4 all_gather_reshape.3
  11.2 2.8 %collective-permute-start.1 = (f32[1,256]{1,0:T(1,128)S(1)}, f32[1,256]{1,0:T(1,128)S(1)}, u32[]{:S(2)}, u32[]{:S(2)}) collective-permute-start(f32[1,256]{1,0:T(1,128)S(1)} %add.19), channel_id=1, source_target_pairs={{0,2},{1,3},{2,0},{3,1},{4,6},{5,7},{6,4},{7,5},{8,10},{9,11},{10,... | collective-permute-start | bytes 3080 | tf_op jit(solution)/shard_map/ppermute | solution.py:96
  15.8 1.8 collective-permute-start.2
  18.4 1.1 collective-permute-done.2
  19.5 6.4 %shard_map.139 = (f32[128,3200]{1,0:T(8,128)S(1)}, f32[128,3200]{1,0:T(8,128)S(1)}) custom-call(s32[1]{0:T(128)} %bitcast.refs_0_, s32[960,256]{1,0:T(8,128)S(1)} %bitcast.33, f32[1,256]{1,0:T(1,128)S(1)} %get-tuple-element.79.refs_2_, bf16[960,6400]{1,0:T(8,128)(2,1)} %refs_3_.3, s32[128,1]{1,0:T(8,128)S(1)} %reshape_tile.12.refs_4_.refs_1_, ...), custom_call_target="tpu_custom_call" | custom-call | flops 1572864000 | bytes 9420800 | tf_op jit(solution)/shard_map/pallas_call | solution.py:43
  25.9 6.3 %shard_map.142 = (f32[128,3200]{1,0:T(8,128)S(1)}, f32[128,3200]{1,0:T(8,128)S(1)}) custom-call(s32[1]{0:T(128)} %bitcast.refs_0_, s32[960,256]{1,0:T(8,128)S(1)} %bitcast.34, f32[1,256]{1,0:T(1,128)S(1)} %get-tuple-element.79.refs_2_, bf16[960,6400]{1,0:T(8,128)(2,1)} %refs_3_.3), custom_call_target="tpu_custom_call" | custom-call | flops 1572864000 | bytes 9420800 | tf_op jit(solution)/shard_map/pallas_call | solution.py:43
  33.7 1.7 collective-permute-start.4
  37.7 1.7 collective-permute-start.7
  39.4 4.2 %reshape.78.refs_2_.refs_0_ = bf16[600,1600]{1,0:T(8,128)(2,1)} reshape(bf16[150,4,1600]{2,1,0:T(4,128)(2,1)} %bitcast.63) | data formatting | bytes 3840000 | tf_op jit(solution)/shard_map/reshape | solution.py:716
  43.6 4.3 %reshape.79.refs_2_.refs_0_ = bf16[600,1600]{1,0:T(8,128)(2,1)} reshape(bf16[150,4,1600]{2,1,0:T(4,128)(2,1)} %bitcast.64) | data formatting | bytes 3840000 | tf_op jit(solution)/shard_map/reshape | solution.py:716
  47.9 1.5 reshape.80.refs_3_.refs_11_
  49.6 1.7 copy-done.3
  51.2 1.1 shard_map.141
  52.4 1.9 collective-permute-start.5
  54.3 8.4 %collective-permute-done.7.refs_1_ = bf16[64,3200]{1,0:T(8,128)(2,1)} collective-permute-done((bf16[64,3200]{1,0:T(8,128)(2,1)}, bf16[64,3200]{1,0:T(8,128)(2,1)}, u32[]{:S(2)}, u32[]{:S(2)}) %collective-permute-start.7) | collective-permute-done | bytes 409632 | tf_op jit(solution)/shard_map/ppermute | solution.py:96
  62.8 1.1 shard_map.144
  63.9 1.7 collective-permute-start.8
  65.6 4.1 %collective-permute-done.8.refs_3_ = bf16[32,3200]{1,0:T(8,128)(2,1)S(1)} collective-permute-done((bf16[32,3200]{1,0:T(8,128)(2,1)S(1)}, bf16[32,3200]{1,0:T(8,128)(2,1)S(1)}, u32[]{:S(2)}, u32[]{:S(2)}) %collective-permute-start.8) | collective-permute-done | bytes 204832 | tf_op jit(solution)/shard_map/ppermute | solution.py:96
  73.1 1.7 collective-permute-start.9
  74.8 6.5 %collective-permute-done.9.refs_1_.refs_4_ = bf16[4,32,1600]{2,1,0:T(8,128)(2,1)S(1)} collective-permute-done((bf16[4,32,1600]{2,1,0:T(8,128)(2,1)S(1)}, bf16[4,32,1600]{2,1,0:T(8,128)(2,1)S(1)}, u32[]{:S(2)}, u32[]{:S(2)}) %collective-permute-start.9) | collective-permute-done | bytes 409632 | tf_op jit(solution)/shard_map/ppermute | solution.py:96
  81.3 1.0 collective-permute-start.10
  82.3 1.0 collective-permute-start.11
  83.9 5.6 %collective-permute-done.10.refs_5_ = bf16[4,32,1600]{2,1,0:T(8,128)(2,1)S(1)} collective-permute-done((bf16[4,32,1600]{2,1,0:T(8,128)(2,1)S(1)}, bf16[4,32,1600]{2,1,0:T(8,128)(2,1)S(1)}, u32[]{:S(2)}, u32[]{:S(2)}) %collective-permute-start.10) | collective-permute-done | bytes 409632 | tf_op jit(solution)/shard_map/ppermute | solution.py:96
  89.5 4.6 %collective-permute-done.11.refs_6_ = bf16[4,32,1600]{2,1,0:T(8,128)(2,1)S(1)} collective-permute-done((bf16[4,32,1600]{2,1,0:T(8,128)(2,1)S(1)}, bf16[4,32,1600]{2,1,0:T(8,128)(2,1)S(1)}, u32[]{:S(2)}, u32[]{:S(2)}) %collective-permute-start.11) | collective-permute-done | bytes 409632 | tf_op jit(solution)/shard_map/ppermute | solution.py:96
  94.1 1.7 collective-permute-done.15.refs_10_
  95.8 5.6 %shard_map.149.refs_3_ = bf16[8,128,200]{2,1,0:T(8,128)(2,1)S(1)} custom-call(bf16[600,1600]{1,0:T(8,128)(2,1)S(1)} %copy-done.4, s32[128,1]{1,0:T(8,128)S(1)} %reshape_tile.12.refs_4_.refs_1_, s32[1,128]{1,0:T(1,128)S(1)} %reshape_tile.11.refs_5_.refs_2_, bf16[4,32,1600]{2,1,0:T(8,128)(2,1)S(1)} %bitcast.51, ...), custom_call_target="tpu_custom_call" | custom-call | flops 2385510400 | bytes 5606400 | tf_op jit(solution)/shard_map/pallas_call | solution.py:43
  101.5 1.7 collective-permute-start.16
  105.0 1.1 collective-permute-start.20
  106.8 1.4 collective-permute-done.17.refs_5_
  108.2 1.2 collective-permute-start.22
  110.8 2.2 collective-permute-done.22.refs_10_
  113.0 3.8 %shard_map.150 = (f32[4,32,1600]{2,1,0:T(8,128)S(1)}, bf16[4,32,1600]{2,1,0:T(8,128)(2,1)S(1)}) custom-call(s32[1]{0:T(128)} %bitcast.refs_0_, bf16[8,200,1600]{2,1,0:T(8,128)(2,1)} %all-gather.4.cloned.1.call-done.refs_1_, f32[4,32,1600]{2,1,0:T(8,128)S(1)} %get-tuple-element.52.refs_2_, bf16[8,128,200]{2,1,0:T(8,128)(2,1)S(1)} %shard_map.149.refs_3_, ...), custom_call_target="tpu_custom_call" | custom-call | flops 655360000 | bytes 7577600 | tf_op jit(solution)/shard_map/pallas_call | solution.py:43
  119.6 8.1 %collective-permute-done.23.refs_1_.refs_4_ = bf16[4,32,1600]{2,1,0:T(8,128)(2,1)S(1)} collective-permute-done((bf16[4,32,1600]{2,1,0:T(8,128)(2,1)S(1)}, bf16[4,32,1600]{2,1,0:T(8,128)(2,1)S(1)}, u32[]{:S(2)}, u32[]{:S(2)}) %collective-permute-start.23) | collective-permute-done | bytes 409632 | tf_op jit(solution)/shard_map/ppermute | solution.py:96
  127.8 1.0 collective-permute-start.24
  128.8 1.0 collective-permute-start.25
  130.4 5.6 %collective-permute-done.24.refs_5_ = bf16[4,32,1600]{2,1,0:T(8,128)(2,1)S(1)} collective-permute-done((bf16[4,32,1600]{2,1,0:T(8,128)(2,1)S(1)}, bf16[4,32,1600]{2,1,0:T(8,128)(2,1)S(1)}, u32[]{:S(2)}, u32[]{:S(2)}) %collective-permute-start.24) | collective-permute-done | bytes 409632 | tf_op jit(solution)/shard_map/ppermute | solution.py:96
  136.0 4.6 %collective-permute-done.25.refs_6_ = bf16[4,32,1600]{2,1,0:T(8,128)(2,1)S(1)} collective-permute-done((bf16[4,32,1600]{2,1,0:T(8,128)(2,1)S(1)}, bf16[4,32,1600]{2,1,0:T(8,128)(2,1)S(1)}, u32[]{:S(2)}, u32[]{:S(2)}) %collective-permute-start.25) | collective-permute-done | bytes 409632 | tf_op jit(solution)/shard_map/ppermute | solution.py:96
  140.5 1.7 collective-permute-done.29.refs_10_
  142.3 6.3 %shard_map.153 = (f32[4,32,1600]{2,1,0:T(8,128)S(1)}, f32[4,32,1600]{2,1,0:T(8,128)S(1)}) custom-call(bf16[600,1600]{1,0:T(8,128)(2,1)S(1)} %copy-done.2, s32[256,1]{1,0:T(8,128)S(1)} %select_n.43.refs_6_.refs_1_, s32[1,256]{1,0:T(1,128)S(1)} %select_n.42.refs_7_.refs_2_, bf16[4,32,1600]{2,1,0:T(8,128)(2,1)S(1)} %bitcast.48, ...), custom_call_target="tpu_custom_call" | custom-call | flops 2804940800 | bytes 5606400 | tf_op jit(solution)/shard_map/pallas_call | solution.py:43
  148.8 2.2 collective-permute-done.30.refs_1_
  151.3 1.3 collective-permute-start.32
  152.6 2.1 collective-permute-start.33
  154.7 4.6 %collective-permute-done.31.refs_2_ = f32[32,1600]{1,0:T(8,128)S(1)} collective-permute-done((f32[32,1600]{1,0:T(8,128)S(1)}, f32[32,1600]{1,0:T(8,128)S(1)}, u32[]{:S(2)}, u32[]{:S(2)}) %collective-permute-start.31) | collective-permute-done | bytes 204832 | tf_op jit(solution)/shard_map/ppermute | solution.py:96
  159.4 4.9 %collective-permute-done.33.refs_4_ = f32[32,1600]{1,0:T(8,128)S(1)} collective-permute-done((f32[32,1600]{1,0:T(8,128)S(1)}, f32[32,1600]{1,0:T(8,128)S(1)}, u32[]{:S(2)}, u32[]{:S(2)}) %collective-permute-start.33) | collective-permute-done | bytes 204832 | tf_op jit(solution)/shard_map/ppermute | solution.py:96
  165.6 2.4 collective-permute-start.36
  168.2 2.1 collective-permute-done.34.refs_8_.refs_4_
  171.1 1.7 collective-permute-start.45
  173.4 1.1 collective-permute-done.43.refs_0_
  174.5 5.9 %collective-permute-done.44.refs_1_ = bf16[32,1600]{1,0:T(8,128)(2,1)S(1)} collective-permute-done((bf16[32,1600]{1,0:T(8,128)(2,1)S(1)}, bf16[32,1600]{1,0:T(8,128)(2,1)S(1)}, u32[]{:S(2)}, u32[]{:S(2)}) %collective-permute-start.44) | collective-permute-done | bytes 102432 | tf_op jit(solution)/shard_map/ppermute | solution.py:96
  181.1 1.3 collective-permute-start.47
  182.4 1.6 collective-permute-start.48
  184.1 9.5 %shard_map.156 = (bf16[960,256]{1,0:T(8,128)(2,1)S(1)}, bf16[960,256]{1,0:T(8,128)(2,1)S(1)}, f32[72,256]{1,0:T(8,128)S(1)}, bf16[256,1600]{1,0:T(8,128)(2,1)S(1)}) custom-call(s32[1]{0:T(128)} %bitcast.refs_0_, s32[960,256]{1,0:T(8,128)S(1)} %bitcast.36, s32[960,1]{1,0:T(8,128)S(1)} %copy.31.refs_8_.refs_2_.col_ref, ...), custom_call_target="tpu_custom_call" | custom-call | flops 823296000 | bytes 5038080 | tf_op jit(solution)/shard_map/pallas_call | solution.py:43
  194.5 1.5 collective-permute-done.48.refs_3_
  197.5 2.5 %collective-permute-done.41.refs_1_ = f32[72,256]{1,0:T(8,128)S(1)} collective-permute-done((f32[72,256]{1,0:T(8,128)S(1)}, f32[72,256]{1,0:T(8,128)S(1)}, u32[]{:S(2)}, u32[]{:S(2)}) %collective-permute-start.41) | collective-permute-done | bytes 73760 | tf_op jit(solution)/shard_map/ppermute | solution.py:96
  200.0 1.0 copy-done.7
  201.5 5.7 %shard_map.160 = (bf16[960,256]{1,0:T(8,128)(2,1)S(1)}, bf16[960,256]{1,0:T(8,128)(2,1)S(1)}, bf16[256,1600]{1,0:T(8,128)(2,1)S(1)}) custom-call(s32[2]{0:T(128)S(1)} %pad_add_fusion.place_ref.refs_0_, bf16[4,976,256]{2,1,0:T(8,128)(2,1)} %bitcast.53, bf16[4,976,256]{2,1,0:T(8,128)(2,1)} %bitcast.54, s32[960,1]{1,0:T(8,128)S(1)} %copy.31.refs_8_.refs_2_.col_ref, ...), custom_call_target="tpu_custom_call" | custom-call | flops 801177600 | bytes 4546560 | tf_op jit(solution)/shard_map/pallas_call | solution.py:560
  207.3 1.6 collective-permute-start.50
  209.0 5.8 %shard_map.164 = (bf16[960,256]{1,0:T(8,128)(2,1)S(1)}, bf16[960,256]{1,0:T(8,128)(2,1)S(1)}, bf16[256,1600]{1,0:T(8,128)(2,1)S(1)}) custom-call(s32[2]{0:T(128)S(1)} %pad_add_fusion.place_ref.refs_0_, bf16[4,976,256]{2,1,0:T(8,128)(2,1)} %bitcast.55, bf16[4,976,256]{2,1,0:T(8,128)(2,1)} %bitcast.56, s32[960,1]{1,0:T(8,128)S(1)} %copy.31.refs_8_.refs_2_.col_ref, ...), custom_call_target="tpu_custom_call" | custom-call | flops 801177600 | bytes 4546560 | tf_op jit(solution)/shard_map/pallas_call | solution.py:560
  214.8 5.8 %shard_map.162 = (bf16[960,256]{1,0:T(8,128)(2,1)S(1)}, bf16[960,256]{1,0:T(8,128)(2,1)S(1)}, bf16[256,1600]{1,0:T(8,128)(2,1)S(1)}) custom-call(s32[2]{0:T(128)S(1)} %pad_add_fusion.place_ref.refs_0_, bf16[4,976,256]{2,1,0:T(8,128)(2,1)} %bitcast.57, bf16[4,976,256]{2,1,0:T(8,128)(2,1)} %bitcast.58, s32[960,1]{1,0:T(8,128)S(1)} %copy.31.refs_8_.refs_2_.col_ref, ...), custom_call_target="tpu_custom_call" | custom-call | flops 801177600 | bytes 4546560 | tf_op jit(solution)/shard_map/pallas_call | solution.py:560
  220.5 2.1 collective-permute-start.51
  222.7 1.2 collective-permute-start.52
  223.9 1.4 collective-permute-start.53
  225.3 6.3 %shard_map.165.refs_10_ = f32[400,960]{1,0:T(8,128)} custom-call(s32[2]{0:T(128)S(1)} %pad_add_fusion.place_ref.refs_0_, bf16[256,1600]{1,0:T(8,128)(2,1)S(1)} %copy-done.12, bf16[960,256]{1,0:T(8,128)(2,1)S(1)} %copy-done.8, bf16[960,256]{1,0:T(8,128)(2,1)S(1)} %copy-done.20, bf16[256,1600]{1,0:T(8,128)(2,1)S(1)} %get-tuple-element.67.refs_4_.refs_7_, ...), custom_call_target="tpu_custom_call" | custom-call | flops 2883584000 | bytes 8744960 | tf_op jit(solution)/shard_map/pallas_call | solution.py:43
  231.5 5.1 %shard_map.166 = (f32[64,1600]{1,0:T(8,128)}, f32[1,256]{1,0:T(1,128)}) custom-call(s32[2]{0:T(128)S(1)} %pad_add_fusion.place_ref.refs_0_, bf16[64,1600]{1,0:T(8,128)(2,1)S(1)} %bitcast.41, f32[72,256]{1,0:T(8,128)S(1)} %shard_map.163.refs_2_, f32[72,256]{1,0:T(8,128)S(1)} %collective-permute-done.51.refs_3_, ...), custom_call_target="tpu_custom_call" | custom-call | tf_op jit(solution)/shard_map/pallas_call | solution.py:43
  (154 shorter events, 26.2 us)
Async XLA Ops:
  7.2 10.7 %copy-start.21 = (s32[960]{0:T(1024)S(1)}, s32[960]{0:T(1024)}, u32[]{:S(2)}) copy-start(s32[960]{0:T(1024)} %param.13) | copy-start | bytes 11524
  7.2 64.8 %all-gather.4.cloned.1.call-start = ((), (), s32[]{:S(2)}) async-start(), calls=%async_computation | async-start | bytes 5990400 | tf_op jit(solution)/shard_map/all_gather | solution.py:762
  9.7 108.8 %all-gather.6.cloned.1.call-start = ((), (), s32[]{:S(2)}) async-start(), calls=%async_computation.1 | async-start | bytes 2498560 | tf_op jit(solution)/shard_map/all_gather | solution.py:790
  9.9 1.3 collective-permute-start
  11.2 4.6 %collective-permute-start.1 = (f32[1,256]{1,0:T(1,128)S(1)}, f32[1,256]{1,0:T(1,128)S(1)}, u32[]{:S(2)}, u32[]{:S(2)}) collective-permute-start(f32[1,256]{1,0:T(1,128)S(1)} %add.19), channel_id=1, source_target_pairs={{0,2},{1,3},{2,0},{3,1},{4,6},{5,7},{6,4},{7,5},{8,10},{9,11},{10,... | collective-permute-start | bytes 3080 | tf_op jit(solution)/shard_map/ppermute | solution.py:96
  15.8 3.6 %collective-permute-start.2 = (f32[1,256]{1,0:T(1,128)S(1)}, f32[1,256]{1,0:T(1,128)S(1)}, u32[]{:S(2)}, u32[]{:S(2)}) collective-permute-start(f32[1,256]{1,0:T(1,128)S(1)} %add.20), channel_id=1, source_target_pairs={{0,4},{1,5},{2,6},{3,7},{4,0},{5,1},{6,2},{7,3},{8,12},{9,13},{10,... | collective-permute-start | bytes 3080 | tf_op jit(solution)/shard_map/ppermute | solution.py:96
  25.9 6.9 %collective-permute-start.3 = (f32[128,3200]{1,0:T(8,128)S(1)}, f32[128,3200]{1,0:T(8,128)S(1)}, u32[]{:S(2)}, u32[]{:S(2)}) collective-permute-start(f32[128,3200]{1,0:T(8,128)S(1)} %get-tuple-element.41), channel_id=1, source_target_pairs={{0,1},{1,0},{2,3},{3,2},{4,5},{5,4},{6,7},{7,6},{8,9},{9,8},{10,11... | collective-permute-start | bytes 4915208 | tf_op jit(solution)/shard_map/ppermute | solution.py:96
  32.2 3.7 %collective-permute-start.6 = (f32[128,3200]{1,0:T(8,128)S(1)}, f32[128,3200]{1,0:T(8,128)S(1)}, u32[]{:S(2)}, u32[]{:S(2)}) collective-permute-start(f32[128,3200]{1,0:T(8,128)S(1)} %get-tuple-element.47), channel_id=1, source_target_pairs={{0,1},{1,0},{2,3},{3,2},{4,5},{5,4},{6,7},{7,6},{8,9},{9,8},{10,11... | collective-permute-start | bytes 4915208 | tf_op jit(solution)/shard_map/ppermute | solution.py:96
  33.7 15.9 %collective-permute-start.4 = (bf16[64,3200]{1,0:T(8,128)(2,1)}, bf16[64,3200]{1,0:T(8,128)(2,1)}, u32[]{:S(2)}, u32[]{:S(2)}) collective-permute-start(bf16[64,3200]{1,0:T(8,128)(2,1)} %get-tuple-element.43), channel_id=1, source_target_pairs={{0,4},{1,3},{2,6},{3,1},{4,0},{5,7},{6,2},{7,5},{8,12},{9,11},{10,... | collective-permute-start | bytes 1228808 | tf_op jit(solution)/shard_map/ppermute | solution.py:96
  37.7 25.1 %collective-permute-start.7 = (bf16[64,3200]{1,0:T(8,128)(2,1)}, bf16[64,3200]{1,0:T(8,128)(2,1)}, u32[]{:S(2)}, u32[]{:S(2)}) collective-permute-start(bf16[64,3200]{1,0:T(8,128)(2,1)} %get-tuple-element.49), channel_id=1, source_target_pairs={{0,4},{1,3},{2,6},{3,1},{4,0},{5,7},{6,2},{7,5},{8,12},{9,11},{10,... | collective-permute-start | bytes 1228808 | tf_op jit(solution)/shard_map/ppermute | solution.py:96
  49.4 13.4 %copy-start.1 = (bf16[600,1600]{1,0:T(8,128)(2,1)S(1)}, bf16[600,1600]{1,0:T(8,128)(2,1)}, u32[]{:S(2)}) copy-start(bf16[600,1600]{1,0:T(8,128)(2,1)} %reshape.79.refs_2_.refs_0_) | copy-start | bytes 5760004
  51.2 11.5 %copy-start.14 = (f32[64,3200]{1,0:T(8,128)S(1)}, f32[64,3200]{1,0:T(8,128)}, u32[]{:S(2)}) copy-start(f32[64,3200]{1,0:T(8,128)} %copy-done.13) | copy-start | bytes 2457604
  52.4 13.2 %collective-permute-start.5 = (bf16[32,3200]{1,0:T(8,128)(2,1)S(1)}, bf16[32,3200]{1,0:T(8,128)(2,1)S(1)}, u32[]{:S(2)}, u32[]{:S(2)}) collective-permute-start(bf16[32,3200]{1,0:T(8,128)(2,1)S(1)} %get-tuple-element.45), channel_id=1, source_target_pairs={{0,2},{1,5},{2,0},{3,7},{4,6},{5,1},{6,4},{7,3},{8,10},{9,13},{10,... | collective-permute-start | bytes 614408 | tf_op jit(solution)/shard_map/ppermute | solution.py:96
  63.9 5.8 %collective-permute-start.8 = (bf16[32,3200]{1,0:T(8,128)(2,1)S(1)}, bf16[32,3200]{1,0:T(8,128)(2,1)S(1)}, u32[]{:S(2)}, u32[]{:S(2)}) collective-permute-start(bf16[32,3200]{1,0:T(8,128)(2,1)S(1)} %get-tuple-element.51), channel_id=1, source_target_pairs={{0,2},{1,5},{2,0},{3,7},{4,6},{5,1},{6,4},{7,3},{8,10},{9,13},{10,... | collective-permute-start | bytes 614408 | tf_op jit(solution)/shard_map/ppermute | solution.py:96
  73.0 22.8 %copy-start.4 = (bf16[600,1600]{1,0:T(8,128)(2,1)S(1)}, bf16[600,1600]{1,0:T(8,128)(2,1)}, u32[]{:S(2)}) copy-start(bf16[600,1600]{1,0:T(8,128)(2,1)} %reshape.78.refs_2_.refs_0_) | copy-start | bytes 5760004
  73.1 8.2 %collective-permute-start.9 = (bf16[4,32,1600]{2,1,0:T(8,128)(2,1)S(1)}, bf16[4,32,1600]{2,1,0:T(8,128)(2,1)S(1)}, u32[]{:S(2)}, u32[]{:S(2)}) collective-permute-start(bf16[4,32,1600]{2,1,0:T(8,128)(2,1)S(1)} %bitcast.42), channel_id=1, source_target_pairs={{0,2},{1,5},{2,0},{3,7},{4,6},{5,1},{6,4},{7,3},{8,10},{9,13},{10,... | collective-permute-start | bytes 1228808 | tf_op jit(solution)/shard_map/ppermute | solution.py:96
  81.3 8.2 %collective-permute-start.10 = (bf16[4,32,1600]{2,1,0:T(8,128)(2,1)S(1)}, bf16[4,32,1600]{2,1,0:T(8,128)(2,1)S(1)}, u32[]{:S(2)}, u32[]{:S(2)}) collective-permute-start(bf16[4,32,1600]{2,1,0:T(8,128)(2,1)S(1)} %bitcast.49), channel_id=1, source_target_pairs={{0,4},{1,3},{2,6},{3,1},{4,0},{5,7},{6,2},{7,5},{8,12},{9,11},{10,... | collective-permute-start | bytes 1228808 | tf_op jit(solution)/shard_map/ppermute | solution.py:96
  82.3 11.7 %collective-permute-start.11 = (bf16[4,32,1600]{2,1,0:T(8,128)(2,1)S(1)}, bf16[4,32,1600]{2,1,0:T(8,128)(2,1)S(1)}, u32[]{:S(2)}, u32[]{:S(2)}) collective-permute-start(bf16[4,32,1600]{2,1,0:T(8,128)(2,1)S(1)} %collective-permute-done.9.refs_1_.refs_4_), channel_id=1, source_target_pairs={{0,4},{1,3},{2,6},{3,1},{4,0},{5,7},{6,2},{7,5},{8,12},{9,11},{10,... | collective-permute-start | bytes 1228808 | tf_op jit(solution)/shard_map/ppermute | solution.py:96
  83.4 10.7 %collective-permute-start.12 = (bf16[4,32,1600]{2,1,0:T(8,128)(2,1)S(1)}, bf16[4,32,1600]{2,1,0:T(8,128)(2,1)S(1)}, u32[]{:S(2)}, u32[]{:S(2)}) collective-permute-start(bf16[4,32,1600]{2,1,0:T(8,128)(2,1)S(1)} %bitcast.50), channel_id=1, source_target_pairs={{0,1},{1,0},{2,3},{3,2},{4,5},{5,4},{6,7},{7,6},{8,9},{9,8},{10,11... | collective-permute-start | bytes 1228808 | tf_op jit(solution)/shard_map/ppermute | solution.py:96
  83.4 10.7 %collective-permute-start.13 = (bf16[4,32,1600]{2,1,0:T(8,128)(2,1)S(1)}, bf16[4,32,1600]{2,1,0:T(8,128)(2,1)S(1)}, u32[]{:S(2)}, u32[]{:S(2)}) collective-permute-start(bf16[4,32,1600]{2,1,0:T(8,128)(2,1)S(1)} %collective-permute-done.9.refs_1_.refs_4_), channel_id=1, source_target_pairs={{0,1},{1,0},{2,3},{3,2},{4,5},{5,4},{6,7},{7,6},{8,9},{9,8},{10,11... | collective-permute-start | bytes 1228808 | tf_op jit(solution)/shard_map/ppermute | solution.py:96
  89.5 4.6 %collective-permute-start.14 = (bf16[4,32,1600]{2,1,0:T(8,128)(2,1)S(1)}, bf16[4,32,1600]{2,1,0:T(8,128)(2,1)S(1)}, u32[]{:S(2)}, u32[]{:S(2)}) collective-permute-start(bf16[4,32,1600]{2,1,0:T(8,128)(2,1)S(1)} %collective-permute-done.10.refs_5_), channel_id=1, source_target_pairs={{0,1},{1,0},{2,3},{3,2},{4,5},{5,4},{6,7},{7,6},{8,9},{9,8},{10,11... | collective-permute-start | bytes 1228808 | tf_op jit(solution)/shard_map/ppermute | solution.py:96
  94.1 1.8 collective-permute-start.15
  101.5 4.9 %collective-permute-start.16 = (bf16[128,200]{1,0:T(8,128)(2,1)S(1)}, bf16[128,200]{1,0:T(8,128)(2,1)S(1)}, u32[]{:S(2)}, u32[]{:S(2)}) collective-permute-start(bf16[128,200]{1,0:T(8,128)(2,1)S(1)} %get-tuple-element.87), channel_id=1, source_target_pairs={{0,2},{1,5},{2,0},{3,7},{4,6},{5,1},{6,4},{7,3},{8,10},{9,13},{10,... | collective-permute-start | bytes 153608 | tf_op jit(solution)/shard_map/ppermute | solution.py:96
  103.2 5.0 %collective-permute-start.17 = (bf16[128,200]{1,0:T(8,128)(2,1)S(1)}, bf16[128,200]{1,0:T(8,128)(2,1)S(1)}, u32[]{:S(2)}, u32[]{:S(2)}) collective-permute-start(bf16[128,200]{1,0:T(8,128)(2,1)S(1)} %get-tuple-element.86), channel_id=1, source_target_pairs={{0,4},{1,3},{2,6},{3,1},{4,0},{5,7},{6,2},{7,5},{8,12},{9,11},{10,... | collective-permute-start | bytes 153608 | tf_op jit(solution)/shard_map/ppermute | solution.py:96
  104.2 5.8 %collective-permute-start.18 = (bf16[128,200]{1,0:T(8,128)(2,1)S(1)}, bf16[128,200]{1,0:T(8,128)(2,1)S(1)}, u32[]{:S(2)}, u32[]{:S(2)}) collective-permute-start(bf16[128,200]{1,0:T(8,128)(2,1)S(1)} %get-tuple-element.85), channel_id=1, source_target_pairs={{0,6},{1,7},{2,4},{3,5},{4,2},{5,3},{6,0},{7,1},{8,14},{9,15},{10,... | collective-permute-start | bytes 153608 | tf_op jit(solution)/shard_map/ppermute | solution.py:96
  105.0 5.0 %collective-permute-start.19 = (bf16[128,200]{1,0:T(8,128)(2,1)S(1)}, bf16[128,200]{1,0:T(8,128)(2,1)S(1)}, u32[]{:S(2)}, u32[]{:S(2)}) collective-permute-start(bf16[128,200]{1,0:T(8,128)(2,1)S(1)} %get-tuple-element.84), channel_id=1, source_target_pairs={{0,1},{1,0},{2,3},{3,2},{4,5},{5,4},{6,7},{7,6},{8,9},{9,8},{10,11... | collective-permute-start | bytes 153608 | tf_op jit(solution)/shard_map/ppermute | solution.py:96
  105.0 5.0 %collective-permute-start.20 = (bf16[128,200]{1,0:T(8,128)(2,1)S(1)}, bf16[128,200]{1,0:T(8,128)(2,1)S(1)}, u32[]{:S(2)}, u32[]{:S(2)}) collective-permute-start(bf16[128,200]{1,0:T(8,128)(2,1)S(1)} %get-tuple-element.83), channel_id=1, source_target_pairs={{0,5},{1,2},{2,7},{3,0},{4,1},{5,6},{6,3},{7,4},{8,13},{9,10},{10,... | collective-permute-start | bytes 153608 | tf_op jit(solution)/shard_map/ppermute | solution.py:96
  106.4 4.4 %collective-permute-start.21 = (bf16[128,200]{1,0:T(8,128)(2,1)S(1)}, bf16[128,200]{1,0:T(8,128)(2,1)S(1)}, u32[]{:S(2)}, u32[]{:S(2)}) collective-permute-start(bf16[128,200]{1,0:T(8,128)(2,1)S(1)} %get-tuple-element.82), channel_id=1, source_target_pairs={{0,3},{1,4},{2,1},{3,6},{4,7},{5,0},{6,5},{7,2},{8,11},{9,12},{10,... | collective-permute-start | bytes 153608 | tf_op jit(solution)/shard_map/ppermute | solution.py:96
  108.2 4.8 %collective-permute-start.22 = (bf16[128,200]{1,0:T(8,128)(2,1)S(1)}, bf16[128,200]{1,0:T(8,128)(2,1)S(1)}, u32[]{:S(2)}, u32[]{:S(2)}) collective-permute-start(bf16[128,200]{1,0:T(8,128)(2,1)S(1)} %get-tuple-element.81), channel_id=1, source_target_pairs={{0,7},{1,6},{2,5},{3,4},{4,3},{5,2},{6,1},{7,0},{8,15},{9,14},{10,... | collective-permute-start | bytes 153608 | tf_op jit(solution)/shard_map/ppermute | solution.py:96
  119.5 22.8 %copy-start.2 = (bf16[600,1600]{1,0:T(8,128)(2,1)S(1)}, bf16[600,1600]{1,0:T(8,128)(2,1)}, u32[]{:S(2)}) copy-start(bf16[600,1600]{1,0:T(8,128)(2,1)} %reshape.79.refs_2_.refs_0_) | copy-start | bytes 5760004
  119.5 8.2 %collective-permute-start.23 = (bf16[4,32,1600]{2,1,0:T(8,128)(2,1)S(1)}, bf16[4,32,1600]{2,1,0:T(8,128)(2,1)S(1)}, u32[]{:S(2)}, u32[]{:S(2)}) collective-permute-start(bf16[4,32,1600]{2,1,0:T(8,128)(2,1)S(1)} %bitcast.44), channel_id=1, source_target_pairs={{0,2},{1,5},{2,0},{3,7},{4,6},{5,1},{6,4},{7,3},{8,10},{9,13},{10,... | collective-permute-start | bytes 1228808 | tf_op jit(solution)/shard_map/ppermute | solution.py:96
  127.8 8.2 %collective-permute-start.24 = (bf16[4,32,1600]{2,1,0:T(8,128)(2,1)S(1)}, bf16[4,32,1600]{2,1,0:T(8,128)(2,1)S(1)}, u32[]{:S(2)}, u32[]{:S(2)}) collective-permute-start(bf16[4,32,1600]{2,1,0:T(8,128)(2,1)S(1)} %bitcast.46), channel_id=1, source_target_pairs={{0,4},{1,3},{2,6},{3,1},{4,0},{5,7},{6,2},{7,5},{8,12},{9,11},{10,... | collective-permute-start | bytes 1228808 | tf_op jit(solution)/shard_map/ppermute | solution.py:96
  128.8 11.7 %collective-permute-start.25 = (bf16[4,32,1600]{2,1,0:T(8,128)(2,1)S(1)}, bf16[4,32,1600]{2,1,0:T(8,128)(2,1)S(1)}, u32[]{:S(2)}, u32[]{:S(2)}) collective-permute-start(bf16[4,32,1600]{2,1,0:T(8,128)(2,1)S(1)} %collective-permute-done.23.refs_1_.refs_4_), channel_id=1, source_target_pairs={{0,4},{1,3},{2,6},{3,1},{4,0},{5,7},{6,2},{7,5},{8,12},{9,11},{10,... | collective-permute-start | bytes 1228808 | tf_op jit(solution)/shard_map/ppermute | solution.py:96
  129.9 10.7 %collective-permute-start.26 = (bf16[4,32,1600]{2,1,0:T(8,128)(2,1)S(1)}, bf16[4,32,1600]{2,1,0:T(8,128)(2,1)S(1)}, u32[]{:S(2)}, u32[]{:S(2)}) collective-permute-start(bf16[4,32,1600]{2,1,0:T(8,128)(2,1)S(1)} %bitcast.47), channel_id=1, source_target_pairs={{0,1},{1,0},{2,3},{3,2},{4,5},{5,4},{6,7},{7,6},{8,9},{9,8},{10,11... | collective-permute-start | bytes 1228808 | tf_op jit(solution)/shard_map/ppermute | solution.py:96
  129.9 10.7 %collective-permute-start.27 = (bf16[4,32,1600]{2,1,0:T(8,128)(2,1)S(1)}, bf16[4,32,1600]{2,1,0:T(8,128)(2,1)S(1)}, u32[]{:S(2)}, u32[]{:S(2)}) collective-permute-start(bf16[4,32,1600]{2,1,0:T(8,128)(2,1)S(1)} %collective-permute-done.23.refs_1_.refs_4_), channel_id=1, source_target_pairs={{0,1},{1,0},{2,3},{3,2},{4,5},{5,4},{6,7},{7,6},{8,9},{9,8},{10,11... | collective-permute-start | bytes 1228808 | tf_op jit(solution)/shard_map/ppermute | solution.py:96
  136.0 4.6 %collective-permute-start.28 = (bf16[4,32,1600]{2,1,0:T(8,128)(2,1)S(1)}, bf16[4,32,1600]{2,1,0:T(8,128)(2,1)S(1)}, u32[]{:S(2)}, u32[]{:S(2)}) collective-permute-start(bf16[4,32,1600]{2,1,0:T(8,128)(2,1)S(1)} %collective-permute-done.24.refs_5_), channel_id=1, source_target_pairs={{0,1},{1,0},{2,3},{3,2},{4,5},{5,4},{6,7},{7,6},{8,9},{9,8},{10,11... | collective-permute-start | bytes 1228808 | tf_op jit(solution)/shard_map/ppermute | solution.py:96
  140.5 1.8 collective-permute-start.29
  148.6 15.7 %copy-start.10 = (f32[4,32,1600]{2,1,0:T(8,128)S(1)}, f32[4,32,1600]{2,1,0:T(8,128)}, u32[]{:S(2)}) copy-start(f32[4,32,1600]{2,1,0:T(8,128)} %copy-done.9) | copy-start | bytes 2457604
  148.6 2.4 %collective-permute-start.30 = (f32[4,32,1600]{2,1,0:T(8,128)S(1)}, f32[4,32,1600]{2,1,0:T(8,128)S(1)}, u32[]{:S(2)}, u32[]{:S(2)}) collective-permute-start(f32[4,32,1600]{2,1,0:T(8,128)S(1)} %get-tuple-element.57), channel_id=1, source_target_pairs={{0,1},{1,0},{2,3},{3,2},{4,5},{5,4},{6,7},{7,6},{8,9},{9,8},{10,11... | collective-permute-start | bytes 2457608 | tf_op jit(solution)/shard_map/ppermute | solution.py:96
  151.2 8.2 %collective-permute-start.31 = (f32[32,1600]{1,0:T(8,128)S(1)}, f32[32,1600]{1,0:T(8,128)S(1)}, u32[]{:S(2)}, u32[]{:S(2)}) collective-permute-start(f32[32,1600]{1,0:T(8,128)S(1)} %get-tuple-element.59), channel_id=1, source_target_pairs={{0,2},{1,5},{2,0},{3,7},{4,6},{5,1},{6,4},{7,3},{8,10},{9,13},{10,... | collective-permute-start | bytes 614408 | tf_op jit(solution)/shard_map/ppermute | solution.py:96
  151.3 8.1 %collective-permute-start.32 = (f32[32,1600]{1,0:T(8,128)S(1)}, f32[32,1600]{1,0:T(8,128)S(1)}, u32[]{:S(2)}, u32[]{:S(2)}) collective-permute-start(f32[32,1600]{1,0:T(8,128)S(1)} %get-tuple-element.60), channel_id=1, source_target_pairs={{0,4},{1,3},{2,6},{3,1},{4,0},{5,7},{6,2},{7,5},{8,12},{9,11},{10,... | collective-permute-start | bytes 614408 | tf_op jit(solution)/shard_map/ppermute | solution.py:96
  152.6 11.7 %collective-permute-start.33 = (f32[32,1600]{1,0:T(8,128)S(1)}, f32[32,1600]{1,0:T(8,128)S(1)}, u32[]{:S(2)}, u32[]{:S(2)}) collective-permute-start(f32[32,1600]{1,0:T(8,128)S(1)} %get-tuple-element.61), channel_id=1, source_target_pairs={{0,6},{1,7},{2,4},{3,5},{4,2},{5,3},{6,0},{7,1},{8,14},{9,15},{10,... | collective-permute-start | bytes 614408 | tf_op jit(solution)/shard_map/ppermute | solution.py:96
  164.3 19.8 %copy-start.5 = (bf16[1600,64]{0,1:T(8,128)(2,1)S(1)}, bf16[1600,64]{0,1:T(8,128)(2,1)}, u32[]{:S(2)}) copy-start(bf16[1600,64]{0,1:T(8,128)(2,1)} %param.21) | copy-start | bytes 614404
  164.4 5.9 %collective-permute-start.34 = (bf16[32,1600]{1,0:T(8,128)(2,1)S(1)}, bf16[32,1600]{1,0:T(8,128)(2,1)S(1)}, u32[]{:S(2)}, u32[]{:S(2)}) collective-permute-start(bf16[32,1600]{1,0:T(8,128)(2,1)S(1)} %shard_map.155.refs_7_.refs_3_), channel_id=1, source_target_pairs={{0,2},{1,5},{2,0},{3,7},{4,6},{5,1},{6,4},{7,3},{8,10},{9,13},{10,... | collective-permute-start | bytes 307208 | tf_op jit(solution)/shard_map/ppermute | solution.py:96
  164.8 6.3 %collective-permute-start.35 = (bf16[32,1600]{1,0:T(8,128)(2,1)S(1)}, bf16[32,1600]{1,0:T(8,128)(2,1)S(1)}, u32[]{:S(2)}, u32[]{:S(2)}) collective-permute-start(bf16[32,1600]{1,0:T(8,128)(2,1)S(1)} %shard_map.155.refs_7_.refs_3_), channel_id=1, source_target_pairs={{0,4},{1,3},{2,6},{3,1},{4,0},{5,7},{6,2},{7,5},{8,12},{9,11},{10,... | collective-permute-start | bytes 307208 | tf_op jit(solution)/shard_map/ppermute | solution.py:96
  165.6 7.3 %collective-permute-start.36 = (bf16[32,1600]{1,0:T(8,128)(2,1)S(1)}, bf16[32,1600]{1,0:T(8,128)(2,1)S(1)}, u32[]{:S(2)}, u32[]{:S(2)}) collective-permute-start(bf16[32,1600]{1,0:T(8,128)(2,1)S(1)} %shard_map.155.refs_7_.refs_3_), channel_id=1, source_target_pairs={{0,6},{1,7},{2,4},{3,5},{4,2},{5,3},{6,0},{7,1},{8,14},{9,15},{10,... | collective-permute-start | bytes 307208 | tf_op jit(solution)/shard_map/ppermute | solution.py:96
  168.0 4.9 %collective-permute-start.37 = (bf16[32,1600]{1,0:T(8,128)(2,1)S(1)}, bf16[32,1600]{1,0:T(8,128)(2,1)S(1)}, u32[]{:S(2)}, u32[]{:S(2)}) collective-permute-start(bf16[32,1600]{1,0:T(8,128)(2,1)S(1)} %shard_map.155.refs_7_.refs_3_), channel_id=1, source_target_pairs={{0,1},{1,0},{2,3},{3,2},{4,5},{5,4},{6,7},{7,6},{8,9},{9,8},{10,11... | collective-permute-start | bytes 307208 | tf_op jit(solution)/shard_map/ppermute | solution.py:96
  168.0 6.5 %collective-permute-start.43 = (bf16[32,1600]{1,0:T(8,128)(2,1)S(1)}, bf16[32,1600]{1,0:T(8,128)(2,1)S(1)}, u32[]{:S(2)}, u32[]{:S(2)}) collective-permute-start(bf16[32,1600]{1,0:T(8,128)(2,1)S(1)} %shard_map.155.refs_7_.refs_3_), channel_id=1, source_target_pairs={{0,8},{8,0},{16,24},{24,16},{1,9},{9,1},{17,25},{25,17},{2,10},{10... | collective-permute-start | bytes 307208 | tf_op jit(solution)/shard_map/ppermute | solution.py:96
  170.3 10.1 %collective-permute-start.44 = (bf16[32,1600]{1,0:T(8,128)(2,1)S(1)}, bf16[32,1600]{1,0:T(8,128)(2,1)S(1)}, u32[]{:S(2)}, u32[]{:S(2)}) collective-permute-start(bf16[32,1600]{1,0:T(8,128)(2,1)S(1)} %shard_map.155.refs_7_.refs_3_), channel_id=1, source_target_pairs={{0,16},{8,24},{16,0},{24,8},{1,17},{9,25},{17,1},{25,9},{2,18},{10... | collective-permute-start | bytes 307208 | tf_op jit(solution)/shard_map/ppermute | solution.py:96
  171.1 9.4 %collective-permute-start.45 = (bf16[32,1600]{1,0:T(8,128)(2,1)S(1)}, bf16[32,1600]{1,0:T(8,128)(2,1)S(1)}, u32[]{:S(2)}, u32[]{:S(2)}) collective-permute-start(bf16[32,1600]{1,0:T(8,128)(2,1)S(1)} %shard_map.155.refs_7_.refs_3_), channel_id=1, source_target_pairs={{0,24},{8,16},{16,8},{24,0},{1,25},{9,17},{17,9},{25,1},{2,26},{10... | collective-permute-start | bytes 307208 | tf_op jit(solution)/shard_map/ppermute | solution.py:96
  172.9 7.6 %collective-permute-start.38 = (bf16[32,1600]{1,0:T(8,128)(2,1)S(1)}, bf16[32,1600]{1,0:T(8,128)(2,1)S(1)}, u32[]{:S(2)}, u32[]{:S(2)}) collective-permute-start(bf16[32,1600]{1,0:T(8,128)(2,1)S(1)} %collective-permute-done.34.refs_8_.refs_4_), channel_id=1, source_target_pairs={{0,1},{1,0},{2,3},{3,2},{4,5},{5,4},{6,7},{7,6},{8,9},{9,8},{10,11... | collective-permute-start | bytes 307208 | tf_op jit(solution)/shard_map/ppermute | solution.py:96
  172.9 7.6 %collective-permute-start.39 = (bf16[32,1600]{1,0:T(8,128)(2,1)S(1)}, bf16[32,1600]{1,0:T(8,128)(2,1)S(1)}, u32[]{:S(2)}, u32[]{:S(2)}) collective-permute-start(bf16[32,1600]{1,0:T(8,128)(2,1)S(1)} %collective-permute-done.35.refs_9_.refs_5_), channel_id=1, source_target_pairs={{0,1},{1,0},{2,3},{3,2},{4,5},{5,4},{6,7},{7,6},{8,9},{9,8},{10,11... | collective-permute-start | bytes 307208 | tf_op jit(solution)/shard_map/ppermute | solution.py:96
  174.5 6.0 %collective-permute-start.40 = (bf16[32,1600]{1,0:T(8,128)(2,1)S(1)}, bf16[32,1600]{1,0:T(8,128)(2,1)S(1)}, u32[]{:S(2)}, u32[]{:S(2)}) collective-permute-start(bf16[32,1600]{1,0:T(8,128)(2,1)S(1)} %collective-permute-done.36.refs_10_.refs_6_), channel_id=1, source_target_pairs={{0,1},{1,0},{2,3},{3,2},{4,5},{5,4},{6,7},{7,6},{8,9},{9,8},{10,11... | collective-permute-start | bytes 307208 | tf_op jit(solution)/shard_map/ppermute | solution.py:96
  180.5 14.0 %collective-permute-start.46 = (bf16[3,32,1600]{2,1,0:T(8,128)(2,1)S(1)}, bf16[3,32,1600]{2,1,0:T(8,128)(2,1)S(1)}, u32[]{:S(2)}, u32[]{:S(2)}) collective-permute-start(bf16[3,32,1600]{2,1,0:T(8,128)(2,1)S(1)} %shard_map.158.refs_0_), channel_id=1, source_target_pairs={{0,2},{1,5},{2,0},{3,7},{4,6},{5,1},{6,4},{7,3},{8,10},{9,13},{10,... | collective-permute-start | bytes 921608 | tf_op jit(solution)/shard_map/ppermute | solution.py:96
  181.1 13.4 %collective-permute-start.47 = (bf16[3,32,1600]{2,1,0:T(8,128)(2,1)S(1)}, bf16[3,32,1600]{2,1,0:T(8,128)(2,1)S(1)}, u32[]{:S(2)}, u32[]{:S(2)}) collective-permute-start(bf16[3,32,1600]{2,1,0:T(8,128)(2,1)S(1)} %shard_map.158.refs_0_), channel_id=1, source_target_pairs={{0,4},{1,3},{2,6},{3,1},{4,0},{5,7},{6,2},{7,5},{8,12},{9,11},{10,... | collective-permute-start | bytes 921608 | tf_op jit(solution)/shard_map/ppermute | solution.py:96
  182.4 13.6 %collective-permute-start.48 = (bf16[3,32,1600]{2,1,0:T(8,128)(2,1)S(1)}, bf16[3,32,1600]{2,1,0:T(8,128)(2,1)S(1)}, u32[]{:S(2)}, u32[]{:S(2)}) collective-permute-start(bf16[3,32,1600]{2,1,0:T(8,128)(2,1)S(1)} %shard_map.158.refs_0_), channel_id=1, source_target_pairs={{0,6},{1,7},{2,4},{3,5},{4,2},{5,3},{6,0},{7,1},{8,14},{9,15},{10,... | collective-permute-start | bytes 921608 | tf_op jit(solution)/shard_map/ppermute | solution.py:96
  196.9 4.6 %collective-permute-start.49 = (bf16[4,3,32,1600]{3,2,1,0:T(8,128)(2,1)S(1)}, bf16[4,3,32,1600]{3,2,1,0:T(8,128)(2,1)S(1)}, u32[]{:S(2)}, u32[]{:S(2)}) collective-permute-start(bf16[4,3,32,1600]{3,2,1,0:T(8,128)(2,1)S(1)} %shard_map.159.refs_0_), channel_id=1, source_target_pairs={{0,1},{1,0},{2,3},{3,2},{4,5},{5,4},{6,7},{7,6},{8,9},{9,8},{10,11... | collective-permute-start | bytes 3686408 | tf_op jit(solution)/shard_map/ppermute | solution.py:96
  196.9 3.1 %collective-permute-start.41 = (f32[72,256]{1,0:T(8,128)S(1)}, f32[72,256]{1,0:T(8,128)S(1)}, u32[]{:S(2)}, u32[]{:S(2)}) collective-permute-start(f32[72,256]{1,0:T(8,128)S(1)} %get-tuple-element.62.refs_0_), channel_id=1, source_target_pairs={{0,1},{1,0},{2,3},{3,2},{4,5},{5,4},{6,7},{7,6},{8,9},{9,8},{10,11... | collective-permute-start | bytes 221192 | tf_op jit(solution)/shard_map/ppermute | solution.py:96
  201.1 6.2 %collective-permute-start.42 = (f32[72,256]{1,0:T(8,128)S(1)}, f32[72,256]{1,0:T(8,128)S(1)}, u32[]{:S(2)}, u32[]{:S(2)}) collective-permute-start(f32[72,256]{1,0:T(8,128)S(1)} %shard_map.157.refs_0_), channel_id=1, source_target_pairs={{0,2},{1,3},{2,0},{3,1},{4,6},{5,7},{6,4},{7,5},{8,10},{9,11},{10,... | collective-permute-start | bytes 221192 | tf_op jit(solution)/shard_map/ppermute | solution.py:96
  207.3 13.2 %collective-permute-start.50 = (f32[72,256]{1,0:T(8,128)S(1)}, f32[72,256]{1,0:T(8,128)S(1)}, u32[]{:S(2)}, u32[]{:S(2)}) collective-permute-start(f32[72,256]{1,0:T(8,128)S(1)} %shard_map.161.refs_0_), channel_id=1, source_target_pairs={{0,4},{1,5},{2,6},{3,7},{4,0},{5,1},{6,2},{7,3},{8,12},{9,13},{10,... | collective-permute-start | bytes 221192 | tf_op jit(solution)/shard_map/ppermute | solution.py:96
  214.7 10.5 %copy-start.8 = (bf16[960,256]{1,0:T(8,128)(2,1)S(1)}, bf16[960,256]{1,0:T(8,128)(2,1)}, u32[]{:S(2)}) copy-start(bf16[960,256]{1,0:T(8,128)(2,1)} %copy-done.6) | copy-start | bytes 1474564
  220.5 11.0 %collective-permute-start.51 = (f32[72,256]{1,0:T(8,128)S(1)}, f32[72,256]{1,0:T(8,128)S(1)}, u32[]{:S(2)}, u32[]{:S(2)}) collective-permute-start(f32[72,256]{1,0:T(8,128)S(1)} %shard_map.163.refs_2_), channel_id=1, source_target_pairs={{0,8},{8,0},{16,24},{24,16},{1,9},{9,1},{17,25},{25,17},{2,10},{10... | collective-permute-start | bytes 221192 | tf_op jit(solution)/shard_map/ppermute | solution.py:96
  222.7 8.9 %collective-permute-start.52 = (f32[72,256]{1,0:T(8,128)S(1)}, f32[72,256]{1,0:T(8,128)S(1)}, u32[]{:S(2)}, u32[]{:S(2)}) collective-permute-start(f32[72,256]{1,0:T(8,128)S(1)} %shard_map.163.refs_2_), channel_id=1, source_target_pairs={{0,16},{8,24},{16,0},{24,8},{1,17},{9,25},{17,1},{25,9},{2,18},{10... | collective-permute-start | bytes 221192 | tf_op jit(solution)/shard_map/ppermute | solution.py:96
  223.9 7.7 %collective-permute-start.53 = (f32[72,256]{1,0:T(8,128)S(1)}, f32[72,256]{1,0:T(8,128)S(1)}, u32[]{:S(2)}, u32[]{:S(2)}) collective-permute-start(f32[72,256]{1,0:T(8,128)S(1)} %shard_map.163.refs_2_), channel_id=1, source_target_pairs={{0,24},{8,16},{16,8},{24,0},{1,25},{9,17},{17,9},{25,1},{2,26},{10... | collective-permute-start | bytes 221192 | tf_op jit(solution)/shard_map/ppermute | solution.py:96
  (17 other events, 48.6 us)
Sparse Core Ops, SparseCore 0:
  9.9 52.8 all-gather.3
  72.1 44.7 all-gather.5

commit v5 on v4

--- a/solution.py
+++ b/solution.py
@@ -406,8 +406,10 @@
     )
 
 
-def panel_table(w_disp_ref, hidden, with_log):
-    base = DISP_BASE + softplus(dot_nt(w_disp_ref[...], hidden))
+def panel_table(w_disp_ref, hidden, with_log, slope_ref, norm):
+    disp = dot_nt(w_disp_ref[...], hidden)
+    slope_ref[...] = sigmoid(disp) * norm
+    base = DISP_BASE + softplus(disp)
     parts = split3(base)
     if with_log:
         parts = [jnp.concatenate(pair, axis=1) for pair in zip(parts, split3(jnp.log(base)))]
@@ -440,14 +442,14 @@
     keys, norm, me_ref, counts_ref, col_ref, row_ref, scale_ref, wm_ref, wd_ref, *refs
 ):
     hids = refs[: len(keys)]
-    high_ref, low_ref, sum_ref, hid_ref, table_ref = refs[len(keys) :]
+    high_ref, low_ref, sum_ref, hid_ref, slope_ref, table_ref = refs[len(keys) :]
     cells = hid_ref.shape[0]
     panel_count = wd_ref.shape[0]
 
     @pl.when(pl.program_id(0) == 0)
     def _():
         place_cells(keys, me_ref[0], [block[...] for block in hids], hid_ref)
-        table_ref[...] = panel_table(wd_ref, hid_ref[...], True)
+        table_ref[...] = panel_table(wd_ref, hid_ref[...], True, slope_ref, norm)
         sum_ref[...] = jnp.zeros_like(sum_ref)
 
     both = dot_nn(panel_pick(col_ref, panel_count), table_ref[...])
@@ -514,8 +516,15 @@
             shape_of((genes, cells), BF16),
             shape_of((wide, cells), F32),
             shape_of((cells, width), BF16),
-        ),
-        out_specs=[by_gene(cells), by_gene(cells), fixed(wide, cells), fixed(cells, width)],
+            shape_of((panel_count, cells), F32),
+        ),
+        out_specs=[
+            by_gene(cells),
+            by_gene(cells),
+            fixed(wide, cells),
+            fixed(cells, width),
+            fixed(panel_count, cells),
+        ],
         scratch_shapes=[pltpu.VMEM((3 * panel_count, 2 * cells), BF16)],
         cost_estimate=pl.CostEstimate(
             flops=2 * genes * cells * width + 150 * genes * cells,
@@ -527,7 +536,7 @@
 
 def far_kernel(keys, norm, genes_all, place_ref, seen_ref, lib_ref, col_ref, wm_ref, wd_ref, *refs):
     hids = refs[:2]
-    high_ref, low_ref, hid_ref, table_ref = refs[2:]
+    high_ref, low_ref, hid_ref, slope_ref, table_ref = refs[2:]
     seen = seen_ref[0].astype(F32)
     lib = lib_ref[0].astype(F32)
     panel_count = wd_ref.shape[0]
@@ -536,7 +545,7 @@
     def _():
         blocks = [half[at, 0] for half in hids for at in range(half.shape[0])]
         place_cells(keys, place_ref[0], blocks, hid_ref)
-        table_ref[...] = panel_table(wd_ref, hid_ref[...], False)
+        table_ref[...] = panel_table(wd_ref, hid_ref[...], False, slope_ref, norm)
 
     library = jnp.sum(lib, axis=0, keepdims=True)
     _, _, d_logit = rate_terms(
@@ -575,6 +584,7 @@
                 by_gene(cells),
                 by_gene(cells),
                 pl.BlockSpec((cells, width), lambda i, at: (0, 0)),
+                pl.BlockSpec((panel_count, cells), lambda i, at: (0, 0)),
             ],
             scratch_shapes=[pltpu.VMEM((3 * panel_count, cells), BF16)],
         ),
@@ -582,6 +592,7 @@
             shape_of((genes, cells), BF16),
             shape_of((genes, cells), BF16),
             shape_of((cells, width), BF16),
+            shape_of((panel_count, cells), F32),
         ),
         compiler_params=PARAMS,
         cost_estimate=pl.CostEstimate(
@@ -625,14 +636,14 @@
     )
 
 
-def disp_kernel(norm, genes_all, place_ref, wd_ref, *refs):
-    count = (len(refs) - 3) // 2
-    sums, hids = refs[:count], refs[count : 2 * count]
-    grad_ref, loss_ref, term_ref = refs[2 * count :]
-    panel_count = wd_ref.shape[0]
+def disp_kernel(genes_all, place_ref, *refs):
+    count = (len(refs) - 3) // 3
+    sums, hids, slopes = refs[:count], refs[count : 2 * count], refs[2 * count : 3 * count]
+    grad_ref, loss_ref, term_ref = refs[3 * count :]
+    panel_count = grad_ref.shape[0]
     for other in range(count):
         hidden = hids[other][...]
-        d_disp = sums[other][:panel_count] * sigmoid(dot_nt(wd_ref[...], hidden)) * norm
+        d_disp = sums[other][:panel_count] * slopes[other][...]
         parts = jnp.concatenate([part.astype(F32) for part in split3(d_disp)], axis=0)
         three = dot_nn(parts.astype(BF16), hidden)
         term_ref[place_ref[1] ^ other] = (
@@ -647,13 +658,13 @@
     loss_ref[...] = sums[0][panel_count : panel_count + 1] * (1.0 / genes_all)
 
 
-def disp_call(place, sums, hids, w_disp_t, norm, genes_all, after):
-    panel_count, width = w_disp_t.shape
-    cells = sums[0].shape[1]
-    return launch(
-        functools.partial(disp_kernel, norm, genes_all),
-        (place, w_disp_t, *sums, *hids),
-        [SCALAR] + [WHOLE] * (1 + len(sums) + len(hids)),
+def disp_call(place, sums, hids, slopes, genes_all, after):
+    panel_count, cells = slopes[0].shape
+    width = hids[0].shape[1]
+    return launch(
+        functools.partial(disp_kernel, genes_all),
+        (place, *sums, *hids, *slopes),
+        [SCALAR] + [WHOLE] * 3 * len(sums),
         after,
         out_shape=(shape_of((panel_count, width), F32), shape_of((1, cells), F32)),
         out_specs=[WHOLE] * 2,
@@ -819,21 +830,25 @@
     parts = parts[:1] + [hop(part, "gene", key) for part, key in zip(parts[1:], keys[1:])]
     hidden = pool(mid, parts)
 
-    hids = [hidden] + [hop(hidden, "gene", key) for key in keys[1 : gene_count // 2]]
+    away = [hop(hidden, "grp", straight(rel)) for rel in range(1, grp_count)]
+    own = stack([hidden], away[:2])[0]
+    hids = [own] + [hop(own, "gene", key) for key in keys[1 : gene_count // 2]]
     hids += [hop(block, "gene", straight(1)) for block in hids]
-    far_hids = [stack([hop(hidden, "grp", straight(rel)) for rel in range(1, grp_count)], hids)]
+    far_hids = [stack(away, [])]
     far_hids += [hop(far_hids[0], "gene", key) for key in keys[1 : gene_count // 2]]
-    high, low, sums, own_hid = decode(
+    high, low, sums, own_hid, slope = decode(
         me, keys, counts_t, panel_col, panel_row, library / genes_all, w_mean_t, w_disp_t, hids, norm
     )
     groups = [(own_hid, high, low)]
+    slopes = [slope]
     far_hids = [stack(far_hids, [high])]
     far_hids.append(hop(far_hids[0], "gene", straight(1)))
     for other in range(1, grp_count):
-        high, low, hid = far_call(
+        high, low, hid, slope = far_call(
             place, keys, other, seen, panel_col, w_mean_t, w_disp_t, far_hids, norm, genes_all
         )
         groups.append((hid, high, low))
+        slopes.append(slope)
     bits = gene_count.bit_length() - 1
     for bit in range(bits):
         after = [groups[min(bit, grp_count - 1)][1]]
@@ -841,7 +856,7 @@
     sums = [sums] + [hop(sums, "grp", straight(rel)) for rel in range(1, grp_count)]
     grad_mean = in_hbm(grad_mean_call(place, groups))
     grad_disp, loss = disp_call(
-        place, sums, [group[0] for group in groups], w_disp_t, norm, genes_all, [grad_mean]
+        place, sums, [group[0] for group in groups], slopes, genes_all, [grad_mean]
     )
     return (loss.reshape(cells), grad_mean, grad_disp.T)
 

time: 244 us -> 243 us (level)
  Pallas kernels: 72.6 us -> 69.9 us
  starting transfers between devices: 47.6 us -> 50.1 us
    pallas_call x25 -> x26, Pallas kernels: 55.4 us -> 52.5 us  [launch(): pl.pallas_call(body, in_specs=list(in_specs) + [ANYWHERE] * len(after), c...]
    ppermute x54, starting transfers between devices: 47.5 us -> 50 us  [hop(): return lax.ppermute(value, axis, [(i, i ^ key[i & 1]) for i in range(size)])]
  transfers between devices with their start and end apart: 56 -> 56, of which waited for: 28 -> 30; matrix products, arithmetic and copies ran while one was open for 5% -> 5% of each run, Pallas kernels for 25% -> 25%
where the time goes in v5:
time: 243 us; the launch traced here: 242 us
  waiting for transfers between devices  83.6 us (34%)
  Pallas kernels  69.9 us (29%)
  starting transfers between devices  50.1 us (21%)
  local copies, waits for them, and re-layouts  23.1 us (10%)
  between operations  14.6 us (6%)
    ppermute x54, waiting for transfers between devices, hop(): return lax.ppermute(value, axis, [(i, i ^ key[i & 1]) for i in range(size)])  83.5 us
    pallas_call x26, Pallas kernels, launch(): pl.pallas_call(body, in_specs=list(in_specs) + [ANYWHERE] * len(after), c...  52.5 us
    ppermute x54, starting transfers between devices, hop(): return lax.ppermute(value, axis, [(i, i ^ key[i & 1]) for i in range(size)])  50 us
    pallas_call x3, Pallas kernels, far_call(): pl.pallas_call(functools.partial(far_kernel, keys, norm, genes_all), grid...  17.3 us
    unnamed x51, local copies, waits for them, and re-layouts  9.37 us
    reshape x2, local copies, waits for them, and re-layouts, flat_qkv(): return weights.transpose(2, 1, 0).reshape(-1, weights.shape[0])  8.55 us
  transfers between devices with their start and end apart: 56, of which 30 were waited for; matrix products, arithmetic and copies ran while one was open for 5% of the time, Pallas kernels for 25%

profile of v5, /device:TPU:0, one launch (start us, length us, event | category | flops | bytes accessed | tf_op | source)
XLA Modules:
  0.0 242.2 jit_solution(278873164856431657)
XLA Ops:
  7.3 2.4 all_gather_reshape.3
  11.2 2.8 %collective-permute-start.1 = (f32[1,256]{1,0:T(1,128)S(1)}, f32[1,256]{1,0:T(1,128)S(1)}, u32[]{:S(2)}, u32[]{:S(2)}) collective-permute-start(f32[1,256]{1,0:T(1,128)S(1)} %add.19), channel_id=1, source_target_pairs={{0,2},{1,3},{2,0},{3,1},{4,6},{5,7},{6,4},{7,5},{8,10},{9,11},{10,... | collective-permute-start | bytes 3080 | tf_op jit(solution)/shard_map/ppermute | solution.py:96
  15.8 1.8 collective-permute-start.2
  18.4 1.1 collective-permute-done.2
  19.5 6.4 %shard_map.139 = (f32[128,3200]{1,0:T(8,128)S(1)}, f32[128,3200]{1,0:T(8,128)S(1)}) custom-call(s32[1]{0:T(128)} %bitcast.refs_0_, s32[960,256]{1,0:T(8,128)S(1)} %bitcast.34, f32[1,256]{1,0:T(1,128)S(1)} %get-tuple-element.87.refs_2_, bf16[960,6400]{1,0:T(8,128)(2,1)} %refs_3_.3, s32[128,1]{1,0:T(8,128)S(1)} %reshape_tile.12.refs_4_.refs_1_, ...), custom_call_target="tpu_custom_call" | custom-call | flops 1572864000 | bytes 9420800 | tf_op jit(solution)/shard_map/pallas_call | solution.py:43
  25.9 6.3 %shard_map.142 = (f32[128,3200]{1,0:T(8,128)S(1)}, f32[128,3200]{1,0:T(8,128)S(1)}) custom-call(s32[1]{0:T(128)} %bitcast.refs_0_, s32[960,256]{1,0:T(8,128)S(1)} %bitcast.35, f32[1,256]{1,0:T(1,128)S(1)} %get-tuple-element.87.refs_2_, bf16[960,6400]{1,0:T(8,128)(2,1)} %refs_3_.3), custom_call_target="tpu_custom_call" | custom-call | flops 1572864000 | bytes 9420800 | tf_op jit(solution)/shard_map/pallas_call | solution.py:43
  33.7 1.7 collective-permute-start.4
  37.7 1.7 collective-permute-start.7
  39.4 4.2 %reshape.78.refs_2_.refs_0_ = bf16[600,1600]{1,0:T(8,128)(2,1)} reshape(bf16[150,4,1600]{2,1,0:T(4,128)(2,1)} %bitcast.68) | data formatting | bytes 3840000 | tf_op jit(solution)/shard_map/reshape | solution.py:727
  43.6 4.3 %reshape.79.refs_2_.refs_0_ = bf16[600,1600]{1,0:T(8,128)(2,1)} reshape(bf16[150,4,1600]{2,1,0:T(4,128)(2,1)} %bitcast.69) | data formatting | bytes 3840000 | tf_op jit(solution)/shard_map/reshape | solution.py:727
  47.9 1.5 reshape.80.refs_3_.refs_11_
  49.6 1.7 copy-done.3
  51.2 1.1 shard_map.141
  52.4 1.9 collective-permute-start.5
  54.3 8.4 %collective-permute-done.7.refs_1_ = bf16[64,3200]{1,0:T(8,128)(2,1)} collective-permute-done((bf16[64,3200]{1,0:T(8,128)(2,1)}, bf16[64,3200]{1,0:T(8,128)(2,1)}, u32[]{:S(2)}, u32[]{:S(2)}) %collective-permute-start.7) | collective-permute-done | bytes 409632 | tf_op jit(solution)/shard_map/ppermute | solution.py:96
  62.8 1.1 shard_map.144
  63.9 1.7 collective-permute-start.8
  65.6 4.1 %collective-permute-done.8.refs_3_ = bf16[32,3200]{1,0:T(8,128)(2,1)S(1)} collective-permute-done((bf16[32,3200]{1,0:T(8,128)(2,1)S(1)}, bf16[32,3200]{1,0:T(8,128)(2,1)S(1)}, u32[]{:S(2)}, u32[]{:S(2)}) %collective-permute-start.8) | collective-permute-done | bytes 204832 | tf_op jit(solution)/shard_map/ppermute | solution.py:96
  73.1 1.7 collective-permute-start.9
  74.8 6.5 %collective-permute-done.9.refs_1_.refs_4_ = bf16[4,32,1600]{2,1,0:T(8,128)(2,1)S(1)} collective-permute-done((bf16[4,32,1600]{2,1,0:T(8,128)(2,1)S(1)}, bf16[4,32,1600]{2,1,0:T(8,128)(2,1)S(1)}, u32[]{:S(2)}, u32[]{:S(2)}) %collective-permute-start.9) | collective-permute-done | bytes 409632 | tf_op jit(solution)/shard_map/ppermute | solution.py:96
  81.3 1.0 collective-permute-start.10
  82.3 1.0 collective-permute-start.11
  83.9 5.6 %collective-permute-done.10.refs_5_ = bf16[4,32,1600]{2,1,0:T(8,128)(2,1)S(1)} collective-permute-done((bf16[4,32,1600]{2,1,0:T(8,128)(2,1)S(1)}, bf16[4,32,1600]{2,1,0:T(8,128)(2,1)S(1)}, u32[]{:S(2)}, u32[]{:S(2)}) %collective-permute-start.10) | collective-permute-done | bytes 409632 | tf_op jit(solution)/shard_map/ppermute | solution.py:96
  89.5 4.6 %collective-permute-done.11.refs_6_ = bf16[4,32,1600]{2,1,0:T(8,128)(2,1)S(1)} collective-permute-done((bf16[4,32,1600]{2,1,0:T(8,128)(2,1)S(1)}, bf16[4,32,1600]{2,1,0:T(8,128)(2,1)S(1)}, u32[]{:S(2)}, u32[]{:S(2)}) %collective-permute-start.11) | collective-permute-done | bytes 409632 | tf_op jit(solution)/shard_map/ppermute | solution.py:96
  94.1 1.7 collective-permute-done.15.refs_10_
  95.8 5.6 %shard_map.149.refs_3_ = bf16[8,128,200]{2,1,0:T(8,128)(2,1)S(1)} custom-call(bf16[600,1600]{1,0:T(8,128)(2,1)S(1)} %copy-done.4, s32[128,1]{1,0:T(8,128)S(1)} %reshape_tile.12.refs_4_.refs_1_, s32[1,128]{1,0:T(1,128)S(1)} %reshape_tile.11.refs_5_.refs_2_, bf16[4,32,1600]{2,1,0:T(8,128)(2,1)S(1)} %bitcast.51, ...), custom_call_target="tpu_custom_call" | custom-call | flops 2385510400 | bytes 5606400 | tf_op jit(solution)/shard_map/pallas_call | solution.py:43
  101.5 1.7 collective-permute-start.16
  105.0 1.1 collective-permute-start.20
  106.8 1.4 collective-permute-done.17.refs_5_
  108.2 1.2 collective-permute-start.22
  110.8 2.2 collective-permute-done.22.refs_10_
  113.0 3.8 %shard_map.150 = (f32[4,32,1600]{2,1,0:T(8,128)S(1)}, bf16[4,32,1600]{2,1,0:T(8,128)(2,1)S(1)}) custom-call(s32[1]{0:T(128)} %bitcast.refs_0_, bf16[8,200,1600]{2,1,0:T(8,128)(2,1)} %all-gather.4.cloned.1.call-done.refs_1_, f32[4,32,1600]{2,1,0:T(8,128)S(1)} %get-tuple-element.56.refs_2_, bf16[8,128,200]{2,1,0:T(8,128)(2,1)S(1)} %shard_map.149.refs_3_, ...), custom_call_target="tpu_custom_call" | custom-call | flops 655360000 | bytes 7577600 | tf_op jit(solution)/shard_map/pallas_call | solution.py:43
  119.6 8.1 %collective-permute-done.23.refs_1_.refs_4_ = bf16[4,32,1600]{2,1,0:T(8,128)(2,1)S(1)} collective-permute-done((bf16[4,32,1600]{2,1,0:T(8,128)(2,1)S(1)}, bf16[4,32,1600]{2,1,0:T(8,128)(2,1)S(1)}, u32[]{:S(2)}, u32[]{:S(2)}) %collective-permute-start.23) | collective-permute-done | bytes 409632 | tf_op jit(solution)/shard_map/ppermute | solution.py:96
  127.8 1.0 collective-permute-start.24
  128.8 1.0 collective-permute-start.25
  130.4 5.6 %collective-permute-done.24.refs_5_ = bf16[4,32,1600]{2,1,0:T(8,128)(2,1)S(1)} collective-permute-done((bf16[4,32,1600]{2,1,0:T(8,128)(2,1)S(1)}, bf16[4,32,1600]{2,1,0:T(8,128)(2,1)S(1)}, u32[]{:S(2)}, u32[]{:S(2)}) %collective-permute-start.24) | collective-permute-done | bytes 409632 | tf_op jit(solution)/shard_map/ppermute | solution.py:96
  136.0 4.6 %collective-permute-done.25.refs_6_ = bf16[4,32,1600]{2,1,0:T(8,128)(2,1)S(1)} collective-permute-done((bf16[4,32,1600]{2,1,0:T(8,128)(2,1)S(1)}, bf16[4,32,1600]{2,1,0:T(8,128)(2,1)S(1)}, u32[]{:S(2)}, u32[]{:S(2)}) %collective-permute-start.25) | collective-permute-done | bytes 409632 | tf_op jit(solution)/shard_map/ppermute | solution.py:96
  140.5 1.7 collective-permute-done.29.refs_10_
  142.3 6.3 %shard_map.153 = (f32[4,32,1600]{2,1,0:T(8,128)S(1)}, f32[4,32,1600]{2,1,0:T(8,128)S(1)}) custom-call(bf16[600,1600]{1,0:T(8,128)(2,1)S(1)} %copy-done.2, s32[256,1]{1,0:T(8,128)S(1)} %select_n.43.refs_6_.refs_1_, s32[1,256]{1,0:T(1,128)S(1)} %select_n.42.refs_7_.refs_2_, bf16[4,32,1600]{2,1,0:T(8,128)(2,1)S(1)} %bitcast.48, ...), custom_call_target="tpu_custom_call" | custom-call | flops 2804940800 | bytes 5606400 | tf_op jit(solution)/shard_map/pallas_call | solution.py:43
  148.8 2.2 collective-permute-done.30.refs_1_
  151.3 1.3 collective-permute-start.32
  152.6 2.1 collective-permute-start.33
  154.7 4.6 %collective-permute-done.31.refs_2_ = f32[32,1600]{1,0:T(8,128)S(1)} collective-permute-done((f32[32,1600]{1,0:T(8,128)S(1)}, f32[32,1600]{1,0:T(8,128)S(1)}, u32[]{:S(2)}, u32[]{:S(2)}) %collective-permute-start.31) | collective-permute-done | bytes 204832 | tf_op jit(solution)/shard_map/ppermute | solution.py:96
  159.4 4.9 %collective-permute-done.33.refs_4_ = f32[32,1600]{1,0:T(8,128)S(1)} collective-permute-done((f32[32,1600]{1,0:T(8,128)S(1)}, f32[32,1600]{1,0:T(8,128)S(1)}, u32[]{:S(2)}, u32[]{:S(2)}) %collective-permute-start.33) | collective-permute-done | bytes 204832 | tf_op jit(solution)/shard_map/ppermute | solution.py:96
  164.7 2.5 %collective-permute-start.35 = (bf16[32,1600]{1,0:T(8,128)(2,1)S(1)}, bf16[32,1600]{1,0:T(8,128)(2,1)S(1)}, u32[]{:S(2)}, u32[]{:S(2)}) collective-permute-start(bf16[32,1600]{1,0:T(8,128)(2,1)S(1)} %shard_map.155.refs_0_), channel_id=1, source_target_pairs={{0,16},{8,24},{16,0},{24,8},{1,17},{9,25},{17,1},{25,9},{2,18},{10... | collective-permute-start | bytes 307208 | tf_op jit(solution)/shard_map/ppermute | solution.py:96
  167.3 4.2 %collective-permute-done.34.refs_1_.refs_0_ = bf16[32,1600]{1,0:T(8,128)(2,1)S(1)} collective-permute-done((bf16[32,1600]{1,0:T(8,128)(2,1)S(1)}, bf16[32,1600]{1,0:T(8,128)(2,1)S(1)}, u32[]{:S(2)}, u32[]{:S(2)}) %collective-permute-start.34) | collective-permute-done | bytes 102432 | tf_op jit(solution)/shard_map/ppermute | solution.py:96
  171.5 1.7 collective-permute-done.35.refs_2_.refs_1_
  173.9 2.4 collective-permute-start.45
  177.1 2.1 collective-permute-start.38
  180.4 1.5 collective-permute-start.46
  181.9 1.8 collective-permute-done.37.refs_9_
  184.0 1.3 collective-permute-start.48
  186.8 9.5 %shard_map.157 = (bf16[960,256]{1,0:T(8,128)(2,1)S(1)}, bf16[960,256]{1,0:T(8,128)(2,1)S(1)}, f32[72,256]{1,0:T(8,128)S(1)}, bf16[256,1600]{1,0:T(8,128)(2,1)S(1)}, f32[64,256]{1,0:T(8,128)S(1)}) custom-call(s32[1]{0:T(128)} %bitcast.refs_0_, s32[960,256]{1,0:T(8,128)S(1)} %bitcast.37, s32[960,1]{1,0:T(8,128)S(1)} %copy.31.refs_8_.refs_2_.col_ref, ...), custom_call_target="tpu_custom_call" | custom-call | flops 823296000 | bytes 5038080 | tf_op jit(solution)/shard_map/pallas_call | solution.py:43
  196.4 1.1 collective-permute-done.47.refs_2_
  199.0 2.5 %collective-permute-done.43.refs_1_ = f32[72,256]{1,0:T(8,128)S(1)} collective-permute-done((f32[72,256]{1,0:T(8,128)S(1)}, f32[72,256]{1,0:T(8,128)S(1)}, u32[]{:S(2)}, u32[]{:S(2)}) %collective-permute-start.43) | collective-permute-done | bytes 73760 | tf_op jit(solution)/shard_map/ppermute | solution.py:96
  201.5 1.0 copy-done.7
  202.5 1.7 collective-permute-start.44
  204.3 5.8 %shard_map.161 = (bf16[960,256]{1,0:T(8,128)(2,1)S(1)}, bf16[960,256]{1,0:T(8,128)(2,1)S(1)}, bf16[256,1600]{1,0:T(8,128)(2,1)S(1)}, f32[64,256]{1,0:T(8,128)S(1)}) custom-call(s32[2]{0:T(128)S(1)} %pad_add_fusion.place_ref.refs_0_, bf16[4,976,256]{2,1,0:T(8,128)(2,1)} %bitcast.58, bf16[4,976,256]{2,1,0:T(8,128)(2,1)} %bitcast.59, ...), custom_call_target="tpu_custom_call" | custom-call | flops 801177600 | bytes 4546560 | tf_op jit(solution)/shard_map/pallas_call | solution.py:569
  210.7 5.8 %shard_map.165 = (bf16[960,256]{1,0:T(8,128)(2,1)S(1)}, bf16[960,256]{1,0:T(8,128)(2,1)S(1)}, bf16[256,1600]{1,0:T(8,128)(2,1)S(1)}, f32[64,256]{1,0:T(8,128)S(1)}) custom-call(s32[2]{0:T(128)S(1)} %pad_add_fusion.place_ref.refs_0_, bf16[4,976,256]{2,1,0:T(8,128)(2,1)} %bitcast.60, bf16[4,976,256]{2,1,0:T(8,128)(2,1)} %bitcast.61, ...), custom_call_target="tpu_custom_call" | custom-call | flops 801177600 | bytes 4546560 | tf_op jit(solution)/shard_map/pallas_call | solution.py:569
  216.5 5.8 %shard_map.163 = (bf16[960,256]{1,0:T(8,128)(2,1)S(1)}, bf16[960,256]{1,0:T(8,128)(2,1)S(1)}, bf16[256,1600]{1,0:T(8,128)(2,1)S(1)}, f32[64,256]{1,0:T(8,128)S(1)}) custom-call(s32[2]{0:T(128)S(1)} %pad_add_fusion.place_ref.refs_0_, bf16[4,976,256]{2,1,0:T(8,128)(2,1)} %bitcast.62, bf16[4,976,256]{2,1,0:T(8,128)(2,1)} %bitcast.63, ...), custom_call_target="tpu_custom_call" | custom-call | flops 801177600 | bytes 4546560 | tf_op jit(solution)/shard_map/pallas_call | solution.py:569
  222.4 1.8 collective-permute-start.52
  224.2 2.6 %collective-permute-start.53 = (f32[72,256]{1,0:T(8,128)S(1)}, f32[72,256]{1,0:T(8,128)S(1)}, u32[]{:S(2)}, u32[]{:S(2)}) collective-permute-start(f32[72,256]{1,0:T(8,128)S(1)} %shard_map.164.refs_1_), channel_id=1, source_target_pairs={{0,24},{8,16},{16,8},{24,0},{1,25},{9,17},{17,9},{25,1},{2,26},{10... | collective-permute-start | bytes 221192 | tf_op jit(solution)/shard_map/ppermute | solution.py:96
  226.8 6.3 %shard_map.166.refs_13_ = f32[400,960]{1,0:T(8,128)} custom-call(s32[2]{0:T(128)S(1)} %pad_add_fusion.place_ref.refs_0_, bf16[256,1600]{1,0:T(8,128)(2,1)S(1)} %copy-done.12, bf16[960,256]{1,0:T(8,128)(2,1)S(1)} %copy-done.8, bf16[960,256]{1,0:T(8,128)(2,1)S(1)} %copy-done.20, bf16[256,1600]{1,0:T(8,128)(2,1)S(1)} %get-tuple-element.71.refs_4_.refs_6_, ...), custom_call_target="tpu_custom_call" | custom-call | flops 2883584000 | bytes 8744960 | tf_op jit(solution)/shard_map/pallas_call | solution.py:43
  233.0 2.3 shard_map.167
  (155 shorter events, 27.0 us)
Async XLA Ops:
  7.2 10.7 %copy-start.21 = (s32[960]{0:T(1024)S(1)}, s32[960]{0:T(1024)}, u32[]{:S(2)}) copy-start(s32[960]{0:T(1024)} %param.13) | copy-start | bytes 11524
  7.2 64.8 %all-gather.4.cloned.1.call-start = ((), (), s32[]{:S(2)}) async-start(), calls=%async_computation | async-start | bytes 5990400 | tf_op jit(solution)/shard_map/all_gather | solution.py:773
  9.7 108.8 %all-gather.6.cloned.1.call-start = ((), (), s32[]{:S(2)}) async-start(), calls=%async_computation.1 | async-start | bytes 2498560 | tf_op jit(solution)/shard_map/all_gather | solution.py:801
  9.9 1.3 collective-permute-start
  11.2 4.6 %collective-permute-start.1 = (f32[1,256]{1,0:T(1,128)S(1)}, f32[1,256]{1,0:T(1,128)S(1)}, u32[]{:S(2)}, u32[]{:S(2)}) collective-permute-start(f32[1,256]{1,0:T(1,128)S(1)} %add.19), channel_id=1, source_target_pairs={{0,2},{1,3},{2,0},{3,1},{4,6},{5,7},{6,4},{7,5},{8,10},{9,11},{10,... | collective-permute-start | bytes 3080 | tf_op jit(solution)/shard_map/ppermute | solution.py:96
  15.8 3.6 %collective-permute-start.2 = (f32[1,256]{1,0:T(1,128)S(1)}, f32[1,256]{1,0:T(1,128)S(1)}, u32[]{:S(2)}, u32[]{:S(2)}) collective-permute-start(f32[1,256]{1,0:T(1,128)S(1)} %add.20), channel_id=1, source_target_pairs={{0,4},{1,5},{2,6},{3,7},{4,0},{5,1},{6,2},{7,3},{8,12},{9,13},{10,... | collective-permute-start | bytes 3080 | tf_op jit(solution)/shard_map/ppermute | solution.py:96
  25.9 6.9 %collective-permute-start.3 = (f32[128,3200]{1,0:T(8,128)S(1)}, f32[128,3200]{1,0:T(8,128)S(1)}, u32[]{:S(2)}, u32[]{:S(2)}) collective-permute-start(f32[128,3200]{1,0:T(8,128)S(1)} %get-tuple-element.45), channel_id=1, source_target_pairs={{0,1},{1,0},{2,3},{3,2},{4,5},{5,4},{6,7},{7,6},{8,9},{9,8},{10,11... | collective-permute-start | bytes 4915208 | tf_op jit(solution)/shard_map/ppermute | solution.py:96
  32.2 3.7 %collective-permute-start.6 = (f32[128,3200]{1,0:T(8,128)S(1)}, f32[128,3200]{1,0:T(8,128)S(1)}, u32[]{:S(2)}, u32[]{:S(2)}) collective-permute-start(f32[128,3200]{1,0:T(8,128)S(1)} %get-tuple-element.51), channel_id=1, source_target_pairs={{0,1},{1,0},{2,3},{3,2},{4,5},{5,4},{6,7},{7,6},{8,9},{9,8},{10,11... | collective-permute-start | bytes 4915208 | tf_op jit(solution)/shard_map/ppermute | solution.py:96
  33.7 15.9 %collective-permute-start.4 = (bf16[64,3200]{1,0:T(8,128)(2,1)}, bf16[64,3200]{1,0:T(8,128)(2,1)}, u32[]{:S(2)}, u32[]{:S(2)}) collective-permute-start(bf16[64,3200]{1,0:T(8,128)(2,1)} %get-tuple-element.47), channel_id=1, source_target_pairs={{0,4},{1,3},{2,6},{3,1},{4,0},{5,7},{6,2},{7,5},{8,12},{9,11},{10,... | collective-permute-start | bytes 1228808 | tf_op jit(solution)/shard_map/ppermute | solution.py:96
  37.7 25.1 %collective-permute-start.7 = (bf16[64,3200]{1,0:T(8,128)(2,1)}, bf16[64,3200]{1,0:T(8,128)(2,1)}, u32[]{:S(2)}, u32[]{:S(2)}) collective-permute-start(bf16[64,3200]{1,0:T(8,128)(2,1)} %get-tuple-element.53), channel_id=1, source_target_pairs={{0,4},{1,3},{2,6},{3,1},{4,0},{5,7},{6,2},{7,5},{8,12},{9,11},{10,... | collective-permute-start | bytes 1228808 | tf_op jit(solution)/shard_map/ppermute | solution.py:96
  49.4 13.4 %copy-start.1 = (bf16[600,1600]{1,0:T(8,128)(2,1)S(1)}, bf16[600,1600]{1,0:T(8,128)(2,1)}, u32[]{:S(2)}) copy-start(bf16[600,1600]{1,0:T(8,128)(2,1)} %reshape.79.refs_2_.refs_0_) | copy-start | bytes 5760004
  51.2 11.5 %copy-start.14 = (f32[64,3200]{1,0:T(8,128)S(1)}, f32[64,3200]{1,0:T(8,128)}, u32[]{:S(2)}) copy-start(f32[64,3200]{1,0:T(8,128)} %copy-done.13) | copy-start | bytes 2457604
  52.4 13.2 %collective-permute-start.5 = (bf16[32,3200]{1,0:T(8,128)(2,1)S(1)}, bf16[32,3200]{1,0:T(8,128)(2,1)S(1)}, u32[]{:S(2)}, u32[]{:S(2)}) collective-permute-start(bf16[32,3200]{1,0:T(8,128)(2,1)S(1)} %get-tuple-element.49), channel_id=1, source_target_pairs={{0,2},{1,5},{2,0},{3,7},{4,6},{5,1},{6,4},{7,3},{8,10},{9,13},{10,... | collective-permute-start | bytes 614408 | tf_op jit(solution)/shard_map/ppermute | solution.py:96
  63.9 5.8 %collective-permute-start.8 = (bf16[32,3200]{1,0:T(8,128)(2,1)S(1)}, bf16[32,3200]{1,0:T(8,128)(2,1)S(1)}, u32[]{:S(2)}, u32[]{:S(2)}) collective-permute-start(bf16[32,3200]{1,0:T(8,128)(2,1)S(1)} %get-tuple-element.55), channel_id=1, source_target_pairs={{0,2},{1,5},{2,0},{3,7},{4,6},{5,1},{6,4},{7,3},{8,10},{9,13},{10,... | collective-permute-start | bytes 614408 | tf_op jit(solution)/shard_map/ppermute | solution.py:96
  73.0 22.8 %copy-start.4 = (bf16[600,1600]{1,0:T(8,128)(2,1)S(1)}, bf16[600,1600]{1,0:T(8,128)(2,1)}, u32[]{:S(2)}) copy-start(bf16[600,1600]{1,0:T(8,128)(2,1)} %reshape.78.refs_2_.refs_0_) | copy-start | bytes 5760004
  73.1 8.2 %collective-permute-start.9 = (bf16[4,32,1600]{2,1,0:T(8,128)(2,1)S(1)}, bf16[4,32,1600]{2,1,0:T(8,128)(2,1)S(1)}, u32[]{:S(2)}, u32[]{:S(2)}) collective-permute-start(bf16[4,32,1600]{2,1,0:T(8,128)(2,1)S(1)} %bitcast.42), channel_id=1, source_target_pairs={{0,2},{1,5},{2,0},{3,7},{4,6},{5,1},{6,4},{7,3},{8,10},{9,13},{10,... | collective-permute-start | bytes 1228808 | tf_op jit(solution)/shard_map/ppermute | solution.py:96
  81.3 8.2 %collective-permute-start.10 = (bf16[4,32,1600]{2,1,0:T(8,128)(2,1)S(1)}, bf16[4,32,1600]{2,1,0:T(8,128)(2,1)S(1)}, u32[]{:S(2)}, u32[]{:S(2)}) collective-permute-start(bf16[4,32,1600]{2,1,0:T(8,128)(2,1)S(1)} %bitcast.49), channel_id=1, source_target_pairs={{0,4},{1,3},{2,6},{3,1},{4,0},{5,7},{6,2},{7,5},{8,12},{9,11},{10,... | collective-permute-start | bytes 1228808 | tf_op jit(solution)/shard_map/ppermute | solution.py:96
  82.3 11.7 %collective-permute-start.11 = (bf16[4,32,1600]{2,1,0:T(8,128)(2,1)S(1)}, bf16[4,32,1600]{2,1,0:T(8,128)(2,1)S(1)}, u32[]{:S(2)}, u32[]{:S(2)}) collective-permute-start(bf16[4,32,1600]{2,1,0:T(8,128)(2,1)S(1)} %collective-permute-done.9.refs_1_.refs_4_), channel_id=1, source_target_pairs={{0,4},{1,3},{2,6},{3,1},{4,0},{5,7},{6,2},{7,5},{8,12},{9,11},{10,... | collective-permute-start | bytes 1228808 | tf_op jit(solution)/shard_map/ppermute | solution.py:96
  83.4 10.7 %collective-permute-start.12 = (bf16[4,32,1600]{2,1,0:T(8,128)(2,1)S(1)}, bf16[4,32,1600]{2,1,0:T(8,128)(2,1)S(1)}, u32[]{:S(2)}, u32[]{:S(2)}) collective-permute-start(bf16[4,32,1600]{2,1,0:T(8,128)(2,1)S(1)} %bitcast.50), channel_id=1, source_target_pairs={{0,1},{1,0},{2,3},{3,2},{4,5},{5,4},{6,7},{7,6},{8,9},{9,8},{10,11... | collective-permute-start | bytes 1228808 | tf_op jit(solution)/shard_map/ppermute | solution.py:96
  83.4 10.7 %collective-permute-start.13 = (bf16[4,32,1600]{2,1,0:T(8,128)(2,1)S(1)}, bf16[4,32,1600]{2,1,0:T(8,128)(2,1)S(1)}, u32[]{:S(2)}, u32[]{:S(2)}) collective-permute-start(bf16[4,32,1600]{2,1,0:T(8,128)(2,1)S(1)} %collective-permute-done.9.refs_1_.refs_4_), channel_id=1, source_target_pairs={{0,1},{1,0},{2,3},{3,2},{4,5},{5,4},{6,7},{7,6},{8,9},{9,8},{10,11... | collective-permute-start | bytes 1228808 | tf_op jit(solution)/shard_map/ppermute | solution.py:96
  89.5 4.6 %collective-permute-start.14 = (bf16[4,32,1600]{2,1,0:T(8,128)(2,1)S(1)}, bf16[4,32,1600]{2,1,0:T(8,128)(2,1)S(1)}, u32[]{:S(2)}, u32[]{:S(2)}) collective-permute-start(bf16[4,32,1600]{2,1,0:T(8,128)(2,1)S(1)} %collective-permute-done.10.refs_5_), channel_id=1, source_target_pairs={{0,1},{1,0},{2,3},{3,2},{4,5},{5,4},{6,7},{7,6},{8,9},{9,8},{10,11... | collective-permute-start | bytes 1228808 | tf_op jit(solution)/shard_map/ppermute | solution.py:96
  94.1 1.8 collective-permute-start.15
  101.5 4.9 %collective-permute-start.16 = (bf16[128,200]{1,0:T(8,128)(2,1)S(1)}, bf16[128,200]{1,0:T(8,128)(2,1)S(1)}, u32[]{:S(2)}, u32[]{:S(2)}) collective-permute-start(bf16[128,200]{1,0:T(8,128)(2,1)S(1)} %get-tuple-element.95), channel_id=1, source_target_pairs={{0,2},{1,5},{2,0},{3,7},{4,6},{5,1},{6,4},{7,3},{8,10},{9,13},{10,... | collective-permute-start | bytes 153608 | tf_op jit(solution)/shard_map/ppermute | solution.py:96
  103.2 5.0 %collective-permute-start.17 = (bf16[128,200]{1,0:T(8,128)(2,1)S(1)}, bf16[128,200]{1,0:T(8,128)(2,1)S(1)}, u32[]{:S(2)}, u32[]{:S(2)}) collective-permute-start(bf16[128,200]{1,0:T(8,128)(2,1)S(1)} %get-tuple-element.94), channel_id=1, source_target_pairs={{0,4},{1,3},{2,6},{3,1},{4,0},{5,7},{6,2},{7,5},{8,12},{9,11},{10,... | collective-permute-start | bytes 153608 | tf_op jit(solution)/shard_map/ppermute | solution.py:96
  104.2 5.8 %collective-permute-start.18 = (bf16[128,200]{1,0:T(8,128)(2,1)S(1)}, bf16[128,200]{1,0:T(8,128)(2,1)S(1)}, u32[]{:S(2)}, u32[]{:S(2)}) collective-permute-start(bf16[128,200]{1,0:T(8,128)(2,1)S(1)} %get-tuple-element.93), channel_id=1, source_target_pairs={{0,6},{1,7},{2,4},{3,5},{4,2},{5,3},{6,0},{7,1},{8,14},{9,15},{10,... | collective-permute-start | bytes 153608 | tf_op jit(solution)/shard_map/ppermute | solution.py:96
  105.0 5.0 %collective-permute-start.19 = (bf16[128,200]{1,0:T(8,128)(2,1)S(1)}, bf16[128,200]{1,0:T(8,128)(2,1)S(1)}, u32[]{:S(2)}, u32[]{:S(2)}) collective-permute-start(bf16[128,200]{1,0:T(8,128)(2,1)S(1)} %get-tuple-element.92), channel_id=1, source_target_pairs={{0,1},{1,0},{2,3},{3,2},{4,5},{5,4},{6,7},{7,6},{8,9},{9,8},{10,11... | collective-permute-start | bytes 153608 | tf_op jit(solution)/shard_map/ppermute | solution.py:96
  105.0 5.0 %collective-permute-start.20 = (bf16[128,200]{1,0:T(8,128)(2,1)S(1)}, bf16[128,200]{1,0:T(8,128)(2,1)S(1)}, u32[]{:S(2)}, u32[]{:S(2)}) collective-permute-start(bf16[128,200]{1,0:T(8,128)(2,1)S(1)} %get-tuple-element.91), channel_id=1, source_target_pairs={{0,5},{1,2},{2,7},{3,0},{4,1},{5,6},{6,3},{7,4},{8,13},{9,10},{10,... | collective-permute-start | bytes 153608 | tf_op jit(solution)/shard_map/ppermute | solution.py:96
  106.4 4.4 %collective-permute-start.21 = (bf16[128,200]{1,0:T(8,128)(2,1)S(1)}, bf16[128,200]{1,0:T(8,128)(2,1)S(1)}, u32[]{:S(2)}, u32[]{:S(2)}) collective-permute-start(bf16[128,200]{1,0:T(8,128)(2,1)S(1)} %get-tuple-element.90), channel_id=1, source_target_pairs={{0,3},{1,4},{2,1},{3,6},{4,7},{5,0},{6,5},{7,2},{8,11},{9,12},{10,... | collective-permute-start | bytes 153608 | tf_op jit(solution)/shard_map/ppermute | solution.py:96
  108.2 4.8 %collective-permute-start.22 = (bf16[128,200]{1,0:T(8,128)(2,1)S(1)}, bf16[128,200]{1,0:T(8,128)(2,1)S(1)}, u32[]{:S(2)}, u32[]{:S(2)}) collective-permute-start(bf16[128,200]{1,0:T(8,128)(2,1)S(1)} %get-tuple-element.89), channel_id=1, source_target_pairs={{0,7},{1,6},{2,5},{3,4},{4,3},{5,2},{6,1},{7,0},{8,15},{9,14},{10,... | collective-permute-start | bytes 153608 | tf_op jit(solution)/shard_map/ppermute | solution.py:96
  119.5 22.8 %copy-start.2 = (bf16[600,1600]{1,0:T(8,128)(2,1)S(1)}, bf16[600,1600]{1,0:T(8,128)(2,1)}, u32[]{:S(2)}) copy-start(bf16[600,1600]{1,0:T(8,128)(2,1)} %reshape.79.refs_2_.refs_0_) | copy-start | bytes 5760004
  119.5 8.2 %collective-permute-start.23 = (bf16[4,32,1600]{2,1,0:T(8,128)(2,1)S(1)}, bf16[4,32,1600]{2,1,0:T(8,128)(2,1)S(1)}, u32[]{:S(2)}, u32[]{:S(2)}) collective-permute-start(bf16[4,32,1600]{2,1,0:T(8,128)(2,1)S(1)} %bitcast.44), channel_id=1, source_target_pairs={{0,2},{1,5},{2,0},{3,7},{4,6},{5,1},{6,4},{7,3},{8,10},{9,13},{10,... | collective-permute-start | bytes 1228808 | tf_op jit(solution)/shard_map/ppermute | solution.py:96
  127.8 8.2 %collective-permute-start.24 = (bf16[4,32,1600]{2,1,0:T(8,128)(2,1)S(1)}, bf16[4,32,1600]{2,1,0:T(8,128)(2,1)S(1)}, u32[]{:S(2)}, u32[]{:S(2)}) collective-permute-start(bf16[4,32,1600]{2,1,0:T(8,128)(2,1)S(1)} %bitcast.46), channel_id=1, source_target_pairs={{0,4},{1,3},{2,6},{3,1},{4,0},{5,7},{6,2},{7,5},{8,12},{9,11},{10,... | collective-permute-start | bytes 1228808 | tf_op jit(solution)/shard_map/ppermute | solution.py:96
  128.8 11.7 %collective-permute-start.25 = (bf16[4,32,1600]{2,1,0:T(8,128)(2,1)S(1)}, bf16[4,32,1600]{2,1,0:T(8,128)(2,1)S(1)}, u32[]{:S(2)}, u32[]{:S(2)}) collective-permute-start(bf16[4,32,1600]{2,1,0:T(8,128)(2,1)S(1)} %collective-permute-done.23.refs_1_.refs_4_), channel_id=1, source_target_pairs={{0,4},{1,3},{2,6},{3,1},{4,0},{5,7},{6,2},{7,5},{8,12},{9,11},{10,... | collective-permute-start | bytes 1228808 | tf_op jit(solution)/shard_map/ppermute | solution.py:96
  129.9 10.7 %collective-permute-start.26 = (bf16[4,32,1600]{2,1,0:T(8,128)(2,1)S(1)}, bf16[4,32,1600]{2,1,0:T(8,128)(2,1)S(1)}, u32[]{:S(2)}, u32[]{:S(2)}) collective-permute-start(bf16[4,32,1600]{2,1,0:T(8,128)(2,1)S(1)} %bitcast.47), channel_id=1, source_target_pairs={{0,1},{1,0},{2,3},{3,2},{4,5},{5,4},{6,7},{7,6},{8,9},{9,8},{10,11... | collective-permute-start | bytes 1228808 | tf_op jit(solution)/shard_map/ppermute | solution.py:96
  129.9 10.7 %collective-permute-start.27 = (bf16[4,32,1600]{2,1,0:T(8,128)(2,1)S(1)}, bf16[4,32,1600]{2,1,0:T(8,128)(2,1)S(1)}, u32[]{:S(2)}, u32[]{:S(2)}) collective-permute-start(bf16[4,32,1600]{2,1,0:T(8,128)(2,1)S(1)} %collective-permute-done.23.refs_1_.refs_4_), channel_id=1, source_target_pairs={{0,1},{1,0},{2,3},{3,2},{4,5},{5,4},{6,7},{7,6},{8,9},{9,8},{10,11... | collective-permute-start | bytes 1228808 | tf_op jit(solution)/shard_map/ppermute | solution.py:96
  136.0 4.6 %collective-permute-start.28 = (bf16[4,32,1600]{2,1,0:T(8,128)(2,1)S(1)}, bf16[4,32,1600]{2,1,0:T(8,128)(2,1)S(1)}, u32[]{:S(2)}, u32[]{:S(2)}) collective-permute-start(bf16[4,32,1600]{2,1,0:T(8,128)(2,1)S(1)} %collective-permute-done.24.refs_5_), channel_id=1, source_target_pairs={{0,1},{1,0},{2,3},{3,2},{4,5},{5,4},{6,7},{7,6},{8,9},{9,8},{10,11... | collective-permute-start | bytes 1228808 | tf_op jit(solution)/shard_map/ppermute | solution.py:96
  140.5 1.8 collective-permute-start.29
  148.6 15.7 %copy-start.10 = (f32[4,32,1600]{2,1,0:T(8,128)S(1)}, f32[4,32,1600]{2,1,0:T(8,128)}, u32[]{:S(2)}) copy-start(f32[4,32,1600]{2,1,0:T(8,128)} %copy-done.9) | copy-start | bytes 2457604
  148.6 2.4 %collective-permute-start.30 = (f32[4,32,1600]{2,1,0:T(8,128)S(1)}, f32[4,32,1600]{2,1,0:T(8,128)S(1)}, u32[]{:S(2)}, u32[]{:S(2)}) collective-permute-start(f32[4,32,1600]{2,1,0:T(8,128)S(1)} %get-tuple-element.61), channel_id=1, source_target_pairs={{0,1},{1,0},{2,3},{3,2},{4,5},{5,4},{6,7},{7,6},{8,9},{9,8},{10,11... | collective-permute-start | bytes 2457608 | tf_op jit(solution)/shard_map/ppermute | solution.py:96
  151.2 35.6 %copy-start.5 = (bf16[1600,64]{0,1:T(8,128)(2,1)S(1)}, bf16[1600,64]{0,1:T(8,128)(2,1)}, u32[]{:S(2)}) copy-start(bf16[1600,64]{0,1:T(8,128)(2,1)} %param.21) | copy-start | bytes 614404
  151.2 8.2 %collective-permute-start.31 = (f32[32,1600]{1,0:T(8,128)S(1)}, f32[32,1600]{1,0:T(8,128)S(1)}, u32[]{:S(2)}, u32[]{:S(2)}) collective-permute-start(f32[32,1600]{1,0:T(8,128)S(1)} %get-tuple-element.63), channel_id=1, source_target_pairs={{0,2},{1,5},{2,0},{3,7},{4,6},{5,1},{6,4},{7,3},{8,10},{9,13},{10,... | collective-permute-start | bytes 614408 | tf_op jit(solution)/shard_map/ppermute | solution.py:96
  151.3 8.1 %collective-permute-start.32 = (f32[32,1600]{1,0:T(8,128)S(1)}, f32[32,1600]{1,0:T(8,128)S(1)}, u32[]{:S(2)}, u32[]{:S(2)}) collective-permute-start(f32[32,1600]{1,0:T(8,128)S(1)} %get-tuple-element.64), channel_id=1, source_target_pairs={{0,4},{1,3},{2,6},{3,1},{4,0},{5,7},{6,2},{7,5},{8,12},{9,11},{10,... | collective-permute-start | bytes 614408 | tf_op jit(solution)/shard_map/ppermute | solution.py:96
  152.6 11.7 %collective-permute-start.33 = (f32[32,1600]{1,0:T(8,128)S(1)}, f32[32,1600]{1,0:T(8,128)S(1)}, u32[]{:S(2)}, u32[]{:S(2)}) collective-permute-start(f32[32,1600]{1,0:T(8,128)S(1)} %get-tuple-element.65), channel_id=1, source_target_pairs={{0,6},{1,7},{2,4},{3,5},{4,2},{5,3},{6,0},{7,1},{8,14},{9,15},{10,... | collective-permute-start | bytes 614408 | tf_op jit(solution)/shard_map/ppermute | solution.py:96
  164.5 7.1 %collective-permute-start.34 = (bf16[32,1600]{1,0:T(8,128)(2,1)S(1)}, bf16[32,1600]{1,0:T(8,128)(2,1)S(1)}, u32[]{:S(2)}, u32[]{:S(2)}) collective-permute-start(bf16[32,1600]{1,0:T(8,128)(2,1)S(1)} %shard_map.155.refs_0_), channel_id=1, source_target_pairs={{0,8},{8,0},{16,24},{24,16},{1,9},{9,1},{17,25},{25,17},{2,10},{10... | collective-permute-start | bytes 307208 | tf_op jit(solution)/shard_map/ppermute | solution.py:96
  164.7 8.4 %collective-permute-start.35 = (bf16[32,1600]{1,0:T(8,128)(2,1)S(1)}, bf16[32,1600]{1,0:T(8,128)(2,1)S(1)}, u32[]{:S(2)}, u32[]{:S(2)}) collective-permute-start(bf16[32,1600]{1,0:T(8,128)(2,1)S(1)} %shard_map.155.refs_0_), channel_id=1, source_target_pairs={{0,16},{8,24},{16,0},{24,8},{1,17},{9,25},{17,1},{25,9},{2,18},{10... | collective-permute-start | bytes 307208 | tf_op jit(solution)/shard_map/ppermute | solution.py:96
  173.2 5.9 %collective-permute-start.36 = (bf16[32,1600]{1,0:T(8,128)(2,1)S(1)}, bf16[32,1600]{1,0:T(8,128)(2,1)S(1)}, u32[]{:S(2)}, u32[]{:S(2)}) collective-permute-start(bf16[32,1600]{1,0:T(8,128)(2,1)S(1)} %bitcast.52), channel_id=1, source_target_pairs={{0,2},{1,5},{2,0},{3,7},{4,6},{5,1},{6,4},{7,3},{8,10},{9,13},{10,... | collective-permute-start | bytes 307208 | tf_op jit(solution)/shard_map/ppermute | solution.py:96
  173.9 6.5 %collective-permute-start.45 = (bf16[32,1600]{1,0:T(8,128)(2,1)S(1)}, bf16[32,1600]{1,0:T(8,128)(2,1)S(1)}, u32[]{:S(2)}, u32[]{:S(2)}) collective-permute-start(bf16[32,1600]{1,0:T(8,128)(2,1)S(1)} %shard_map.155.refs_0_), channel_id=1, source_target_pairs={{0,24},{8,16},{16,8},{24,0},{1,25},{9,17},{17,9},{25,1},{2,26},{10... | collective-permute-start | bytes 307208 | tf_op jit(solution)/shard_map/ppermute | solution.py:96
  176.2 7.4 %collective-permute-start.37 = (bf16[32,1600]{1,0:T(8,128)(2,1)S(1)}, bf16[32,1600]{1,0:T(8,128)(2,1)S(1)}, u32[]{:S(2)}, u32[]{:S(2)}) collective-permute-start(bf16[32,1600]{1,0:T(8,128)(2,1)S(1)} %bitcast.53), channel_id=1, source_target_pairs={{0,4},{1,3},{2,6},{3,1},{4,0},{5,7},{6,2},{7,5},{8,12},{9,11},{10,... | collective-permute-start | bytes 307208 | tf_op jit(solution)/shard_map/ppermute | solution.py:96
  177.1 6.9 %collective-permute-start.38 = (bf16[32,1600]{1,0:T(8,128)(2,1)S(1)}, bf16[32,1600]{1,0:T(8,128)(2,1)S(1)}, u32[]{:S(2)}, u32[]{:S(2)}) collective-permute-start(bf16[32,1600]{1,0:T(8,128)(2,1)S(1)} %bitcast.54), channel_id=1, source_target_pairs={{0,6},{1,7},{2,4},{3,5},{4,2},{5,3},{6,0},{7,1},{8,14},{9,15},{10,... | collective-permute-start | bytes 307208 | tf_op jit(solution)/shard_map/ppermute | solution.py:96
  179.1 6.2 %collective-permute-start.39 = (bf16[32,1600]{1,0:T(8,128)(2,1)S(1)}, bf16[32,1600]{1,0:T(8,128)(2,1)S(1)}, u32[]{:S(2)}, u32[]{:S(2)}) collective-permute-start(bf16[32,1600]{1,0:T(8,128)(2,1)S(1)} %bitcast.55), channel_id=1, source_target_pairs={{0,1},{1,0},{2,3},{3,2},{4,5},{5,4},{6,7},{7,6},{8,9},{9,8},{10,11... | collective-permute-start | bytes 307208 | tf_op jit(solution)/shard_map/ppermute | solution.py:96
  179.1 6.2 %collective-permute-start.40 = (bf16[32,1600]{1,0:T(8,128)(2,1)S(1)}, bf16[32,1600]{1,0:T(8,128)(2,1)S(1)}, u32[]{:S(2)}, u32[]{:S(2)}) collective-permute-start(bf16[32,1600]{1,0:T(8,128)(2,1)S(1)} %collective-permute-done.36.refs_8_), channel_id=1, source_target_pairs={{0,1},{1,0},{2,3},{3,2},{4,5},{5,4},{6,7},{7,6},{8,9},{9,8},{10,11... | collective-permute-start | bytes 307208 | tf_op jit(solution)/shard_map/ppermute | solution.py:96
  180.4 15.9 %collective-permute-start.46 = (bf16[3,32,1600]{2,1,0:T(8,128)(2,1)S(1)}, bf16[3,32,1600]{2,1,0:T(8,128)(2,1)S(1)}, u32[]{:S(2)}, u32[]{:S(2)}) collective-permute-start(bf16[3,32,1600]{2,1,0:T(8,128)(2,1)S(1)} %shard_map.159.refs_0_), channel_id=1, source_target_pairs={{0,2},{1,5},{2,0},{3,7},{4,6},{5,1},{6,4},{7,3},{8,10},{9,13},{10,... | collective-permute-start | bytes 921608 | tf_op jit(solution)/shard_map/ppermute | solution.py:96
  183.7 13.8 %collective-permute-start.47 = (bf16[3,32,1600]{2,1,0:T(8,128)(2,1)S(1)}, bf16[3,32,1600]{2,1,0:T(8,128)(2,1)S(1)}, u32[]{:S(2)}, u32[]{:S(2)}) collective-permute-start(bf16[3,32,1600]{2,1,0:T(8,128)(2,1)S(1)} %shard_map.159.refs_0_), channel_id=1, source_target_pairs={{0,4},{1,3},{2,6},{3,1},{4,0},{5,7},{6,2},{7,5},{8,12},{9,11},{10,... | collective-permute-start | bytes 921608 | tf_op jit(solution)/shard_map/ppermute | solution.py:96
  184.0 13.5 %collective-permute-start.48 = (bf16[3,32,1600]{2,1,0:T(8,128)(2,1)S(1)}, bf16[3,32,1600]{2,1,0:T(8,128)(2,1)S(1)}, u32[]{:S(2)}, u32[]{:S(2)}) collective-permute-start(bf16[3,32,1600]{2,1,0:T(8,128)(2,1)S(1)} %shard_map.159.refs_0_), channel_id=1, source_target_pairs={{0,6},{1,7},{2,4},{3,5},{4,2},{5,3},{6,0},{7,1},{8,14},{9,15},{10,... | collective-permute-start | bytes 921608 | tf_op jit(solution)/shard_map/ppermute | solution.py:96
  185.3 1.3 collective-permute-start.41
  185.3 1.5 collective-permute-start.42
  198.4 5.9 %collective-permute-start.49 = (bf16[4,3,32,1600]{3,2,1,0:T(8,128)(2,1)S(1)}, bf16[4,3,32,1600]{3,2,1,0:T(8,128)(2,1)S(1)}, u32[]{:S(2)}, u32[]{:S(2)}) collective-permute-start(bf16[4,3,32,1600]{3,2,1,0:T(8,128)(2,1)S(1)} %shard_map.160.refs_0_), channel_id=1, source_target_pairs={{0,1},{1,0},{2,3},{3,2},{4,5},{5,4},{6,7},{7,6},{8,9},{9,8},{10,11... | collective-permute-start | bytes 3686408 | tf_op jit(solution)/shard_map/ppermute | solution.py:96
  198.5 3.0 %collective-permute-start.43 = (f32[72,256]{1,0:T(8,128)S(1)}, f32[72,256]{1,0:T(8,128)S(1)}, u32[]{:S(2)}, u32[]{:S(2)}) collective-permute-start(f32[72,256]{1,0:T(8,128)S(1)} %get-tuple-element.66.refs_0_), channel_id=1, source_target_pairs={{0,1},{1,0},{2,3},{3,2},{4,5},{5,4},{6,7},{7,6},{8,9},{9,8},{10,11... | collective-permute-start | bytes 221192 | tf_op jit(solution)/shard_map/ppermute | solution.py:96
  202.5 7.5 %collective-permute-start.44 = (f32[72,256]{1,0:T(8,128)S(1)}, f32[72,256]{1,0:T(8,128)S(1)}, u32[]{:S(2)}, u32[]{:S(2)}) collective-permute-start(f32[72,256]{1,0:T(8,128)S(1)} %shard_map.158.refs_0_), channel_id=1, source_target_pairs={{0,2},{1,3},{2,0},{3,1},{4,6},{5,7},{6,4},{7,5},{8,10},{9,11},{10,... | collective-permute-start | bytes 221192 | tf_op jit(solution)/shard_map/ppermute | solution.py:96
  210.1 12.2 %collective-permute-start.50 = (f32[72,256]{1,0:T(8,128)S(1)}, f32[72,256]{1,0:T(8,128)S(1)}, u32[]{:S(2)}, u32[]{:S(2)}) collective-permute-start(f32[72,256]{1,0:T(8,128)S(1)} %shard_map.162.refs_0_), channel_id=1, source_target_pairs={{0,4},{1,5},{2,6},{3,7},{4,0},{5,1},{6,2},{7,3},{8,12},{9,13},{10,... | collective-permute-start | bytes 221192 | tf_op jit(solution)/shard_map/ppermute | solution.py:96
  216.5 10.3 %copy-start.8 = (bf16[960,256]{1,0:T(8,128)(2,1)S(1)}, bf16[960,256]{1,0:T(8,128)(2,1)}, u32[]{:S(2)}) copy-start(bf16[960,256]{1,0:T(8,128)(2,1)} %copy-done.6) | copy-start | bytes 1474564
  222.3 10.7 %collective-permute-start.51 = (f32[72,256]{1,0:T(8,128)S(1)}, f32[72,256]{1,0:T(8,128)S(1)}, u32[]{:S(2)}, u32[]{:S(2)}) collective-permute-start(f32[72,256]{1,0:T(8,128)S(1)} %shard_map.164.refs_1_), channel_id=1, source_target_pairs={{0,8},{8,0},{16,24},{24,16},{1,9},{9,1},{17,25},{25,17},{2,10},{10... | collective-permute-start | bytes 221192 | tf_op jit(solution)/shard_map/ppermute | solution.py:96
  222.4 10.7 %collective-permute-start.52 = (f32[72,256]{1,0:T(8,128)S(1)}, f32[72,256]{1,0:T(8,128)S(1)}, u32[]{:S(2)}, u32[]{:S(2)}) collective-permute-start(f32[72,256]{1,0:T(8,128)S(1)} %shard_map.164.refs_1_), channel_id=1, source_target_pairs={{0,16},{8,24},{16,0},{24,8},{1,17},{9,25},{17,1},{25,9},{2,18},{10... | collective-permute-start | bytes 221192 | tf_op jit(solution)/shard_map/ppermute | solution.py:96
  224.2 8.9 %collective-permute-start.53 = (f32[72,256]{1,0:T(8,128)S(1)}, f32[72,256]{1,0:T(8,128)S(1)}, u32[]{:S(2)}, u32[]{:S(2)}) collective-permute-start(f32[72,256]{1,0:T(8,128)S(1)} %shard_map.164.refs_1_), channel_id=1, source_target_pairs={{0,24},{8,16},{16,8},{24,0},{1,25},{9,17},{17,9},{25,1},{2,26},{10... | collective-permute-start | bytes 221192 | tf_op jit(solution)/shard_map/ppermute | solution.py:96
  (17 other events, 48.2 us)
Sparse Core Ops, SparseCore 0:
  9.9 52.8 all-gather.3
  72.1 44.7 all-gather.5
